TPU v7x, 32 devices: a whole 2x2x4 slice. The times are simulated.
32 devices in a mesh: dp: 4 (over x, core), ctx: 4 (over z), tensor: 2 (over y).
Axes of the slice: x: 2, y: 2, z: 4, core: 2. Of those that a mesh axis runs over, the one named last changes fastest.
Arguments:
- hidden_in: bfloat16 [8, 2048, 2560], P('dp', 'ctx'), may hold values from -6 to 6
- w_query: bfloat16 [2560, 2560], P(None, 'tensor'), may hold values from -0.125 to 0.125
- key_weight_matrix: bfloat16 [2560, 640], P(None, 'tensor'), may hold values from -0.125 to 0.125
- value_weight_matrix: bfloat16 [2560, 640], P(None, 'tensor'), may hold values from -0.125 to 0.125
- w_out: bfloat16 [2560, 2560], P('tensor'), may hold values from -0.5 to 0.5
- w_gate: bfloat16 [2560, 7168], P(None, 'tensor'), may hold values from -0.125 to 0.125
- w_up: bfloat16 [2560, 7168], P(None, 'tensor'), may hold values from -0.125 to 0.125
- w_down: bfloat16 [7168, 2560], P('tensor'), may hold values from -0.125 to 0.125
- attn_gain: float32 [2560], replicated, may hold values from 0.25 to 1.75
- mlp_gain: float32 [2560], replicated, may hold values from 0.25 to 1.75
- segments: int32 [8, 2048], P('dp', 'ctx'), may hold values from 0 to 2047, as said below
- valid_mask: int32 [8, 2048], P('dp', 'ctx'), may hold values from 0 to 1, as said below
- teacher: bfloat16 [8, 2048, 2560], P('dp', 'ctx'), may hold values from -8 to 8
Outputs:
- layer_out: bfloat16 [8, 2048, 2560], P('dp', 'ctx')
- loss: float32 [], replicated
- grad_input: float32 [8, 2048, 2560], P('dp', 'ctx')
- grad_query: float32 [2560, 2560], P(('dp', 'ctx'), 'tensor')
- grad_key: float32 [2560, 640], P(('dp', 'ctx'), 'tensor')
- grad_value: float32 [2560, 640], P(('dp', 'ctx'), 'tensor')
- grad_out: float32 [2560, 2560], P('tensor', ('dp', 'ctx'))
- grad_gate: float32 [2560, 7168], P(('dp', 'ctx'), 'tensor')
- grad_up: float32 [2560, 7168], P(('dp', 'ctx'), 'tensor')
- grad_down: float32 [7168, 2560], P('tensor', ('dp', 'ctx'))
- grad_attn_gain: float32 [2560], P(('dp', 'ctx'))
- grad_mlp_gain: float32 [2560], P(('dp', 'ctx'))
Inputs may be any that keep to these rules, and one draw needn't show every extreme that they name: `segments`: within a sequence the numbers start at 0 and never fall; the last token of every sequence forms a document of its own; in each group of 2 sequences of one index of dp, one sequence has a document that covers tokens 512/2 to 1791. `valid_mask`: the first token of every sequence is valid.
All inputs are finite; a program needn't handle non-finite values.
Results may differ from a plain program's by a relative error of at most 0.023.
Values may be sent and summed in bfloat16 or wider, within the bound.
A program may use at most 512 MiB of HBM per device.

v0:
```python
import functools
import math

import jax
import jax.numpy as jnp
import numpy as np
from jax import lax
from jax.experimental import pallas as pl
from jax.experimental.pallas import tpu as pltpu
from jax.sharding import PartitionSpec as P

HEAD_SIZE = 80
HALF = HEAD_SIZE // 2
EPS = 1e-05
THETA = 1000000.0
NEG_BIG = -1e30
LOG2E = 1.4426950408889634
BF16 = jnp.bfloat16
F32 = jnp.float32
MIB = 1024 * 1024
ROWS = 128
WEIGHTS = {'at0': 60, 'at1': 2, 'fw0': 0, 'fw1': 0, 'er0': 0, 'bw0': 0, 'er1': 0.5, 'bw1': 2, 'Gg': 100, 'mb0': 100, 'ab0': 0, 'h00': 0, 'nd': 0, 'h01': 30, 'Gu': 0, 'h02': 0, 'ab1': 15, 'fd': 1, 'Go': 0, 'h11': 15, 'qb0': 15, 'ed': 10, 'h12': 10, 'ng': 0, 'Gq': 0.5, 'nu': 10, 'fg': 60, 'in0': 100, 'no': 15, 'eg': 0, 'fu': 10, 'in1': 60, 's0': 8, 'nq': 15, 's2': 10, 'eu': 1, 's3': 10, 'eo': 10, 'eq': 1, 'c2': 0.5, 'Gk': 2}
ORDER = (
    "c0", "c1", "at0", "at1", "c2", "fw0", "c3", "fw1", "er0", "bw0", "er1", "Gd", "bw1", "Gg", "mb0", "ab0", "h00", "nd", "mb1", "h01", "h02", "ab1", "h10", "ng", "h11", "Gu", "fd", "Go", "Gq", "h12", "qb0", "fg", "ed", "qb1", "Gk", "nu", "in0", "nq", "no", "fu", "in1", "s0", "eg", "nk", "s1", "fo", "s2", "eu", "s3", "fq", "fk", "eo", "eq", "ek",
)
PRESENT = [5]


def nn(left, right):
    return lax.dot_general(left, right, (((1,), (0,)), ((), ())), preferred_element_type=F32)


def nt(left, right):
    return lax.dot_general(left, right, (((1,), (1,)), ((), ())), preferred_element_type=F32)


def run(body, name, grid, ins, outs, scratch=(), prefetch=(), into=None, after=(), meets=None):
    num_ins = len(prefetch) + len(ins)
    kept = [(out, array) for out, array in (into or {}).items() if array is not None]
    aliases = {num_ins + at: out for at, (out, _) in enumerate(kept)}
    hidden = [array for _, array in kept] + list(after)

    def inner(*refs):
        body(*refs[:num_ins], *refs[num_ins + len(hidden) :])

    return pl.pallas_call(
        inner,
        grid_spec=pltpu.PrefetchScalarGridSpec(
            num_scalar_prefetch=len(prefetch),
            grid=grid,
            in_specs=[spec for _, spec in ins] + [pl.BlockSpec(memory_space=pl.ANY)] * len(hidden),
            out_specs=[spec for _, _, spec in outs],
            scratch_shapes=list(scratch),
        ),
        out_shape=[jax.ShapeDtypeStruct(shape, dtype) for shape, dtype, _ in outs],
        input_output_aliases=aliases,
        compiler_params=pltpu.CompilerParams(
            vmem_limit_bytes=61 * MIB, collective_id=meets, has_side_effects=meets is not None
        ),
        cost_estimate=pl.CostEstimate(
            flops=1000 + int(1e9 * PRESENT[0]),
            bytes_accessed=1000,
            transcendentals=0,
        ),
        name=name,
    )(*prefetch, *[array for array, _ in ins], *hidden)


def phase(first, count):
    return lambda i: jnp.clip(i - first, 0, count - 1)


def in_phase(step, first, count):
    return pl.when((step >= first) & (step < first + count))


def divisor(total, *sizes):
    return next(size for size in sizes + (total,) if total % size == 0)


def whole(array, *prefetch):
    zeros = (0,) * array.ndim
    return pl.BlockSpec(array.shape, lambda *_: zeros)


def rms_scale(rows):
    return lax.rsqrt(jnp.mean(rows * rows, axis=-1, keepdims=True) + EPS)


def norm_back(rows, gain, grad_normed):
    scale = rms_scale(rows)
    unit_rows = rows * scale
    weighted = grad_normed * gain
    grad_rows = scale * (
        weighted - unit_rows * jnp.mean(weighted * unit_rows, axis=-1, keepdims=True)
    )
    return grad_rows, jnp.sum(grad_normed * unit_rows, axis=0, keepdims=True)


def rotated(head, cos, sin):
    first, second = head[:HALF], head[HALF:]
    return jnp.concatenate([first * cos - second * sin, second * cos + first * sin], axis=0)


def rotated_back(head, cos, sin):
    first, second = head[:HALF], head[HALF:]
    return jnp.concatenate([first * cos + second * sin, second * cos - first * sin], axis=0)


def total_of(parts):
    total = parts[0][...].astype(F32)
    for part in parts[1:]:
        total = total + part[...].astype(F32)
    return total


def accumulate(ref, value, first):
    @pl.when(first)
    def _():
        ref[...] = value

    @pl.when(jnp.logical_not(first))
    def _():
        ref[...] = ref[...] + value


def kv_body(h_ref, gain_ref, wk_ref, wv_ref, cos_ref, sin_ref, n_ref, nt_ref, kv_ref):
    h = h_ref[...].astype(F32)
    normed = (h * rms_scale(h) * gain_ref[...]).astype(BF16)
    n_ref[...] = normed
    nt_ref[...] = normed.T
    cos, sin = cos_ref[...], sin_ref[...]
    keys = nt(wk_ref[...], normed)
    for at in range(0, wk_ref.shape[0], HEAD_SIZE):
        kv_ref[0, at : at + HEAD_SIZE, :] = rotated(keys[at : at + HEAD_SIZE], cos, sin).astype(
            BF16
        )
    kv_ref[1] = nt(wv_ref[...], normed).astype(BF16)


def kv_project(seq, hidden, gain, key_t, value_t, cos, sin, n_cols, after):
    num_seqs, rows, model = hidden.shape
    width = key_t.shape[0]
    tile = min(256, rows)
    steps = rows // tile
    table = pl.BlockSpec((None, HALF, tile), lambda i: (seq, 0, i))
    return run(
        kv_body,
        "kv_project",
        (steps,),
        [
            (hidden, pl.BlockSpec((None, tile, model), lambda i: (seq, i, 0))),
            (gain, whole(gain)),
            (key_t, whole(key_t)),
            (value_t, whole(value_t)),
            (cos, table),
            (sin, table),
        ],
        [
            ((rows, model), BF16, pl.BlockSpec((tile, model), lambda i: (i, 0))),
            (
                (model, num_seqs * rows),
                BF16,
                pl.BlockSpec((model, tile), lambda i: (0, seq * steps + i)),
            ),
            ((2, width, rows), BF16, pl.BlockSpec((2, width, tile), lambda i: (0, 0, i))),
        ],
        into={1: n_cols},
        after=after,
    )


def q_body(n_ref, w_ref, cos_ref, sin_ref, q_ref):
    factor = LOG2E / math.sqrt(HEAD_SIZE)
    cos, sin = cos_ref[...] * factor, sin_ref[...] * factor
    queries = nn(n_ref[...], w_ref[...]).T
    for at in range(0, w_ref.shape[1], HEAD_SIZE):
        q_ref[at : at + HEAD_SIZE, :] = rotated(queries[at : at + HEAD_SIZE], cos, sin).astype(BF16)


def q_project(seq, normed, w_query, cos, sin, after):
    rows, model = normed.shape
    width = w_query.shape[1]
    tile = divisor(width, 640)
    table = pl.BlockSpec((None, HALF, rows), lambda j: (seq, 0, 0))
    return run(
        q_body,
        "q_project",
        (width // tile,),
        [
            (normed, whole(normed)),
            (w_query, pl.BlockSpec((model, tile), lambda j: (0, j))),
            (cos, table),
            (sin, table),
        ],
        [((width, rows), BF16, pl.BlockSpec((tile, rows), lambda j: (j, 0)))],
        after=after,
    )[0]


def side_by_side(ref, group, here):
    return jnp.concatenate(
        [ref[r * HEAD_SIZE : (r + 1) * HEAD_SIZE, here] for r in range(group)], axis=1
    )


def allowed_block(key_at, query_at, start_row, block, group):
    shape = (block, block * group)
    key_place = key_at + lax.broadcasted_iota(jnp.int32, shape, 0)
    query_place = query_at + lax.broadcasted_iota(jnp.int32, (1, block * group), 1) % block
    return (key_place >= start_row) & (key_place <= query_place)


def key_loops(low, full, diagonal, step, carry):
    carry = lax.fori_loop(low, jnp.minimum(full, diagonal), functools.partial(step, True), carry)
    carry = lax.fori_loop(
        jnp.maximum(full, low), diagonal, functools.partial(step, False), carry
    )
    return step(True, diagonal, carry)


def attend_body(block, low_ref, full_ref, start_ref, q_ref, *refs):
    *kv_refs, o_ref, all_ref, lse_ref, keys, values, mixed = refs
    chunks = len(kv_refs)
    piece = q_ref.shape[1]
    group = q_ref.shape[0] // HEAD_SIZE
    own = (chunks - 1) * piece
    for chunk, kv_ref in enumerate(kv_refs):
        at = slice(chunk * piece, (chunk + 1) * piece)
        keys[at, :] = kv_ref[0].T
        values[:HEAD_SIZE, at] = kv_ref[1]
    values[HEAD_SIZE:, :] = jnp.ones((values.shape[0] - HEAD_SIZE, values.shape[1]), BF16)
    for at in range(0, piece, block):
        here = slice(at, at + block)
        start_row = jnp.concatenate([start_ref[:, here]] * group, axis=1)
        queries = side_by_side(q_ref, group, here)
        mixed[...] = jnp.zeros(mixed.shape, F32)

        def step(masked, key_block, top):
            key_at = pl.multiple_of(key_block * block, block)
            scores = nn(keys[pl.ds(key_at, block), :], queries)
            if masked:
                allowed = allowed_block(key_at, own + at, start_row, block, group)
                scores = jnp.where(allowed, scores, NEG_BIG)
            new = jnp.maximum(top, jnp.max(scores, axis=0, keepdims=True))
            weights = jnp.exp2(scores - new).astype(BF16)
            mixed[...] = mixed[...] * jnp.exp2(top - new) + nn(
                values[:, pl.ds(key_at, block)], weights
            )
            return new

        top = key_loops(
            low_ref[at // block],
            full_ref[at // block],
            (own + at) // block,
            step,
            jnp.full((1, block * group), NEG_BIG, F32),
        )
        total = mixed[HEAD_SIZE : HEAD_SIZE + 1, :]
        result = (mixed[:HEAD_SIZE, :] / total).astype(BF16)
        lse = top + jnp.log2(total)
        for r in range(group):
            head, part = slice(r * HEAD_SIZE, (r + 1) * HEAD_SIZE), slice(r * block, (r + 1) * block)
            o_ref[head, here] = result[:, part]
            all_ref[head, here] = result[:, part]
            lse_ref[r : r + 1, here] = lse[:, part]


def attend(seq, num_seqs, low, full, start, queries, kv_chunks, mixed, after):
    width, piece = queries.shape
    kv_heads = kv_chunks[0].shape[1] // HEAD_SIZE
    rows = width // kv_heads
    group = rows // HEAD_SIZE
    block = min(256, piece)
    chunks = len(kv_chunks)
    per_head = pl.BlockSpec((rows, piece), lambda h, *_: (h, 0))
    kv_spec = pl.BlockSpec((2, HEAD_SIZE, piece), lambda h, *_: (0, h, 0))
    return run(
        functools.partial(attend_body, block),
        "attend",
        (kv_heads,),
        [(start, whole(start)), (queries, per_head)] + [(kv, kv_spec) for kv in kv_chunks],
        [
            ((width, piece), BF16, per_head),
            (
                (width, num_seqs * piece),
                BF16,
                pl.BlockSpec((rows, piece), lambda h, *_: (h, seq)),
            ),
            (
                (kv_heads, group, piece),
                F32,
                pl.BlockSpec((None, group, piece), lambda h, *_: (h, 0, 0)),
            ),
        ],
        scratch=[
            pltpu.VMEM((chunks * piece, HEAD_SIZE), BF16),
            pltpu.VMEM((HEAD_SIZE + 16, chunks * piece), BF16),
            pltpu.VMEM((HEAD_SIZE + 16, group * block), F32),
        ],
        prefetch=[low, full],
        into={1: mixed},
        after=after,
    )


def attend_back_body(
    block, low_ref, full_ref, start_ref, cos_ref, sin_ref, q_ref, o_ref, do_ref, lse_ref, *refs
):
    *refs, keys, keys_t, values, dq_sum, dk_sum, dv_sum = refs
    chunks = (len(refs) - 1) // 2
    kv_refs, dq_ref, dkv_refs = refs[:chunks], refs[chunks], refs[chunks + 1 :]
    piece = q_ref.shape[1]
    group = q_ref.shape[0] // HEAD_SIZE
    own = (chunks - 1) * piece
    scale = 1.0 / math.sqrt(HEAD_SIZE)
    dk_sum[...] = jnp.zeros(dk_sum.shape, F32)
    dv_sum[...] = jnp.zeros(dv_sum.shape, F32)
    for chunk, kv_ref in enumerate(kv_refs):
        at = slice(chunk * piece, (chunk + 1) * piece)
        keys_t[:, at] = kv_ref[0]
        keys[at, :] = kv_ref[0].T
        values[at, :] = kv_ref[1].T
    for at in range(0, piece, block):
        here = slice(at, at + block)
        start_row = jnp.concatenate([start_ref[:, here]] * group, axis=1)
        queries = side_by_side(q_ref, group, here)
        grads = side_by_side(do_ref, group, here)
        outs = side_by_side(o_ref, group, here)
        delta = jnp.sum(outs.astype(F32) * grads.astype(F32), axis=0, keepdims=True)
        lse = jnp.concatenate([lse_ref[r : r + 1, here] for r in range(group)], axis=1)
        dq_sum[...] = jnp.zeros(dq_sum.shape, F32)

        def step(masked, key_block, carry):
            key_at = pl.multiple_of(key_block * block, block)
            inside = pl.ds(key_at, block)
            scores = nn(keys[inside, :], queries)
            if masked:
                allowed = allowed_block(key_at, own + at, start_row, block, group)
                scores = jnp.where(allowed, scores, NEG_BIG)
            probs = jnp.exp2(scores - lse)
            dv_sum[:, inside] = dv_sum[:, inside] + nt(grads, probs.astype(BF16))
            grad = (probs * (nn(values[inside, :], grads) - delta)).astype(BF16)
            dk_sum[:, inside] = dk_sum[:, inside] + nt(queries, grad)
            dq_sum[...] = dq_sum[...] + nn(keys_t[:, inside], grad)
            return carry

        key_loops(low_ref[at // block], full_ref[at // block], (own + at) // block, step, 0)
        cos, sin = cos_ref[:, here], sin_ref[:, here]
        for r in range(group):
            rounded = (dq_sum[:, r * block : (r + 1) * block] * scale).astype(BF16).astype(F32)
            dq_ref[r * HEAD_SIZE : (r + 1) * HEAD_SIZE, here] = rotated_back(
                rounded, cos, sin
            ).astype(BF16)
    for chunk, dkv_ref in enumerate(dkv_refs):
        at = slice(chunk * piece, (chunk + 1) * piece)
        dkv_ref[0] = (dk_sum[:, at] * (1.0 / LOG2E)).astype(BF16)
        dkv_ref[1] = dv_sum[:, at].astype(BF16)


def attend_back(
    seq, num_seqs, low, full, start, cos, sin, queries, mixed, grad_mixed, lse, kv_chunks, dq, after
):
    width, piece = queries.shape
    kv_heads = kv_chunks[0].shape[1] // HEAD_SIZE
    rows = width // kv_heads
    group = rows // HEAD_SIZE
    block = min(256, piece)
    keys = len(kv_chunks) * piece
    per_head = pl.BlockSpec((rows, piece), lambda h, *_: (h, 0))
    per_head_seq = pl.BlockSpec((rows, piece), lambda h, *_: (h, seq))
    table = pl.BlockSpec((None, HALF, piece), lambda h, *_: (seq, 0, 0))
    kv_spec = pl.BlockSpec((2, HEAD_SIZE, piece), lambda h, *_: (0, h, 0))
    return run(
        functools.partial(attend_back_body, block),
        "attend_back",
        (kv_heads,),
        [
            (start, whole(start)),
            (cos, table),
            (sin, table),
            (queries, per_head),
            (mixed, per_head_seq),
            (grad_mixed, per_head),
            (lse, pl.BlockSpec((None, group, piece), lambda h, *_: (h, 0, 0))),
        ]
        + [(kv, kv_spec) for kv in kv_chunks],
        [
            ((width, num_seqs * piece), BF16, per_head_seq),
        ]
        + [(kv.shape, BF16, kv_spec) for kv in kv_chunks],
        scratch=[
            pltpu.VMEM((keys, HEAD_SIZE), BF16),
            pltpu.VMEM((HEAD_SIZE, keys), BF16),
            pltpu.VMEM((keys, HEAD_SIZE), BF16),
            pltpu.VMEM((HEAD_SIZE, group * block), F32),
            pltpu.VMEM((HEAD_SIZE, keys), F32),
            pltpu.VMEM((HEAD_SIZE, keys), F32),
        ],
        prefetch=[low, full],
        into={0: dq},
        after=after,
    )


def qkv_back_body(
    dq_ref, cos_ref, sin_ref, wq_ref, wk_ref, wv_ref, own_ref, came_ref, *refs
):
    dkv_ref, out_ref, dq_rows, dk_rows, dv_rows = refs
    width = wk_ref.shape[0]

    @pl.when(pl.program_id(0) == 0)
    def _():
        cos, sin = cos_ref[...], sin_ref[...]
        for at in range(0, width, HEAD_SIZE):
            head = slice(at, at + HEAD_SIZE)
            rows = own_ref[0, head].astype(F32) + came_ref[0, head].astype(F32)
            rows = rows.astype(BF16).astype(F32)
            dkv_ref[at : at + HEAD_SIZE, :] = rotated_back(rows, cos, sin).astype(BF16)
        dkv_ref[width:, :] = (own_ref[1].astype(F32) + came_ref[1].astype(F32)).astype(BF16)
        dq_rows[...] = dq_ref[...].T
        dk_rows[...] = dkv_ref[:width].T
        dv_rows[...] = dkv_ref[width:].T

    out_ref[...] = (
        nt(dq_rows[...], wq_ref[...])
        + nn(dk_rows[...], wk_ref[...])
        + nn(dv_rows[...], wv_ref[...])
    ).astype(BF16)


def qkv_back(seq, dq, cos, sin, w_query, key_t, value_t, own, came, dkv, after):
    model, width_q = w_query.shape
    width = key_t.shape[0]
    piece = own.shape[-1]
    tile = 1280
    table = pl.BlockSpec((None, HALF, piece), lambda j: (seq, 0, 0))
    narrow = pl.BlockSpec((width, tile), lambda j: (0, j))
    return run(
        qkv_back_body,
        "qkv_back",
        (model // tile,),
        [
            (dq, pl.BlockSpec((width_q, piece), lambda j: (0, seq))),
            (cos, table),
            (sin, table),
            (w_query, pl.BlockSpec((tile, width_q), lambda j: (j, 0))),
            (key_t, narrow),
            (value_t, narrow),
            (own, whole(own)),
            (came, whole(came)),
        ],
        [
            (
                (2 * width, dq.shape[1]),
                BF16,
                pl.BlockSpec((2 * width, piece), lambda j: (0, seq)),
            ),
            ((piece, model), BF16, pl.BlockSpec((piece, tile), lambda j: (0, j))),
        ],
        scratch=[
            pltpu.VMEM((piece, width_q), BF16),
            pltpu.VMEM((piece, width), BF16),
            pltpu.VMEM((piece, width), BF16),
        ],
        into={0: dkv},
        after=after,
    )


def forward_body(counts, heads, h_ref, gain_ref, wg_ref, wu_ref, wd_ref, *refs):
    o_refs, wo_refs, refs = refs[:heads], refs[heads : 2 * heads], refs[2 * heads :]
    m_ref, nt_ref, z_ref, a_ref, b_ref, part_ref, o_rows, attn, normed, inner = refs
    attn_steps, norm_steps, wide_steps, out_steps = counts
    step = pl.program_id(0)

    @pl.when(step == 0)
    def _():
        for at, o_ref in enumerate(o_refs):
            o_rows[at] = o_ref[...].T

    @in_phase(step, 0, attn_steps)
    def _():
        total = nn(o_rows[0], wo_refs[0][...])
        for at in range(1, heads):
            total = total + nn(o_rows[at], wo_refs[at][...])
        attn[step] = total

    @in_phase(step, attn_steps, norm_steps)
    def _():
        at = pl.ds(pl.multiple_of((step - attn_steps) * ROWS, ROWS), ROWS)
        added = jnp.concatenate([attn[part, at, :] for part in range(attn_steps)], axis=1)
        middle = h_ref[...].astype(F32) + added
        m_ref[...] = middle.astype(BF16)
        rows = (middle * rms_scale(middle) * gain_ref[...]).astype(BF16)
        normed[at, :] = rows
        nt_ref[...] = rows.T

    first = attn_steps + norm_steps

    @in_phase(step, first, wide_steps)
    def _():
        gate = nn(normed[...], wg_ref[...])
        up = nn(normed[...], wu_ref[...])
        sig = jax.nn.sigmoid(gate)
        silu = gate * sig
        z = (silu * up).astype(BF16)
        z_ref[...] = z
        inner[step - first] = z
        a_ref[...] = (up * sig * (1.0 + gate * (1.0 - sig))).astype(BF16)
        b_ref[...] = silu.astype(BF16)

    @in_phase(step, first + wide_steps, out_steps)
    def _():
        width = inner.shape[2]
        total = nn(inner[0], wd_ref[:width])
        for at in range(1, wide_steps):
            total = total + nn(inner[at], wd_ref[at * width : (at + 1) * width])
        part_ref[...] = total.astype(BF16)


def forward_mlp(seq, hidden, gain, w_gate, w_up, w_down, mixed, w_outs, normed_t, inner, after):
    num_seqs, rows, model = hidden.shape
    hidden_width = w_gate.shape[1]
    width = mixed[0].shape[0]
    wide, narrow = divisor(hidden_width, 512), 640
    counts = (model // narrow, rows // ROWS, hidden_width // wide, model // narrow)
    attn, norm, mid, out = (phase(sum(counts[:at]), count) for at, count in enumerate(counts))
    row_spec = pl.BlockSpec((ROWS, model), lambda i: (norm(i), 0))
    weight_spec = pl.BlockSpec((model, wide), lambda i: (0, mid(i)))
    wide_spec = pl.BlockSpec((rows, wide), lambda i: (0, mid(i)))
    return run(
        functools.partial(forward_body, counts, len(mixed)),
        "forward_mlp",
        (sum(counts),),
        [
            (hidden, pl.BlockSpec((None, ROWS, model), lambda i: (seq, norm(i), 0))),
            (gain, whole(gain)),
            (w_gate, weight_spec),
            (w_up, weight_spec),
            (w_down, pl.BlockSpec((hidden_width, narrow), lambda i: (0, out(i)))),
        ]
        + [(part, whole(part)) for part in mixed]
        + [(part, pl.BlockSpec((width, narrow), lambda i: (0, attn(i)))) for part in w_outs],
        [
            ((rows, model), BF16, row_spec),
            (
                (model, num_seqs * rows),
                BF16,
                pl.BlockSpec((model, ROWS), lambda i: (0, seq * counts[1] + norm(i))),
            ),
            (
                (num_seqs, rows, hidden_width),
                BF16,
                pl.BlockSpec((None, rows, wide), lambda i: (seq, 0, mid(i))),
            ),
            ((rows, hidden_width), BF16, wide_spec),
            ((rows, hidden_width), BF16, wide_spec),
            ((rows, model), BF16, pl.BlockSpec((rows, narrow), lambda i: (0, out(i)))),
        ],
        scratch=[
            pltpu.VMEM((len(mixed), rows, width), BF16),
            pltpu.VMEM((counts[0], rows, narrow), F32),
            pltpu.VMEM((rows, model), BF16),
            pltpu.VMEM((counts[2], rows, wide), BF16),
        ],
        into={1: normed_t, 2: inner},
        after=after,
    )


def error_body(m_ref, teacher_ref, valid_ref, *refs):
    *parts, out_ref, dy_ref, dyt_ref, loss_ref = refs
    output = m_ref[...].astype(F32) + total_of(parts)
    out_ref[...] = output.astype(BF16)
    errors = output - teacher_ref[...].astype(F32)
    valid = valid_ref[...]
    rounded = (valid * errors).astype(BF16)
    dy_ref[...] = rounded
    dyt_ref[...] = rounded.T
    squares = jnp.sum(valid * errors * errors, axis=0, keepdims=True)
    accumulate(loss_ref, squares, pl.program_id(0) == 0)


def output_error(seq, middle, teacher, valid, parts, layer_out, grad_t, after):
    num_seqs, rows, model = teacher.shape
    steps = rows // ROWS
    row_spec = pl.BlockSpec((ROWS, model), lambda i: (i, 0))
    seq_spec = pl.BlockSpec((None, ROWS, model), lambda i: (seq, i, 0))
    return run(
        error_body,
        "output_error",
        (steps,),
        [
            (middle, row_spec),
            (teacher, seq_spec),
            (valid, pl.BlockSpec((None, ROWS, 1), lambda i: (seq, i, 0))),
        ]
        + [(part, row_spec) for part in parts],
        [
            ((num_seqs, rows, model), BF16, seq_spec),
            ((rows, model), BF16, row_spec),
            (
                (model, num_seqs * rows),
                BF16,
                pl.BlockSpec((model, ROWS), lambda i: (0, seq * steps + i)),
            ),
            ((1, model), F32, pl.BlockSpec((1, model), lambda i: (0, 0))),
        ],
        into={0: layer_out, 2: grad_t},
        after=after,
    )


def backward_body(counts, dy_ref, wd_ref, a_ref, b_ref, wg_ref, wu_ref, *refs):
    dg_ref, du_ref, part_ref, gates, ups = refs
    wide_steps, out_steps = counts
    step = pl.program_id(0)

    @in_phase(step, 0, wide_steps)
    def _():
        grad_inner = nt(dy_ref[...], wd_ref[...])
        d_gate = (grad_inner * a_ref[...].astype(F32)).astype(BF16)
        d_up = (grad_inner * b_ref[...].astype(F32)).astype(BF16)
        dg_ref[...] = d_gate
        du_ref[...] = d_up
        gates[step] = d_gate
        ups[step] = d_up

    @in_phase(step, wide_steps, out_steps)
    def _():
        width = gates.shape[2]
        total = None
        for at in range(wide_steps):
            columns = slice(at * width, (at + 1) * width)
            term = nt(gates[at], wg_ref[:, columns]) + nt(ups[at], wu_ref[:, columns])
            total = term if total is None else total + term
        part_ref[...] = total.astype(BF16)


def backward_mlp(seq, num_seqs, grad_out, w_down, a, b, w_gate, w_up, kept, after):
    rows, model = grad_out.shape
    hidden_width = w_gate.shape[1]
    wide, narrow = divisor(hidden_width, 512), 512
    counts = (hidden_width // wide, model // narrow)
    mid, out = phase(0, counts[0]), phase(counts[0], counts[1])
    wide_spec = pl.BlockSpec((rows, wide), lambda i: (0, mid(i)))
    wide_seq = pl.BlockSpec((None, rows, wide), lambda i: (seq, 0, mid(i)))
    weight_spec = pl.BlockSpec((narrow, hidden_width), lambda i: (out(i), 0))
    return run(
        functools.partial(backward_body, counts),
        "backward_mlp",
        (sum(counts),),
        [
            (grad_out, whole(grad_out)),
            (w_down, pl.BlockSpec((wide, model), lambda i: (mid(i), 0))),
            (a, wide_spec),
            (b, wide_spec),
            (w_gate, weight_spec),
            (w_up, weight_spec),
        ],
        [
            ((num_seqs, rows, hidden_width), BF16, wide_seq),
            ((num_seqs, rows, hidden_width), BF16, wide_seq),
            ((rows, model), BF16, pl.BlockSpec((rows, narrow), lambda i: (0, out(i)))),
        ],
        scratch=[
            pltpu.VMEM((counts[0], rows, wide), BF16),
            pltpu.VMEM((counts[0], rows, wide), BF16),
        ],
        into=dict(zip((0, 1), kept)),
        after=after,
    )


def middle_back_body(counts, m_ref, dy_ref, gain_ref, w_ref, *refs):
    *parts, dm_ref, dmt_ref, dg_ref, do_ref, grad_t = refs
    norm_steps, out_steps = counts
    step = pl.program_id(0)

    @in_phase(step, 0, norm_steps)
    def _():
        grad_rows, grad_gain = norm_back(
            m_ref[...].astype(F32), gain_ref[...], total_of(parts)
        )
        rounded = (dy_ref[...].astype(F32) + grad_rows).astype(BF16)
        dm_ref[...] = rounded
        rounded_t = rounded.T
        dmt_ref[...] = rounded_t
        grad_t[step] = rounded_t
        accumulate(dg_ref, grad_gain, step == 0)

    @in_phase(step, norm_steps, out_steps)
    def _():
        columns = jnp.concatenate([grad_t[at] for at in range(norm_steps)], axis=1)
        do_ref[...] = nn(w_ref[...], columns).astype(BF16)


def middle_back(seq, num_seqs, middle, grad_output, gain, w_out, parts, grad_t, after):
    rows, model = middle.shape
    width = w_out.shape[0]
    tile = divisor(width, 640)
    counts = (rows // ROWS, width // tile)
    norm, out = phase(0, counts[0]), phase(counts[0], counts[1])
    row_spec = pl.BlockSpec((ROWS, model), lambda i: (norm(i), 0))
    return run(
        functools.partial(middle_back_body, counts),
        "middle_back",
        (sum(counts),),
        [
            (middle, row_spec),
            (grad_output, row_spec),
            (gain, whole(gain)),
            (w_out, pl.BlockSpec((tile, model), lambda i: (out(i), 0))),
        ]
        + [(part, row_spec) for part in parts],
        [
            ((rows, model), BF16, row_spec),
            (
                (model, num_seqs * rows),
                BF16,
                pl.BlockSpec((model, ROWS), lambda i: (0, seq * counts[0] + norm(i))),
            ),
            ((1, model), F32, pl.BlockSpec((1, model), lambda i: (0, 0))),
            ((width, rows), BF16, pl.BlockSpec((tile, rows), lambda i: (out(i), 0))),
        ],
        scratch=[pltpu.VMEM((counts[0], model, ROWS), BF16)],
        into={1: grad_t},
        after=after,
    )


def input_back_body(scale_ref, h_ref, dm_ref, gain_ref, *refs):
    *parts, grad_ref, dg_ref = refs
    grad_rows, grad_gain = norm_back(h_ref[...].astype(F32), gain_ref[...], total_of(parts))
    grad_ref[...] = scale_ref[0] * (dm_ref[...].astype(F32) + grad_rows)
    accumulate(dg_ref, grad_gain, pl.program_id(0) == 0)


def input_back(seq, scale, hidden, grad_middle, gain, parts, earlier, after):
    num_seqs, rows, model = hidden.shape
    row_spec = pl.BlockSpec((ROWS, model), lambda i: (i, 0))
    seq_spec = pl.BlockSpec((None, ROWS, model), lambda i: (seq, i, 0))
    return run(
        input_back_body,
        "input_back",
        (rows // ROWS,),
        [
            (scale, pl.BlockSpec(memory_space=pltpu.SMEM)),
            (hidden, seq_spec),
            (grad_middle, row_spec),
            (gain, whole(gain)),
        ]
        + [(part, row_spec) for part in parts],
        [
            ((num_seqs, rows, model), F32, seq_spec),
            ((1, model), F32, pl.BlockSpec((1, model), lambda i: (0, 0))),
        ],
        into={0: earlier},
        after=after,
    )


def weight_body(flipped, x_ref, y_ref, y_before_ref, far_ref, sent_ref, kept_ref, *refs):
    x_all, staged, landed, send_sem, recv_sem = refs
    tiles = landed.shape[0]
    step = pl.program_id(0)
    dp, ctx = lax.axis_index("dp"), lax.axis_index("ctx")
    ctx_size = lax.axis_size("ctx")
    core, chip = dp % 2, dp // 2
    partner = dp + 1 - 2 * core
    half = x_all.shape[0] // 2

    def sending(at):
        return pltpu.make_async_remote_copy(
            src_ref=staged.at[at % 2],
            dst_ref=landed.at[at],
            send_sem=send_sem.at[at % 2],
            recv_sem=recv_sem.at[at],
            device_id={"dp": partner},
            device_id_type=pl.DeviceIdType.MESH,
        )

    @pl.when(step == 0)
    def _():
        barrier = pltpu.get_barrier_semaphore()
        pl.semaphore_signal(
            barrier, inc=1, device_id={"dp": partner}, device_id_type=pl.DeviceIdType.MESH
        )
        pl.semaphore_wait(barrier, 1)
        size = x_ref.shape[0] // (lax.axis_size("dp") * ctx_size)
        low, high = ctx % 2, ctx // 2
        at = 0
        for other_core in (1, 0):
            to_core = core + other_core * (1 - 2 * core)
            for other_chip in (1, 0):
                to_dp = 2 * (chip + other_chip * (1 - 2 * chip)) + to_core
                for other_low in (1, 0):
                    for other_high in (1, 0):
                        to_ctx = 2 * (high + other_high * (1 - 2 * high))
                        to_ctx = to_ctx + low + other_low * (1 - 2 * low)
                        row = pl.multiple_of((to_dp * ctx_size + to_ctx) * size, size)
                        x_all[at : at + size, :] = x_ref[pl.ds(row, size), :]
                        at += size

    def product(rows, ref):
        y = ref[...]
        return nt(rows, y) if flipped else nn(rows, y.reshape(-1, y.shape[-1]))

    @pl.when((step >= 2) & (step < tiles))
    def _():
        sending(step - 2).wait_send()

    @pl.when(step < tiles)
    def _():
        staged[step % 2] = product(x_all[:half, :], y_ref).astype(BF16)
        sending(step).start()

    @pl.when(step > 0)
    def _():
        total = product(x_all[half:, :], y_before_ref)
        sending(step - 1).wait_recv()
        total = (total + landed[step - 1].astype(F32)).astype(BF16)
        far_ref[...] = total[: half // 2]
        sent_ref[...] = total[half // 2 : half // 4 * 3]
        kept_ref[...] = total[half // 4 * 3 :]

    @pl.when(step == tiles)
    def _():
        for at in range(max(tiles - 2, 0), tiles):
            sending(at).wait_send()


def weight_grad(meets, x_t, y, flipped, after):
    model, tokens = x_t.shape
    if flipped:
        tile = divisor(y.shape[0], 640)
        tiles = y.shape[0] // tile
        y_block, place = (tile, tokens), lambda at: (at, 0)
    else:
        tile = divisor(y.shape[2], 512)
        tiles = y.shape[2] // tile
        y_block, place = y.shape[:2] + (tile,), lambda at: (0, 0, at)
    width = tile * tiles
    before = lambda i: jnp.maximum(i - 1, 0)
    outs = [
        ((rows, width), BF16, pl.BlockSpec((rows, tile), lambda i: (0, before(i))))
        for rows in (model // 4, model // 8, model // 8)
    ]
    return run(
        functools.partial(weight_body, flipped),
        "weight_grad",
        (tiles + 1,),
        [
            (x_t, whole(x_t)),
            (y, pl.BlockSpec(y_block, lambda i: place(jnp.minimum(i, tiles - 1)))),
            (y, pl.BlockSpec(y_block, lambda i: place(before(i)))),
        ],
        outs,
        scratch=[
            pltpu.VMEM((model, tokens), BF16),
            pltpu.VMEM((2, model // 2, tile), BF16),
            pltpu.VMEM((tiles, model // 2, tile), BF16),
            pltpu.SemaphoreType.DMA((2,)),
            pltpu.SemaphoreType.DMA((tiles,)),
        ],
        after=after,
        meets=meets,
    )


def add_body(*refs):
    refs[-1][...] = total_of(refs[:-1]).astype(BF16)


def final_body(scale_ref, *refs):
    count = 4
    total = total_of(refs[:count]) * scale_ref[0]
    at = 0
    for out_ref in refs[count:]:
        out_ref[...] = total[:, at : at + out_ref.shape[1]]
        at += out_ref.shape[1]


def swap(value, axis, bit):
    size = lax.axis_size(axis)
    return lax.ppermute(value, axis, [(i, i ^ bit) for i in range(size)])


class Halving:
    def __init__(self, meets, x_t, y, flipped, after):
        far, self.sent, self.kept = weight_grad(meets, x_t, y, flipped, after)
        self.came = swap(far, "dp", 2)
        self.last = far

    def added(self, name, rows, parts, after):
        width = self.sent.shape[1]
        tile = divisor(width, 1792, 640)
        ins = [
            (
                array,
                pl.BlockSpec((rows, tile), functools.partial(lambda at, j: (at, j), first // rows)),
            )
            for array, first in parts
        ]
        spec = pl.BlockSpec((rows, tile), lambda j: (0, j))
        return run(
            add_body, name, (width // tile,), ins, [((rows, width), BF16, spec)], after=after
        )[0]

    def near(self, after):
        rows = self.sent.shape[0]
        send = self.added("near", rows, [(self.sent, 0), (self.came, 0)], after)
        self.pair = swap(send, "ctx", 1)
        return send

    def fold(self, after):
        rows = self.sent.shape[0] // 2
        parts = [(self.kept, 0), (self.came, 2 * rows), (self.pair, 0)]
        send = self.added("fold", rows, parts, after)
        self.end = swap(send, "ctx", 2)
        return send

    def final(self, scale, widths, after):
        rows, width = self.end.shape
        tile = width if len(widths) > 1 else divisor(width, 896, 640)
        tiles = [(tile,), widths][len(widths) > 1]
        parts = [(self.kept, 1), (self.came, 3), (self.pair, 1), (self.end, 0)]
        self.result = run(
            final_body,
            "final",
            (width // tile,),
            [(scale, pl.BlockSpec(memory_space=pltpu.SMEM))]
            + [
                (part, pl.BlockSpec((rows, tile), functools.partial(lambda at, j: (at, j), at)))
                for part, at in parts
            ],
            [
                ((rows, each), F32, pl.BlockSpec((rows, cut), lambda j: (0, j)))
                for each, cut in zip(widths, tiles)
            ],
            after=after,
        )
        return self.result[0]


def tensor_parts(partial):
    if lax.axis_size("tensor") == 2:
        return [partial, swap(partial, "tensor", 1)]
    return [lax.psum(partial, "tensor")]


def tensor_copies(value):
    if lax.axis_size("tensor") == 2:
        return [value, swap(value, "tensor", 1)]
    return list(lax.all_gather(value, "tensor"))


def tensor_weights(weight, after):
    size, count = lax.axis_size("dp"), weight.shape[0]
    if lax.axis_size("tensor") != 2 or count % (16 * size):
        return list(lax.all_gather(weight, "tensor"))
    rows = count // size
    part = lax.dynamic_slice_in_dim(weight, lax.axis_index("dp") * rows, rows)
    return [weight, lax.all_gather(held(swap(part, "tensor", 1), after), "dp", axis=0, tiled=True)]


def held(value, *others):
    return lax.optimization_barrier((value, *others))[0]


def shift(value, step):
    size = lax.axis_size("ctx")
    pairs = [(i, i + step) for i in range(size) if 0 <= i + step < size]
    return lax.ppermute(value, "ctx", pairs)


def local(
    hidden_in,
    w_query,
    key_weight_matrix,
    value_weight_matrix,
    w_out,
    w_gate,
    w_up,
    w_down,
    attn_gain,
    mlp_gain,
    segments,
    valid_mask,
    teacher,
):
    num_seqs, piece, model = hidden_in.shape
    seqs = range(num_seqs)
    ctx_size = lax.axis_size("ctx")
    ctx = lax.axis_index("ctx")
    query_places = ctx * piece + jnp.arange(piece, dtype=jnp.int32)
    positions = (query_places[None, :] - segments).astype(F32)
    freqs = THETA ** (-2.0 * jnp.arange(HALF, dtype=F32) / HEAD_SIZE)
    angles = positions[:, None, :] * freqs[None, :, None]
    cos, sin = jnp.cos(angles), jnp.sin(angles)
    starts = (segments + (ctx_size - 1 - ctx) * piece)[:, None, :]
    block = min(256, piece)
    lows = starts[:, 0, ::block] // block
    fulls = (starts[:, 0, block - 1 :: block] + block - 1) // block
    attn_gain_row, mlp_gain_row = attn_gain[None, :], mlp_gain[None, :]
    key_t, value_t = key_weight_matrix.T, value_weight_matrix.T
    valid = valid_mask.astype(F32)[..., None]


    normed, queries, kv_chunks = [], [], []
    normed_t, last = None, hidden_in
    for s in seqs:
        n_rows, normed_t, kv_own = kv_project(
            s, hidden_in, attn_gain_row, key_t, value_t, cos, sin, normed_t, [last]
        )
        normed.append(n_rows)
        kv_chunks.append([kv_own])
        last = n_rows
    kv_chunks[0].append(shift(kv_chunks[0][0], 1))
    for s in seqs:
        queries.append(q_project(s, normed[s], w_query, cos, sin, [last, kv_chunks[0][-1]]))
        kv_chunks[0].append(shift(held(kv_chunks[0][-1], last), 1))
        last = queries[-1]
    for s in seqs[1:]:
        own = held(kv_chunks[s][0], kv_chunks[0][-1], last)
        for step in range(1, ctx_size):
            kv_chunks[s].append(shift(own, step))

    made = {"count": jnp.sum(valid_mask).reshape(1, 1)}
    lse, middle, rows_a, rows_b = [], [], [], []
    losses, dys, mlp_gains, attn_gains, grad_middle = [], [], [], [], []
    heads, mlp_parts, dn2_parts, dn1_parts, pieces, came = [], [], [], [], [], [None, None]
    w_outs = tensor_weights(w_out, queries[-1])
    tokens = num_seqs * piece * ctx_size * lax.axis_size("dp")
    last_seq = num_seqs - 1

    def scale():
        return (tokens / made["count"].reshape(()).astype(F32)).reshape(1)

    def attention(s, after):
        heads_out, made["mixed"], lse_rows = attend(
            s,
            num_seqs,
            lows[s],
            fulls[s],
            starts[s],
            queries[s],
            kv_chunks[s][::-1],
            made.get("mixed"),
            after + [made["count"]],
        )
        lse.append(lse_rows)
        heads.append(tensor_copies(heads_out))
        return lse_rows

    def forward(s, after):
        m_rows, made["n2"], made["z"], a, b, partial = forward_mlp(
            s,
            hidden_in,
            mlp_gain_row,
            w_gate,
            w_up,
            w_down,
            heads[s],
            w_outs,
            made.get("n2"),
            made.get("z"),
            after,
        )
        middle.append(m_rows)
        rows_a.append(a)
        rows_b.append(b)
        mlp_parts.append(tensor_parts(partial))
        return m_rows

    def error(s, after):
        made["y"], dy, made["dy"], loss_row = output_error(
            s,
            middle[s],
            teacher,
            valid,
            mlp_parts[s],
            made.get("y"),
            made.get("dy"),
            after + [made["count"]],
        )
        dys.append(dy)
        losses.append(loss_row)
        return dy

    def backward(s, after):
        made["dgate"], made["dup"], partial = backward_mlp(
            s,
            num_seqs,
            dys[s],
            w_down,
            rows_a[s],
            rows_b[s],
            w_gate,
            w_up,
            (made.get("dgate"), made.get("dup")),
            after,
        )
        dn2_parts.append(tensor_parts(partial))
        return partial

    def middle_step(s, after):
        dm, made["dm"], gain_row, made["do", s] = middle_back(
            s,
            num_seqs,
            middle[s],
            dys[s],
            mlp_gain_row,
            w_out,
            dn2_parts[s],
            made.get("dm"),
            after,
        )
        grad_middle.append(dm)
        mlp_gains.append(gain_row)
        return dm

    def attention_back(s, after):
        made["dq"], *parts = attend_back(
            s,
            num_seqs,
            lows[s],
            fulls[s],
            starts[s],
            cos,
            sin,
            queries[s],
            made["mixed"],
            made["do", s],
            lse[s],
            kv_chunks[s][::-1],
            made.get("dq"),
            after,
        )
        pieces.append(parts)
        return parts[0]

    def hop(s, at, after):
        total = pieces[s][at]
        if came[s] is not None:
            total = (total.astype(F32) + held(came[s], *after).astype(F32)).astype(BF16)
        came[s] = shift(total, -1)
        return after[0]

    def projections(s, after):
        made["dkv"], partial = qkv_back(
            s,
            made["dq"],
            cos,
            sin,
            w_query,
            key_t,
            value_t,
            pieces[s][-1],
            came[s],
            made.get("dkv"),
            after,
        )
        dn1_parts.append(tensor_parts(partial))
        return partial

    def halving(name, meets, x_t, y, flipped, after):
        made[name] = Halving(meets, made.get(x_t, normed_t), made[y], flipped, after)
        return made[name].last

    def input_step(s, after):
        made["dx"], gain_row = input_back(
            s,
            scale(),
            hidden_in,
            grad_middle[s],
            attn_gain_row,
            dn1_parts[s],
            made.get("dx"),
            after,
        )
        attn_gains.append(gain_row)
        return gain_row

    def hop_of(name, at, after):
        axis, bit = (("dp", 1), ("dp", 2), ("ctx", 1), ("ctx", 2))[at]
        total = made[name] if name == "count" and at < 2 else held(made[name], *after)
        made[name] = total + swap(total, axis, bit)
        return after[0]

    def small_hop(at, after):
        if at == 0:
            loss = jnp.full((1, model), jnp.sum(sum(losses)))
            made["small"] = jnp.concatenate([sum(attn_gains), sum(mlp_gains), loss], axis=0)
        return hop_of("small", at, after)

    def finish(name, after):
        widths = (made[name].sent.shape[1],)
        if name == "k":
            widths = key_t.shape[:1] * 2
        return made[name].final(scale(), widths, after)

    steps = {
        "Gd": functools.partial(halving, "d", 0, "dy", "z", False),
        "Gg": functools.partial(halving, "g", 3, "n2", "dgate", False),
        "Gu": functools.partial(halving, "u", 4, "n2", "dup", False),
        "Go": functools.partial(halving, "o", 1, "dm", "mixed", True),
        "Gq": functools.partial(halving, "q", 2, "n1", "dq", True),
        "Gk": functools.partial(halving, "k", 5, "n1", "dkv", True),
    }
    for name in "dguoqk":
        for short, stage in (("n", "near"), ("f", "fold")):
            steps[short + name] = lambda after, name=name, stage=stage: getattr(
                made[name], stage
            )(after)
        steps["e" + name] = functools.partial(finish, name)
    for at in range(4):
        steps["s%d" % at] = functools.partial(small_hop, at)
        steps["c%d" % at] = functools.partial(hop_of, "count", at)
    for s in seqs:
        for short, one in (
            ("at", attention),
            ("fw", forward),
            ("er", error),
            ("bw", backward),
            ("mb", middle_step),
            ("ab", attention_back),
            ("qb", projections),
            ("in", input_step),
        ):
            steps[short + str(s)] = functools.partial(one, s)
        for at in range(ctx_size - 1):
            steps["h%d%d" % (s, at)] = functools.partial(hop, s, at)
    for name in ORDER:
        PRESENT[0] = WEIGHTS.get(name, 5)
        last = steps[name]([last])

    (out_sum,), (gate_sum,), (up_sum,), (down_sum,) = (made[name].result for name in "ogud")
    size = model // (lax.axis_size("dp") * ctx_size)
    here = (lax.axis_index("dp") * ctx_size + ctx) * size
    small = made["small"]
    gains = lax.dynamic_slice_in_dim(small[:2], here, size, axis=1) * scale()
    return (
        made["y"],
        small[2, 0] / (made["count"].reshape(()).astype(F32) * model),
        made["dx"],
        *made["q"].result,
        *made["k"].result,
        out_sum.T,
        gate_sum,
        up_sum,
        down_sum.T,
        gains[0],
        gains[1],
    )


def solution(mesh):
    placed = (
        P("dp", "ctx", None),
        P(None, "tensor"),
        P(None, "tensor"),
        P(None, "tensor"),
        P("tensor", None),
        P(None, "tensor"),
        P(None, "tensor"),
        P("tensor", None),
        P(),
        P(),
        P("dp", "ctx"),
        P("dp", "ctx"),
        P("dp", "ctx", None),
    )
    return jax.shard_map(
        local,
        mesh=mesh,
        in_specs=placed,
        out_specs=(
            P("dp", "ctx", None),
            P(),
            P("dp", "ctx", None),
            P(("dp", "ctx"), "tensor"),
            P(("dp", "ctx"), "tensor"),
            P(("dp", "ctx"), "tensor"),
            P("tensor", ("dp", "ctx")),
            P(("dp", "ctx"), "tensor"),
            P(("dp", "ctx"), "tensor"),
            P("tensor", ("dp", "ctx")),
            P(("dp", "ctx")),
            P(("dp", "ctx")),
        ),
        check_vma=False,
    )
```

profile of v0, /device:TPU:0, one launch (start us, length us, event | category | flops | bytes accessed | tf_op | source)
XLA Modules:
  0.0 981.2 jit_solution(14155548155777655681)
XLA Ops:
  10.6 6.5 kv_project.2
  17.2 5.0 collective-permute-start
  26.4 6.5 kv_project.3
  40.7 8.4 q_project.2.refs_4_.refs_3_.refs_5_
  49.1 4.7 collective-permute-done.1.refs_5_.refs_10_
  54.6 8.4 q_project.3.refs_8_.refs_3_.refs_5_
  65.0 4.4 collective-permute-start.2
  76.2 8.2 collective-permute-done.2.refs_4_.refs_9_
  84.4 7.2 collective-permute-start.3
  96.6 11.4 %attend.2 = (bf16[1280,512]{1,0:T(8,128)(2,1)}, bf16[1280,1024]{1,0:T(8,128)(2,1)}, f32[4,4,512]{2,1,0:T(4,128)}) custom-call(s32[2]{0:T(128)} %get-tuple-element.223.refs_0_, s32[2]{0:T(128)} %get-tuple-element.218.refs_1_, s32[1,512]{1,0:T(1,128)} %get-tuple-element.212.refs_2_, bf16[1280,512]{1,0:T(8,128)(2,1)} %q_project.2.refs_4_.refs_3_.refs_5_, ...), custom_call_target="tpu_custom_call" | custom-call | flops 60000002048 | bytes 1000 | tf_op jit(solution)/shard_map/attend/pallas_call | solution.py:46
  109.5 10.4 %collective-permute-done.4.refs_5_.refs_10_ = bf16[2,320,512]{2,1,0:T(8,128)(2,1)} collective-permute-done((bf16[2,320,512]{2,1,0:T(8,128)(2,1)S(1)}, bf16[2,320,512]{2,1,0:T(8,128)(2,1)}, u32[]{:S(2)}, u32[]{:S(2)}) %collective-permute-start.4) | collective-permute-done | bytes 655392 | tf_op jit(solution)/shard_map/ppermute | solution.py:975
  120.0 12.9 %collective-permute-done.5.refs_6_.refs_11_ = bf16[2,320,512]{2,1,0:T(8,128)(2,1)} collective-permute-done((bf16[2,320,512]{2,1,0:T(8,128)(2,1)S(1)}, bf16[2,320,512]{2,1,0:T(8,128)(2,1)}, u32[]{:S(2)}, u32[]{:S(2)}) %collective-permute-start.5) | collective-permute-done | bytes 655392 | tf_op jit(solution)/shard_map/ppermute | solution.py:975
  132.9 8.9 attend.3
  144.9 56.6 %forward_mlp.2 = (bf16[512,2560]{1,0:T(8,128)(2,1)}, bf16[2560,1024]{1,0:T(8,128)(2,1)}, bf16[2,512,3584]{2,1,0:T(8,128)(2,1)}, bf16[512,3584]{1,0:T(8,128)(2,1)...) custom-call(bf16[2,512,2560]{2,1,0:T(8,128)(2,1)} %refs_1_.15, f32[1,2560]{1,0:T(1,128)} %broadcast_in_dim.18.refs_1_.refs_2_, ...), custom_call_target="tpu_custom_call" | custom-call | flops 1000 | bytes 1000 | tf_op jit(solution)/shard_map/forward_mlp/pallas_call | solution.py:46
  203.2 57.0 %forward_mlp.3 = (bf16[512,2560]{1,0:T(8,128)(2,1)}, bf16[2560,1024]{1,0:T(8,128)(2,1)}, bf16[2,512,3584]{2,1,0:T(8,128)(2,1)}, bf16[512,3584]{1,0:T(8,128)(2,1)...) custom-call(bf16[2,512,2560]{2,1,0:T(8,128)(2,1)} %refs_1_.15, ...), custom_call_target="tpu_custom_call", output_to_operand_aliasing={{1}: (9, {}), {2}: (10, {})} | custom-call | flops 1000 | bytes 1000 | tf_op jit(solution)/shard_map/forward_mlp/pallas_call | solution.py:46
  262.8 21.9 %collective-permute-start.13 = (s32[1,1]{1,0:T(1,128)}, s32[1,1]{1,0:T(1,128)}, u32[]{:S(2)}, u32[]{:S(2)}) collective-permute-start(s32[1,1]{1,0:T(1,128)} %add.82.refs_9_.refs_10_), channel_id=1, source_target_pairs={{0,2},{2,0},{4,6},{6,4},{1,3},{3,1},{5,7},{7,5},{8,10},{10,8},{12,... | collective-permute-start | bytes 20 | tf_op jit(solution)/shard_map/ppermute | solution.py:887
  285.5 5.4 collective-permute-start.14
  291.8 8.2 output_error.2
  300.1 40.4 %backward_mlp.2 = (bf16[2,512,3584]{2,1,0:T(8,128)(2,1)}, bf16[2,512,3584]{2,1,0:T(8,128)(2,1)}, bf16[512,2560]{1,0:T(8,128)(2,1)}) custom-call(bf16[512,2560]{1,0:T(8,128)(2,1)} %get-tuple-element.134.refs_0_.refs_6_.refs_1_, bf16[3584,2560]{1,0:T(8,128)(2,1)} %refs_1_.13, bf16[512,3584]{1,0:T(8,128)(2,1)} %get-tuple-element.135.refs_2_, ...), custom_call_target="tpu_custom_call" | custom-call | flops 1000 | bytes 1000 | tf_op jit(solution)/shard_map/backward_mlp/pallas_call | solution.py:46
  342.4 8.2 output_error.3
  350.6 30.1 %weight_grad.6 = (bf16[640,3584]{1,0:T(8,128)(2,1)}, bf16[320,3584]{1,0:T(8,128)(2,1)}, bf16[320,3584]{1,0:T(8,128)(2,1)}) custom-call(bf16[2560,1024]{1,0:T(8,128)(2,1)} %get-tuple-element.145.refs_0_, bf16[2,512,3584]{2,1,0:T(8,128)(2,1)} %get-tuple-element.146.refs_1_.refs_2_, bf16[2,512,3584]{2,1,0:T(8,128)(2,1)} %get-tuple-element.146.refs_1_.refs_2_, ...), custom_call_target="tpu_custom_call" | custom-call | flops 5000001024 | bytes 1000 | tf_op jit(solution)/shard_map/weight_grad/pallas_call | solution.py:46
  380.8 16.8 %collective-permute-start.17 = (bf16[640,3584]{1,0:T(8,128)(2,1)}, bf16[640,3584]{1,0:T(8,128)(2,1)}, u32[]{:S(2)}, u32[]{:S(2)}) collective-permute-start(bf16[640,3584]{1,0:T(8,128)(2,1)} %get-tuple-element.147.refs_8_), channel_id=1, source_target_pairs={{0,16},{8,24},{16,0},{24,8},{1,17},{9,25},{17,1},{25,9},{2,18},{10... | collective-permute-start | bytes 13762568 | tf_op jit(solution)/shard_map/ppermute | solution.py:887
  397.6 40.4 %backward_mlp.3 = (bf16[2,512,3584]{2,1,0:T(8,128)(2,1)}, bf16[2,512,3584]{2,1,0:T(8,128)(2,1)}, bf16[512,2560]{1,0:T(8,128)(2,1)}) custom-call(bf16[512,2560]{1,0:T(8,128)(2,1)} %get-tuple-element.140.refs_3_.refs_0_.refs_1_, bf16[3584,2560]{1,0:T(8,128)(2,1)} %refs_1_.13, ...), custom_call_target="tpu_custom_call", output_to_operand_aliasing={{0}: (6, {}), {1}: (7, {})} | custom-call | flops 2000001024 | bytes 1000 | tf_op jit(solution)/shard_map/backward_mlp/pallas_call | solution.py:46
  439.5 30.0 %weight_grad.7 = (bf16[640,3584]{1,0:T(8,128)(2,1)}, bf16[320,3584]{1,0:T(8,128)(2,1)}, bf16[320,3584]{1,0:T(8,128)(2,1)}) custom-call(bf16[2560,1024]{1,0:T(8,128)(2,1)} %get-tuple-element.139.refs_0_, bf16[2,512,3584]{2,1,0:T(8,128)(2,1)} %get-tuple-element.148.refs_1_.refs_2_, bf16[2,512,3584]{2,1,0:T(8,128)(2,1)} %get-tuple-element.148.refs_1_.refs_2_, ...), custom_call_target="tpu_custom_call" | custom-call | flops 99999997952 | bytes 1000 | tf_op jit(solution)/shard_map/weight_grad/pallas_call | solution.py:46
  469.8 13.9 %middle_back.2 = (bf16[512,2560]{1,0:T(8,128)(2,1)}, bf16[2560,1024]{1,0:T(8,128)(2,1)}, f32[1,2560]{1,0:T(1,128)}, bf16[1280,512]{1,0:T(8,128)(2,1)}) custom-call(bf16[512,2560]{1,0:T(8,128)(2,1)} %get-tuple-element.126.refs_11_.refs_0_, bf16[512,2560]{1,0:T(8,128)(2,1)} %get-tuple-element.134.refs_0_.refs_6_.refs_1_, ...), custom_call_target="tpu_custom_call" | custom-call | flops 99999997952 | bytes 1000 | tf_op jit(solution)/shard_map/middle_back/pallas_call | solution.py:46
  483.7 16.1 %attend_back.2 = (bf16[1280,1024]{1,0:T(8,128)(2,1)}, bf16[2,320,512]{2,1,0:T(8,128)(2,1)}, bf16[2,320,512]{2,1,0:T(8,128)(2,1)}, bf16[2,320,512]{2,1,0:T(8,128)(2,1)}, bf16[2,320,512]{2,1,0:T(8,128)(2,1)}) custom-call(s32[2]{0:T(128)} %get-tuple-element.223.refs_0_, s32[2]{0:T(128)} %get-tuple-element.218.refs_1_, s32[1,512]{1,0:T(1,128)} %get-tuple-element.212.refs_2_, ...), custom_call_target="tpu_custom_call" | custom-call | flops 1000 | bytes 1000 | tf_op jit(solution)/shard_map/attend_back/pallas_call | solution.py:46
  504.7 13.7 %collective-permute-start.21 = (bf16[320,3584]{1,0:T(8,128)(2,1)}, bf16[320,3584]{1,0:T(8,128)(2,1)S(1)}, u32[]{:S(2)}, u32[]{:S(2)}) collective-permute-start(bf16[320,3584]{1,0:T(8,128)(2,1)} %near.6.refs_7_), channel_id=1, source_target_pairs={{0,2},{2,0},{4,6},{6,4},{1,3},{3,1},{5,7},{7,5},{8,10},{10,8},{12,... | collective-permute-start | bytes 6881288 | tf_op jit(solution)/shard_map/ppermute | solution.py:887
  518.4 14.0 %middle_back.3 = (bf16[512,2560]{1,0:T(8,128)(2,1)}, bf16[2560,1024]{1,0:T(8,128)(2,1)}, f32[1,2560]{1,0:T(1,128)}, bf16[1280,512]{1,0:T(8,128)(2,1)}) custom-call(bf16[512,2560]{1,0:T(8,128)(2,1)} %get-tuple-element.127.refs_5_.refs_0_, bf16[512,2560]{1,0:T(8,128)(2,1)} %get-tuple-element.140.refs_3_.refs_0_.refs_1_, ...), custom_call_target="tpu_custom_call", output_to_operand_aliasing={{1}: (6, {})} | custom-call | flops 5000001024 | bytes 1000 | tf_op jit(solution)/shard_map/middle_back/pallas_call | solution.py:46
  535.8 12.4 %attend_back.3 = (bf16[1280,1024]{1,0:T(8,128)(2,1)}, bf16[2,320,512]{2,1,0:T(8,128)(2,1)}, bf16[2,320,512]{2,1,0:T(8,128)(2,1)}, bf16[2,320,512]{2,1,0:T(8,128)(2,1)}, bf16[2,320,512]{2,1,0:T(8,128)(2,1)}) custom-call(s32[2]{0:T(128)} %get-tuple-element.222.refs_0_, s32[2]{0:T(128)} %get-tuple-element.219.refs_1_, ...), custom_call_target="tpu_custom_call", output_to_operand_aliasing={{0}: (13, {})} | custom-call | flops 15000000512 | bytes 1000 | tf_op jit(solution)/shard_map/attend_back/pallas_call | solution.py:46
  549.6 46.3 %collective-permute-done.22.refs_1_.refs_2_ = bf16[640,3584]{1,0:T(8,128)(2,1)} collective-permute-done((bf16[640,3584]{1,0:T(8,128)(2,1)}, bf16[640,3584]{1,0:T(8,128)(2,1)}, u32[]{:S(2)}, u32[]{:S(2)}) %collective-permute-start.22) | collective-permute-done | bytes 4587552 | tf_op jit(solution)/shard_map/ppermute | solution.py:887
  604.8 29.9 %weight_grad.8 = (bf16[640,3584]{1,0:T(8,128)(2,1)}, bf16[320,3584]{1,0:T(8,128)(2,1)}, bf16[320,3584]{1,0:T(8,128)(2,1)}) custom-call(bf16[2560,1024]{1,0:T(8,128)(2,1)} %get-tuple-element.139.refs_0_, bf16[2,512,3584]{2,1,0:T(8,128)(2,1)} %get-tuple-element.169.refs_1_.refs_2_, bf16[2,512,3584]{2,1,0:T(8,128)(2,1)} %get-tuple-element.169.refs_1_.refs_2_, ...), custom_call_target="tpu_custom_call" | custom-call | flops 1000 | bytes 1000 | tf_op jit(solution)/shard_map/weight_grad/pallas_call | solution.py:46
  645.1 23.3 %collective-permute-start.28 = (bf16[160,3584]{1,0:T(8,128)(2,1)}, bf16[160,3584]{1,0:T(8,128)(2,1)}, u32[]{:S(2)}, u32[]{:S(2)}) collective-permute-start(bf16[160,3584]{1,0:T(8,128)(2,1)} %fold.6.refs_3_), channel_id=1, source_target_pairs={{0,4},{2,6},{4,0},{6,2},{1,5},{3,7},{5,1},{7,3},{8,12},{10,14},{12... | collective-permute-start | bytes 3440648 | tf_op jit(solution)/shard_map/ppermute | solution.py:887
  668.5 15.5 %weight_grad.9 = (bf16[640,1280]{1,0:T(8,128)(2,1)}, bf16[320,1280]{1,0:T(8,128)(2,1)}, bf16[320,1280]{1,0:T(8,128)(2,1)}) custom-call(bf16[2560,1024]{1,0:T(8,128)(2,1)} %get-tuple-element.167.refs_0_, bf16[1280,1024]{1,0:T(8,128)(2,1)} %get-tuple-element.152.refs_6_.refs_1_.refs_2_, bf16[1280,1024]{1,0:T(8,128)(2,1)} %get-tuple-element.152.refs_6_.refs_1_.refs_2_, ...), custom_call_target="tpu_custom_call" | custom-call | flops 1000 | bytes 1000 | tf_op jit(solution)/shard_map/weight_grad/pallas_call | solution.py:46
  684.0 15.5 %weight_grad.10 = (bf16[640,1280]{1,0:T(8,128)(2,1)}, bf16[320,1280]{1,0:T(8,128)(2,1)}, bf16[320,1280]{1,0:T(8,128)(2,1)}) custom-call(bf16[2560,1024]{1,0:T(8,128)(2,1)} %get-tuple-element.166.refs_0_, bf16[1280,1024]{1,0:T(8,128)(2,1)} %get-tuple-element.160.refs_1_.refs_2_.refs_0_, bf16[1280,1024]{1,0:T(8,128)(2,1)} %get-tuple-element.160.refs_1_.refs_2_.refs_0_, ...), custom_call_target="tpu_custom_call" | custom-call | flops 500000992 | bytes 1000 | tf_op jit(solution)/shard_map/weight_grad/pallas_call | solution.py:46
  701.5 11.7 %qkv_back.2 = (bf16[640,1024]{1,0:T(8,128)(2,1)}, bf16[512,2560]{1,0:T(8,128)(2,1)}) custom-call(bf16[1280,1024]{1,0:T(8,128)(2,1)} %get-tuple-element.160.refs_1_.refs_2_.refs_0_, f32[2,40,512]{2,1,0:T(8,128)} %get-tuple-element.209.refs_4_.refs_2_.refs_3_.refs_1_, f32[2,40,512]{2,1,0:T(8,128)} %get-tuple-element.208.refs_5_.refs_3_.refs_4_.refs_2_, ...), custom_call_target="tpu_custom_call" | custom-call | flops 15000000512 | bytes 1000 | tf_op jit(solution)/shard_map/qkv_back/pallas_call | solution.py:46
  718.6 4.5 final.6.refs_9_
  723.1 32.4 %collective-permute-done.27.refs_7_ = bf16[2,320,512]{2,1,0:T(8,128)(2,1)S(1)} collective-permute-done((bf16[2,320,512]{2,1,0:T(8,128)(2,1)S(1)}, bf16[2,320,512]{2,1,0:T(8,128)(2,1)S(1)}, u32[]{:S(2)}, u32[]{:S(2)}) %collective-permute-start.27) | collective-permute-done | bytes 655392 | tf_op jit(solution)/shard_map/ppermute | solution.py:975
  756.3 11.6 %qkv_back.3 = (bf16[640,1024]{1,0:T(8,128)(2,1)}, bf16[512,2560]{1,0:T(8,128)(2,1)}) custom-call(bf16[1280,1024]{1,0:T(8,128)(2,1)} %get-tuple-element.160.refs_1_.refs_2_.refs_0_, f32[2,40,512]{2,1,0:T(8,128)} %get-tuple-element.209.refs_4_.refs_2_.refs_3_.refs_1_, ...), custom_call_target="tpu_custom_call", output_to_operand_aliasing={{0}: (8, {})} | custom-call | flops 5000001024 | bytes 1000 | tf_op jit(solution)/shard_map/qkv_back/pallas_call | solution.py:46
  767.9 12.9 %weight_grad.11 = (bf16[640,640]{1,0:T(8,128)(2,1)}, bf16[320,640]{1,0:T(8,128)(2,1)}, bf16[320,640]{1,0:T(8,128)(2,1)}) custom-call(bf16[2560,1024]{1,0:T(8,128)(2,1)} %get-tuple-element.166.refs_0_, bf16[640,1024]{1,0:T(8,128)(2,1)} %get-tuple-element.184.refs_1_.refs_2_, bf16[640,1024]{1,0:T(8,128)(2,1)} %get-tuple-element.184.refs_1_.refs_2_, ...), custom_call_target="tpu_custom_call" | custom-call | flops 2000001024 | bytes 1000 | tf_op jit(solution)/shard_map/weight_grad/pallas_call | solution.py:46
  785.0 9.0 input_back.2
  797.9 9.2 collective-permute-done.32.refs_1_.refs_2_
  812.1 44.9 %collective-permute-done.31.refs_2_.refs_3_ = bf16[320,3584]{1,0:T(8,128)(2,1)S(1)} collective-permute-done((bf16[320,3584]{1,0:T(8,128)(2,1)}, bf16[320,3584]{1,0:T(8,128)(2,1)S(1)}, u32[]{:S(2)}, u32[]{:S(2)}) %collective-permute-start.31) | collective-permute-done | bytes 2293792 | tf_op jit(solution)/shard_map/ppermute | solution.py:887
  861.6 9.1 input_back.3
  871.5 4.5 final.7.refs_2_
  878.1 38.5 %collective-permute-done.38.refs_2_.refs_3_ = bf16[320,1280]{1,0:T(8,128)(2,1)} collective-permute-done((bf16[320,1280]{1,0:T(8,128)(2,1)}, bf16[320,1280]{1,0:T(8,128)(2,1)}, u32[]{:S(2)}, u32[]{:S(2)}) %collective-permute-start.38) | collective-permute-done | bytes 819232 | tf_op jit(solution)/shard_map/ppermute | solution.py:887
  924.3 4.4 final.8.refs_3_
  941.6 15.6 %collective-permute-done.44.refs_4_ = bf16[160,1280]{1,0:T(8,128)(2,1)S(1)} collective-permute-done((bf16[160,1280]{1,0:T(8,128)(2,1)}, bf16[160,1280]{1,0:T(8,128)(2,1)S(1)}, u32[]{:S(2)}, u32[]{:S(2)}) %collective-permute-start.44) | collective-permute-done | bytes 409632 | tf_op jit(solution)/shard_map/ppermute | solution.py:887
  962.2 4.7 collective-permute-done.43.refs_4_
  (185 shorter events, 129.5 us)
Async XLA Ops:
  7.2 136.7 %all-gather.2.cloned.1.call-start = ((), (), s32[]{:S(2)}) async-start(), calls=%async_computation | async-start | bytes 8192000 | tf_op jit(solution)/shard_map/all_gather | solution.py:965
  17.2 19.2 %collective-permute-start = (bf16[2,320,512]{2,1,0:T(8,128)(2,1)}, bf16[2,320,512]{2,1,0:T(8,128)(2,1)S(1)}, u32[]{:S(2)}, u32[]{:S(2)}) collective-permute-start(bf16[2,320,512]{2,1,0:T(8,128)(2,1)} %get-tuple-element.113.refs_7_.refs_12_), channel_id=1, source_target_pairs={{0,2},{2,4},{4,6},{1,3},{3,5},{5,7},{8,10},{10,12},{12,14},{9,11},... | collective-permute-start | bytes 1966088 | tf_op jit(solution)/shard_map/ppermute | solution.py:975
  24.9 38.1 %collective-permute-start.9 = (bf16[320,2560]{1,0:T(8,128)(2,1)}, bf16[320,2560]{1,0:T(8,128)(2,1)S(1)}, u32[]{:S(2)}, u32[]{:S(2)}) collective-permute-start(bf16[320,2560]{1,0:T(8,128)(2,1)} %constant_dynamic-slice_fusion), channel_id=1, source_target_pairs={{0,1},{1,0},{2,3},{3,2},{4,5},{5,4},{6,7},{7,6},{8,9},{9,8},{10,11... | collective-permute-start | bytes 4915208 | tf_op jit(solution)/shard_map/ppermute | solution.py:887
  36.4 17.4 %collective-permute-start.1 = (bf16[2,320,512]{2,1,0:T(8,128)(2,1)S(1)}, bf16[2,320,512]{2,1,0:T(8,128)(2,1)S(1)}, u32[]{:S(2)}, u32[]{:S(2)}) collective-permute-start(bf16[2,320,512]{2,1,0:T(8,128)(2,1)S(1)} %collective-permute-done.refs_5_.refs_6_.refs_11_), channel_id=1, source_target_pairs={{0,2},{2,4},{4,6},{1,3},{3,5},{5,7},{8,10},{10,12},{12,14},{9,11},... | collective-permute-start | bytes 1966088 | tf_op jit(solution)/shard_map/ppermute | solution.py:975
  64.8 5.8 collective-permute-start.6
  65.0 19.4 %collective-permute-start.2 = (bf16[2,320,512]{2,1,0:T(8,128)(2,1)}, bf16[2,320,512]{2,1,0:T(8,128)(2,1)S(1)}, u32[]{:S(2)}, u32[]{:S(2)}) collective-permute-start(bf16[2,320,512]{2,1,0:T(8,128)(2,1)} %copy-done.8), channel_id=1, source_target_pairs={{0,2},{2,4},{4,6},{1,3},{3,5},{5,7},{8,10},{10,12},{12,14},{9,11},... | collective-permute-start | bytes 1966088 | tf_op jit(solution)/shard_map/ppermute | solution.py:975
  72.0 3.6 collective-permute-start.7
  84.4 25.1 %collective-permute-start.3 = (bf16[2,320,512]{2,1,0:T(8,128)(2,1)S(1)}, bf16[2,320,512]{2,1,0:T(8,128)(2,1)}, u32[]{:S(2)}, u32[]{:S(2)}) collective-permute-start(bf16[2,320,512]{2,1,0:T(8,128)(2,1)S(1)} %copy-done.24), channel_id=1, source_target_pairs={{0,6},{1,7},{8,14},{9,15},{16,22},{17,23},{24,30},{25,31}} | collective-permute-start | bytes 1966088 | tf_op jit(solution)/shard_map/ppermute | solution.py:975
  91.6 28.3 %collective-permute-start.4 = (bf16[2,320,512]{2,1,0:T(8,128)(2,1)S(1)}, bf16[2,320,512]{2,1,0:T(8,128)(2,1)}, u32[]{:S(2)}, u32[]{:S(2)}) collective-permute-start(bf16[2,320,512]{2,1,0:T(8,128)(2,1)S(1)} %copy-done.24), channel_id=1, source_target_pairs={{0,4},{2,6},{1,5},{3,7},{8,12},{10,14},{9,13},{11,15},{16,20},{18,... | collective-permute-start | bytes 1966088 | tf_op jit(solution)/shard_map/ppermute | solution.py:975
  93.8 39.1 %collective-permute-start.5 = (bf16[2,320,512]{2,1,0:T(8,128)(2,1)S(1)}, bf16[2,320,512]{2,1,0:T(8,128)(2,1)}, u32[]{:S(2)}, u32[]{:S(2)}) collective-permute-start(bf16[2,320,512]{2,1,0:T(8,128)(2,1)S(1)} %copy-done.24), channel_id=1, source_target_pairs={{0,2},{2,4},{4,6},{1,3},{3,5},{5,7},{8,10},{10,12},{12,14},{9,11},... | collective-permute-start | bytes 1966088 | tf_op jit(solution)/shard_map/ppermute | solution.py:975
  108.0 35.9 %collective-permute-start.10 = (bf16[1280,512]{1,0:T(8,128)(2,1)}, bf16[1280,512]{1,0:T(8,128)(2,1)S(1)}, u32[]{:S(2)}, u32[]{:S(2)}) collective-permute-start(bf16[1280,512]{1,0:T(8,128)(2,1)} %get-tuple-element.122.refs_5_), channel_id=1, source_target_pairs={{0,1},{1,0},{2,3},{3,2},{4,5},{5,4},{6,7},{7,6},{8,9},{9,8},{10,11... | collective-permute-start | bytes 3932168 | tf_op jit(solution)/shard_map/ppermute | solution.py:887
  141.8 60.4 %collective-permute-start.8 = (bf16[1280,512]{1,0:T(8,128)(2,1)}, bf16[1280,512]{1,0:T(8,128)(2,1)S(1)}, u32[]{:S(2)}, u32[]{:S(2)}) collective-permute-start(bf16[1280,512]{1,0:T(8,128)(2,1)} %get-tuple-element.120.refs_5_), channel_id=1, source_target_pairs={{0,1},{1,0},{2,3},{3,2},{4,5},{5,4},{6,7},{7,6},{8,9},{9,8},{10,11... | collective-permute-start | bytes 3932168 | tf_op jit(solution)/shard_map/ppermute | solution.py:887
  201.6 90.2 %collective-permute-start.12 = (bf16[512,2560]{1,0:T(8,128)(2,1)}, bf16[512,2560]{1,0:T(8,128)(2,1)}, u32[]{:S(2)}, u32[]{:S(2)}) collective-permute-start(bf16[512,2560]{1,0:T(8,128)(2,1)} %get-tuple-element.129.refs_3_), channel_id=1, source_target_pairs={{0,1},{1,0},{2,3},{3,2},{4,5},{5,4},{6,7},{7,6},{8,9},{9,8},{10,11... | collective-permute-start | bytes 7864328 | tf_op jit(solution)/shard_map/ppermute | solution.py:887
  260.2 80.7 %collective-permute-start.11 = (bf16[512,2560]{1,0:T(8,128)(2,1)}, bf16[512,2560]{1,0:T(8,128)(2,1)S(1)}, u32[]{:S(2)}, u32[]{:S(2)}) collective-permute-start(bf16[512,2560]{1,0:T(8,128)(2,1)} %get-tuple-element.128.refs_3_), channel_id=1, source_target_pairs={{0,1},{1,0},{2,3},{3,2},{4,5},{5,4},{6,7},{7,6},{8,9},{9,8},{10,11... | collective-permute-start | bytes 7864328 | tf_op jit(solution)/shard_map/ppermute | solution.py:887
  262.8 22.1 %collective-permute-start.13 = (s32[1,1]{1,0:T(1,128)}, s32[1,1]{1,0:T(1,128)}, u32[]{:S(2)}, u32[]{:S(2)}) collective-permute-start(s32[1,1]{1,0:T(1,128)} %add.82.refs_9_.refs_10_), channel_id=1, source_target_pairs={{0,2},{2,0},{4,6},{6,4},{1,3},{3,1},{5,7},{7,5},{8,10},{10,8},{12,... | collective-permute-start | bytes 20 | tf_op jit(solution)/shard_map/ppermute | solution.py:887
  285.5 5.6 collective-permute-start.14
  340.4 129.4 %collective-permute-start.15 = (bf16[512,2560]{1,0:T(8,128)(2,1)}, bf16[512,2560]{1,0:T(8,128)(2,1)}, u32[]{:S(2)}, u32[]{:S(2)}) collective-permute-start(bf16[512,2560]{1,0:T(8,128)(2,1)} %get-tuple-element.137.refs_7_.refs_4_), channel_id=1, source_target_pairs={{0,1},{1,0},{2,3},{3,2},{4,5},{5,4},{6,7},{7,6},{8,9},{9,8},{10,11... | collective-permute-start | bytes 7864328 | tf_op jit(solution)/shard_map/ppermute | solution.py:887
  380.8 120.3 %collective-permute-start.17 = (bf16[640,3584]{1,0:T(8,128)(2,1)}, bf16[640,3584]{1,0:T(8,128)(2,1)}, u32[]{:S(2)}, u32[]{:S(2)}) collective-permute-start(bf16[640,3584]{1,0:T(8,128)(2,1)} %get-tuple-element.147.refs_8_), channel_id=1, source_target_pairs={{0,16},{8,24},{16,0},{24,8},{1,17},{9,25},{17,1},{25,9},{2,18},{10... | collective-permute-start | bytes 13762568 | tf_op jit(solution)/shard_map/ppermute | solution.py:887
  438.0 80.5 %collective-permute-start.16 = (bf16[512,2560]{1,0:T(8,128)(2,1)}, bf16[512,2560]{1,0:T(8,128)(2,1)}, u32[]{:S(2)}, u32[]{:S(2)}) collective-permute-start(bf16[512,2560]{1,0:T(8,128)(2,1)} %get-tuple-element.149.refs_3_.refs_4_), channel_id=1, source_target_pairs={{0,1},{1,0},{2,3},{3,2},{4,5},{5,4},{6,7},{7,6},{8,9},{9,8},{10,11... | collective-permute-start | bytes 7864328 | tf_op jit(solution)/shard_map/ppermute | solution.py:887
  469.5 126.4 %collective-permute-start.22 = (bf16[640,3584]{1,0:T(8,128)(2,1)}, bf16[640,3584]{1,0:T(8,128)(2,1)}, u32[]{:S(2)}, u32[]{:S(2)}) collective-permute-start(bf16[640,3584]{1,0:T(8,128)(2,1)} %get-tuple-element.150.refs_6_), channel_id=1, source_target_pairs={{0,16},{8,24},{16,0},{24,8},{1,17},{9,25},{17,1},{25,9},{2,18},{10... | collective-permute-start | bytes 13762568 | tf_op jit(solution)/shard_map/ppermute | solution.py:887
  499.8 32.6 %collective-permute-start.18 = (bf16[2,320,512]{2,1,0:T(8,128)(2,1)}, bf16[2,320,512]{2,1,0:T(8,128)(2,1)}, u32[]{:S(2)}, u32[]{:S(2)}) collective-permute-start(bf16[2,320,512]{2,1,0:T(8,128)(2,1)} %get-tuple-element.156.refs_2_), channel_id=1, source_target_pairs={{2,0},{4,2},{6,4},{3,1},{5,3},{7,5},{10,8},{12,10},{14,12},{11,9},... | collective-permute-start | bytes 1966088 | tf_op jit(solution)/shard_map/ppermute | solution.py:975
  504.7 135.9 %collective-permute-start.21 = (bf16[320,3584]{1,0:T(8,128)(2,1)}, bf16[320,3584]{1,0:T(8,128)(2,1)S(1)}, u32[]{:S(2)}, u32[]{:S(2)}) collective-permute-start(bf16[320,3584]{1,0:T(8,128)(2,1)} %near.6.refs_7_), channel_id=1, source_target_pairs={{0,2},{2,0},{4,6},{6,4},{1,3},{3,1},{5,7},{7,5},{8,10},{10,8},{12,... | collective-permute-start | bytes 6881288 | tf_op jit(solution)/shard_map/ppermute | solution.py:887
  534.6 65.0 %collective-permute-start.19 = (bf16[2,320,512]{2,1,0:T(8,128)(2,1)}, bf16[2,320,512]{2,1,0:T(8,128)(2,1)}, u32[]{:S(2)}, u32[]{:S(2)}) collective-permute-start(bf16[2,320,512]{2,1,0:T(8,128)(2,1)} %add_convert_fusion.3), channel_id=1, source_target_pairs={{2,0},{4,2},{6,4},{3,1},{5,3},{7,5},{10,8},{12,10},{14,12},{11,9},... | collective-permute-start | bytes 1966088 | tf_op jit(solution)/shard_map/ppermute | solution.py:975
  548.3 88.9 %collective-permute-start.25 = (bf16[2,320,512]{2,1,0:T(8,128)(2,1)}, bf16[2,320,512]{2,1,0:T(8,128)(2,1)}, u32[]{:S(2)}, u32[]{:S(2)}) collective-permute-start(bf16[2,320,512]{2,1,0:T(8,128)(2,1)} %get-tuple-element.171.refs_2_), channel_id=1, source_target_pairs={{2,0},{4,2},{6,4},{3,1},{5,3},{7,5},{10,8},{12,10},{14,12},{11,9},... | collective-permute-start | bytes 1966088 | tf_op jit(solution)/shard_map/ppermute | solution.py:975
  599.5 113.7 %collective-permute-start.29 = (bf16[320,3584]{1,0:T(8,128)(2,1)}, bf16[320,3584]{1,0:T(8,128)(2,1)}, u32[]{:S(2)}, u32[]{:S(2)}) collective-permute-start(bf16[320,3584]{1,0:T(8,128)(2,1)} %near.7.refs_3_), channel_id=1, source_target_pairs={{0,2},{2,0},{4,6},{6,4},{1,3},{3,1},{5,7},{7,5},{8,10},{10,8},{12,... | collective-permute-start | bytes 6881288 | tf_op jit(solution)/shard_map/ppermute | solution.py:887
  601.6 97.8 %collective-permute-start.20 = (bf16[2,320,512]{2,1,0:T(8,128)(2,1)}, bf16[2,320,512]{2,1,0:T(8,128)(2,1)}, u32[]{:S(2)}, u32[]{:S(2)}) collective-permute-start(bf16[2,320,512]{2,1,0:T(8,128)(2,1)} %add_convert_fusion.2), channel_id=1, source_target_pairs={{2,0},{4,2},{6,4},{3,1},{5,3},{7,5},{10,8},{12,10},{14,12},{11,9},... | collective-permute-start | bytes 1966088 | tf_op jit(solution)/shard_map/ppermute | solution.py:975
  634.8 146.0 %collective-permute-start.24 = (bf16[640,3584]{1,0:T(8,128)(2,1)}, bf16[640,3584]{1,0:T(8,128)(2,1)}, u32[]{:S(2)}, u32[]{:S(2)}) collective-permute-start(bf16[640,3584]{1,0:T(8,128)(2,1)} %get-tuple-element.172.refs_3_), channel_id=1, source_target_pairs={{0,16},{8,24},{16,0},{24,8},{1,17},{9,25},{17,1},{25,9},{2,18},{10... | collective-permute-start | bytes 13762568 | tf_op jit(solution)/shard_map/ppermute | solution.py:887
  639.3 77.5 %collective-permute-start.26 = (bf16[2,320,512]{2,1,0:T(8,128)(2,1)}, bf16[2,320,512]{2,1,0:T(8,128)(2,1)S(1)}, u32[]{:S(2)}, u32[]{:S(2)}) collective-permute-start(bf16[2,320,512]{2,1,0:T(8,128)(2,1)} %add_convert_fusion.1), channel_id=1, source_target_pairs={{2,0},{4,2},{6,4},{3,1},{5,3},{7,5},{10,8},{12,10},{14,12},{11,9},... | collective-permute-start | bytes 1966088 | tf_op jit(solution)/shard_map/ppermute | solution.py:975
  645.1 71.9 %collective-permute-start.28 = (bf16[160,3584]{1,0:T(8,128)(2,1)}, bf16[160,3584]{1,0:T(8,128)(2,1)}, u32[]{:S(2)}, u32[]{:S(2)}) collective-permute-start(bf16[160,3584]{1,0:T(8,128)(2,1)} %fold.6.refs_3_), channel_id=1, source_target_pairs={{0,4},{2,6},{4,0},{6,2},{1,5},{3,7},{5,1},{7,3},{8,12},{10,14},{12... | collective-permute-start | bytes 3440648 | tf_op jit(solution)/shard_map/ppermute | solution.py:887
  699.5 94.5 %collective-permute-start.33 = (bf16[640,1280]{1,0:T(8,128)(2,1)}, bf16[640,1280]{1,0:T(8,128)(2,1)}, u32[]{:S(2)}, u32[]{:S(2)}) collective-permute-start(bf16[640,1280]{1,0:T(8,128)(2,1)} %get-tuple-element.174.refs_8_), channel_id=1, source_target_pairs={{0,16},{8,24},{16,0},{24,8},{1,17},{9,25},{17,1},{25,9},{2,18},{10... | collective-permute-start | bytes 4915208 | tf_op jit(solution)/shard_map/ppermute | solution.py:887
  713.2 71.7 %collective-permute-start.23 = (bf16[512,2560]{1,0:T(8,128)(2,1)}, bf16[512,2560]{1,0:T(8,128)(2,1)}, u32[]{:S(2)}, u32[]{:S(2)}) collective-permute-start(bf16[512,2560]{1,0:T(8,128)(2,1)} %get-tuple-element.175.refs_3_.refs_4_), channel_id=1, source_target_pairs={{0,1},{1,0},{2,3},{3,2},{4,5},{5,4},{6,7},{7,6},{8,9},{9,8},{10,11... | collective-permute-start | bytes 7864328 | tf_op jit(solution)/shard_map/ppermute | solution.py:887
  716.8 90.4 %collective-permute-start.32 = (bf16[640,1280]{1,0:T(8,128)(2,1)}, bf16[640,1280]{1,0:T(8,128)(2,1)}, u32[]{:S(2)}, u32[]{:S(2)}) collective-permute-start(bf16[640,1280]{1,0:T(8,128)(2,1)} %get-tuple-element.173.refs_3_), channel_id=1, source_target_pairs={{0,16},{8,24},{16,0},{24,8},{1,17},{9,25},{17,1},{25,9},{2,18},{10... | collective-permute-start | bytes 4915208 | tf_op jit(solution)/shard_map/ppermute | solution.py:887
  717.0 38.4 %collective-permute-start.27 = (bf16[2,320,512]{2,1,0:T(8,128)(2,1)S(1)}, bf16[2,320,512]{2,1,0:T(8,128)(2,1)S(1)}, u32[]{:S(2)}, u32[]{:S(2)}) collective-permute-start(bf16[2,320,512]{2,1,0:T(8,128)(2,1)S(1)} %add_convert_fusion), channel_id=1, source_target_pairs={{2,0},{4,2},{6,4},{3,1},{5,3},{7,5},{10,8},{12,10},{14,12},{11,9},... | collective-permute-start | bytes 1966088 | tf_op jit(solution)/shard_map/ppermute | solution.py:975
  755.5 116.0 %collective-permute-start.36 = (bf16[160,3584]{1,0:T(8,128)(2,1)}, bf16[160,3584]{1,0:T(8,128)(2,1)}, u32[]{:S(2)}, u32[]{:S(2)}) collective-permute-start(bf16[160,3584]{1,0:T(8,128)(2,1)} %fold.7.refs_5_), channel_id=1, source_target_pairs={{0,4},{2,6},{4,0},{6,2},{1,5},{3,7},{5,1},{7,3},{8,12},{10,14},{12... | collective-permute-start | bytes 3440648 | tf_op jit(solution)/shard_map/ppermute | solution.py:887
  780.8 80.4 %collective-permute-start.30 = (bf16[512,2560]{1,0:T(8,128)(2,1)}, bf16[512,2560]{1,0:T(8,128)(2,1)}, u32[]{:S(2)}, u32[]{:S(2)}) collective-permute-start(bf16[512,2560]{1,0:T(8,128)(2,1)} %get-tuple-element.185.refs_3_.refs_4_), channel_id=1, source_target_pairs={{0,1},{1,0},{2,3},{3,2},{4,5},{5,4},{6,7},{7,6},{8,9},{9,8},{10,11... | collective-permute-start | bytes 7864328 | tf_op jit(solution)/shard_map/ppermute | solution.py:887
  785.0 91.0 %collective-permute-start.35 = (bf16[640,640]{1,0:T(8,128)(2,1)}, bf16[640,640]{1,0:T(8,128)(2,1)}, u32[]{:S(2)}, u32[]{:S(2)}) collective-permute-start(bf16[640,640]{1,0:T(8,128)(2,1)} %get-tuple-element.186.refs_2_), channel_id=1, source_target_pairs={{0,16},{8,24},{16,0},{24,8},{1,17},{9,25},{17,1},{25,9},{2,18},{10... | collective-permute-start | bytes 2457608 | tf_op jit(solution)/shard_map/ppermute | solution.py:887
  793.9 63.0 %collective-permute-start.31 = (bf16[320,3584]{1,0:T(8,128)(2,1)}, bf16[320,3584]{1,0:T(8,128)(2,1)S(1)}, u32[]{:S(2)}, u32[]{:S(2)}) collective-permute-start(bf16[320,3584]{1,0:T(8,128)(2,1)} %near.8.refs_6_), channel_id=1, source_target_pairs={{0,2},{2,0},{4,6},{6,4},{1,3},{3,1},{5,7},{7,5},{8,10},{10,8},{12,... | collective-permute-start | bytes 6881288 | tf_op jit(solution)/shard_map/ppermute | solution.py:887
  807.2 122.1 %collective-permute-start.42 = (bf16[320,1280]{1,0:T(8,128)(2,1)}, bf16[320,1280]{1,0:T(8,128)(2,1)}, u32[]{:S(2)}, u32[]{:S(2)}) collective-permute-start(bf16[320,1280]{1,0:T(8,128)(2,1)} %near.9.refs_2_), channel_id=1, source_target_pairs={{0,2},{2,0},{4,6},{6,4},{1,3},{3,1},{5,7},{7,5},{8,10},{10,8},{12,... | collective-permute-start | bytes 2457608 | tf_op jit(solution)/shard_map/ppermute | solution.py:887
  856.9 59.7 %collective-permute-start.38 = (bf16[320,1280]{1,0:T(8,128)(2,1)}, bf16[320,1280]{1,0:T(8,128)(2,1)}, u32[]{:S(2)}, u32[]{:S(2)}) collective-permute-start(bf16[320,1280]{1,0:T(8,128)(2,1)} %near.10.refs_3_), channel_id=1, source_target_pairs={{0,2},{2,0},{4,6},{6,4},{1,3},{3,1},{5,7},{7,5},{8,10},{10,8},{12,... | collective-permute-start | bytes 2457608 | tf_op jit(solution)/shard_map/ppermute | solution.py:887
  861.3 62.0 %collective-permute-start.40 = (bf16[160,3584]{1,0:T(8,128)(2,1)}, bf16[160,3584]{1,0:T(8,128)(2,1)S(1)}, u32[]{:S(2)}, u32[]{:S(2)}) collective-permute-start(bf16[160,3584]{1,0:T(8,128)(2,1)} %fold.8.refs_7_), channel_id=1, source_target_pairs={{0,4},{2,6},{4,0},{6,2},{1,5},{3,7},{5,1},{7,3},{8,12},{10,14},{12... | collective-permute-start | bytes 3440648 | tf_op jit(solution)/shard_map/ppermute | solution.py:887
  871.5 6.5 collective-permute-start.34
  878.0 40.8 %collective-permute-start.37 = (f32[3,2560]{1,0:T(4,128)S(1)}, f32[3,2560]{1,0:T(4,128)S(1)}, u32[]{:S(2)}, u32[]{:S(2)}) collective-permute-start(f32[3,2560]{1,0:T(4,128)S(1)} %add.93), channel_id=1, source_target_pairs={{0,16},{8,24},{16,0},{24,8},{1,17},{9,25},{17,1},{25,9},{2,18},{10... | collective-permute-start | bytes 92168 | tf_op jit(solution)/shard_map/ppermute | solution.py:887
  918.8 4.5 collective-permute-start.39
  918.9 19.3 %collective-permute-start.45 = (bf16[320,640]{1,0:T(8,128)(2,1)S(1)}, bf16[320,640]{1,0:T(8,128)(2,1)S(1)}, u32[]{:S(2)}, u32[]{:S(2)}) collective-permute-start(bf16[320,640]{1,0:T(8,128)(2,1)S(1)} %copy-done.27), channel_id=1, source_target_pairs={{0,2},{2,0},{4,6},{6,4},{1,3},{3,1},{5,7},{7,5},{8,10},{10,8},{12,... | collective-permute-start | bytes 1228808 | tf_op jit(solution)/shard_map/ppermute | solution.py:887
  920.9 36.3 %collective-permute-start.44 = (bf16[160,1280]{1,0:T(8,128)(2,1)}, bf16[160,1280]{1,0:T(8,128)(2,1)S(1)}, u32[]{:S(2)}, u32[]{:S(2)}) collective-permute-start(bf16[160,1280]{1,0:T(8,128)(2,1)} %fold.9.refs_5_), channel_id=1, source_target_pairs={{0,4},{2,6},{4,0},{6,2},{1,5},{3,7},{5,1},{7,3},{8,12},{10,14},{12... | collective-permute-start | bytes 1228808 | tf_op jit(solution)/shard_map/ppermute | solution.py:887
  928.8 31.5 %collective-permute-start.41 = (f32[3,2560]{1,0:T(4,128)S(1)}, f32[3,2560]{1,0:T(4,128)S(1)}, u32[]{:S(2)}, u32[]{:S(2)}) collective-permute-start(f32[3,2560]{1,0:T(4,128)S(1)} %add.95), channel_id=1, source_target_pairs={{0,4},{2,6},{4,0},{6,2},{1,5},{3,7},{5,1},{7,3},{8,12},{10,14},{12... | collective-permute-start | bytes 92168 | tf_op jit(solution)/shard_map/ppermute | solution.py:887
  931.4 35.4 %collective-permute-start.43 = (bf16[160,1280]{1,0:T(8,128)(2,1)}, bf16[160,1280]{1,0:T(8,128)(2,1)S(1)}, u32[]{:S(2)}, u32[]{:S(2)}) collective-permute-start(bf16[160,1280]{1,0:T(8,128)(2,1)} %fold.10.refs_3_), channel_id=1, source_target_pairs={{0,4},{2,6},{4,0},{6,2},{1,5},{3,7},{5,1},{7,3},{8,12},{10,14},{12... | collective-permute-start | bytes 1228808 | tf_op jit(solution)/shard_map/ppermute | solution.py:887
  940.9 29.1 %collective-permute-start.46 = (bf16[160,640]{1,0:T(8,128)(2,1)}, bf16[160,640]{1,0:T(8,128)(2,1)S(1)}, u32[]{:S(2)}, u32[]{:S(2)}) collective-permute-start(bf16[160,640]{1,0:T(8,128)(2,1)} %fold.11.refs_5_), channel_id=1, source_target_pairs={{0,4},{2,6},{4,0},{6,2},{1,5},{3,7},{5,1},{7,3},{8,12},{10,14},{12... | collective-permute-start | bytes 614408 | tf_op jit(solution)/shard_map/ppermute | solution.py:887
  (30 other events, 246.8 us)
Sparse Core Ops, SparseCore 0:
  64.3 50.0 all-gather.1
where the time goes:
time: 988 us; the launch traced here: 981 us
  Pallas kernels  545 us (55%)
  waiting for transfers between devices  239 us (24%)
  starting transfers between devices  143 us (14%)
  local copies, waits for them, and re-layouts  21.8 us (2%)
  between operations  20.1 us (2%)
  other arithmetic  11.4 us (1%)
    pallas_call x44, Pallas kernels, run(): pl.pallas_call(inner, grid_spec=pltpu.PrefetchScalarGridSpec(num_scalar_p...  545 us
    ppermute x35, waiting for transfers between devices, swap(): return lax.ppermute(value, axis, [(i, i ^ bit) for i in range(size)])  167 us
    ppermute x35, starting transfers between devices, swap(): return lax.ppermute(value, axis, [(i, i ^ bit) for i in range(size)])  110 us
    ppermute x12, waiting for transfers between devices, shift(): return lax.ppermute(value, 'ctx', pairs)  72.1 us
    ppermute x12, starting transfers between devices, shift(): return lax.ppermute(value, 'ctx', pairs)  33.9 us
  transfers between devices with their start and end apart: 48, of which 17 were waited for; matrix products, arithmetic and copies ran while one was open for 2% of the time, Pallas kernels for 55%

commit v1 on v0

--- a/solution.py
+++ b/solution.py
@@ -19,9 +19,9 @@
 F32 = jnp.float32
 MIB = 1024 * 1024
 ROWS = 128
-WEIGHTS = {'at0': 60, 'at1': 2, 'fw0': 0, 'fw1': 0, 'er0': 0, 'bw0': 0, 'er1': 0.5, 'bw1': 2, 'Gg': 100, 'mb0': 100, 'ab0': 0, 'h00': 0, 'nd': 0, 'h01': 30, 'Gu': 0, 'h02': 0, 'ab1': 15, 'fd': 1, 'Go': 0, 'h11': 15, 'qb0': 15, 'ed': 10, 'h12': 10, 'ng': 0, 'Gq': 0.5, 'nu': 10, 'fg': 60, 'in0': 100, 'no': 15, 'eg': 0, 'fu': 10, 'in1': 60, 's0': 8, 'nq': 15, 's2': 10, 'eu': 1, 's3': 10, 'eo': 10, 'eq': 1, 'c2': 0.5, 'Gk': 2}
+WEIGHTS = {'at1': 30, 'ab1': 100, 'eb': 30, 'Gu': 60, 'at0': 30, 's0': 0, 'fw0': 30, 'Gb': 0.5, 'Gk': 0, 'in0': 15, 'eo': 60, 'na': 0.5, 'nk': 60, 'eq': 0, 'Ga': 60, 'nu': 15, 'fa': 0, 'h12': 0, 'fw1': 15, 'mb1': 0.5, 's1': 0, 'qb1': 8, 'h10': 60, 'c2': 1, 's3': 2, 'fg': 15}
 ORDER = (
-    "c0", "c1", "at0", "at1", "c2", "fw0", "c3", "fw1", "er0", "bw0", "er1", "Gd", "bw1", "Gg", "mb0", "ab0", "h00", "nd", "mb1", "h01", "h02", "ab1", "h10", "ng", "h11", "Gu", "fd", "Go", "Gq", "h12", "qb0", "fg", "ed", "qb1", "Gk", "nu", "in0", "nq", "no", "fu", "in1", "s0", "eg", "nk", "s1", "fo", "s2", "eu", "s3", "fq", "fk", "eo", "eq", "ek",
+    "at0", "c2", "at1", "c3", "fw0", "fw1", "er0", "bw0", "er1", "Ga", "Gb", "bw1", "na", "Gg", "mb0", "nb", "fa", "ab0", "h00", "Gu", "fb", "h01", "mb1", "ng", "ab1", "h10", "h02", "ea", "h11", "nu", "h12", "Go", "fg", "qb0", "eb", "Gq", "qb1", "Gk", "in0", "no", "eg", "fu", "in1", "s0", "nk", "s1", "fo", "s2", "nq", "eu", "s3", "fq", "eo", "fk", "eq", "ek",
 )
 PRESENT = [5]
 
@@ -831,16 +831,18 @@
             sending(at).wait_send()
 
 
-def weight_grad(meets, x_t, y, flipped, after):
+def weight_grad(meets, x_t, y, flipped, half, after):
     model, tokens = x_t.shape
     if flipped:
         tile = divisor(y.shape[0], 640)
-        tiles = y.shape[0] // tile
+        tiles, first = y.shape[0] // tile, 0
         y_block, place = (tile, tokens), lambda at: (at, 0)
     else:
-        tile = divisor(y.shape[2], 512)
-        tiles = y.shape[2] // tile
-        y_block, place = y.shape[:2] + (tile,), lambda at: (0, 0, at)
+        tile = divisor(y.shape[2], 512, 128)
+        tiles, first = y.shape[2] // tile, 0
+        if half is not None:
+            first, tiles = ((0, tiles // 2), (tiles // 2, tiles - tiles // 2))[half]
+        y_block, place = y.shape[:2] + (tile,), lambda at: (0, 0, first + at)
     width = tile * tiles
     before = lambda i: jnp.maximum(i - 1, 0)
     outs = [
@@ -888,14 +890,14 @@
 
 
 class Halving:
-    def __init__(self, meets, x_t, y, flipped, after):
-        far, self.sent, self.kept = weight_grad(meets, x_t, y, flipped, after)
+    def __init__(self, meets, x_t, y, flipped, half, after):
+        far, self.sent, self.kept = weight_grad(meets, x_t, y, flipped, half, after)
         self.came = swap(far, "dp", 2)
         self.last = far
 
     def added(self, name, rows, parts, after):
         width = self.sent.shape[1]
-        tile = divisor(width, 1792, 640)
+        tile = divisor(width, 1792, 1024, 768, 640)
         ins = [
             (
                 array,
@@ -923,7 +925,7 @@
 
     def final(self, scale, widths, after):
         rows, width = self.end.shape
-        tile = width if len(widths) > 1 else divisor(width, 896, 640)
+        tile = width if len(widths) > 1 else divisor(width, 896, 1024, 768, 640)
         tiles = [(tile,), widths][len(widths) > 1]
         parts = [(self.kept, 1), (self.came, 3), (self.pair, 1), (self.end, 0)]
         self.result = run(
@@ -1008,6 +1010,8 @@
     valid = valid_mask.astype(F32)[..., None]
 
 
+    count = jnp.sum(valid_mask).reshape(1, 1)
+    count = count + swap(count, "dp", 1)
     normed, queries, kv_chunks = [], [], []
     normed_t, last = None, hidden_in
     for s in seqs:
@@ -1018,16 +1022,20 @@
         kv_chunks.append([kv_own])
         last = n_rows
     kv_chunks[0].append(shift(kv_chunks[0][0], 1))
+    after = [last, kv_chunks[0][-1], count]
+    kv_chunks[0].append(shift(held(kv_chunks[0][-1], last), 1))
     for s in seqs:
-        queries.append(q_project(s, normed[s], w_query, cos, sin, [last, kv_chunks[0][-1]]))
-        kv_chunks[0].append(shift(held(kv_chunks[0][-1], last), 1))
+        queries.append(q_project(s, normed[s], w_query, cos, sin, after))
         last = queries[-1]
+        after = [last]
+    count = count + swap(held(count, queries[0]), "dp", 2)
+    kv_chunks[0].append(shift(held(kv_chunks[0][-1], last), 1))
     for s in seqs[1:]:
         own = held(kv_chunks[s][0], kv_chunks[0][-1], last)
         for step in range(1, ctx_size):
             kv_chunks[s].append(shift(own, step))
 
-    made = {"count": jnp.sum(valid_mask).reshape(1, 1)}
+    made = {"count": count}
     lse, middle, rows_a, rows_b = [], [], [], []
     losses, dys, mlp_gains, attn_gains, grad_middle = [], [], [], [], []
     heads, mlp_parts, dn2_parts, dn1_parts, pieces, came = [], [], [], [], [], [None, None]
@@ -1048,7 +1056,7 @@
             queries[s],
             kv_chunks[s][::-1],
             made.get("mixed"),
-            after + [made["count"]],
+            after,
         )
         lse.append(lse_rows)
         heads.append(tensor_copies(heads_out))
@@ -1066,7 +1074,7 @@
             w_outs,
             made.get("n2"),
             made.get("z"),
-            after,
+            after + [made["count"]],
         )
         middle.append(m_rows)
         rows_a.append(a)
@@ -1083,7 +1091,7 @@
             mlp_parts[s],
             made.get("y"),
             made.get("dy"),
-            after + [made["count"]],
+            after,
         )
         dys.append(dy)
         losses.append(loss_row)
@@ -1165,8 +1173,8 @@
         dn1_parts.append(tensor_parts(partial))
         return partial
 
-    def halving(name, meets, x_t, y, flipped, after):
-        made[name] = Halving(meets, made.get(x_t, normed_t), made[y], flipped, after)
+    def halving(name, meets, x_t, y, flipped, half, after):
+        made[name] = Halving(meets, made.get(x_t, normed_t), made[y], flipped, half, after)
         return made[name].last
 
     def input_step(s, after):
@@ -1185,7 +1193,7 @@
 
     def hop_of(name, at, after):
         axis, bit = (("dp", 1), ("dp", 2), ("ctx", 1), ("ctx", 2))[at]
-        total = made[name] if name == "count" and at < 2 else held(made[name], *after)
+        total = held(made[name], *after)
         made[name] = total + swap(total, axis, bit)
         return after[0]
 
@@ -1202,14 +1210,15 @@
         return made[name].final(scale(), widths, after)
 
     steps = {
-        "Gd": functools.partial(halving, "d", 0, "dy", "z", False),
-        "Gg": functools.partial(halving, "g", 3, "n2", "dgate", False),
-        "Gu": functools.partial(halving, "u", 4, "n2", "dup", False),
-        "Go": functools.partial(halving, "o", 1, "dm", "mixed", True),
-        "Gq": functools.partial(halving, "q", 2, "n1", "dq", True),
-        "Gk": functools.partial(halving, "k", 5, "n1", "dkv", True),
+        "Ga": functools.partial(halving, "a", 0, "dy", "z", False, 0),
+        "Gb": functools.partial(halving, "b", 6, "dy", "z", False, 1),
+        "Gg": functools.partial(halving, "g", 3, "n2", "dgate", False, None),
+        "Gu": functools.partial(halving, "u", 4, "n2", "dup", False, None),
+        "Go": functools.partial(halving, "o", 1, "dm", "mixed", True, None),
+        "Gq": functools.partial(halving, "q", 2, "n1", "dq", True, None),
+        "Gk": functools.partial(halving, "k", 5, "n1", "dkv", True, None),
     }
-    for name in "dguoqk":
+    for name in "abguoqk":
         for short, stage in (("n", "near"), ("f", "fold")):
             steps[short + name] = lambda after, name=name, stage=stage: getattr(
                 made[name], stage
@@ -1236,7 +1245,8 @@
         PRESENT[0] = WEIGHTS.get(name, 5)
         last = steps[name]([last])
 
-    (out_sum,), (gate_sum,), (up_sum,), (down_sum,) = (made[name].result for name in "ogud")
+    (out_sum,), (gate_sum,), (up_sum,) = (made[name].result for name in "ogu")
+    down_sum = jnp.concatenate(made["a"].result + made["b"].result, axis=1)
     size = model // (lax.axis_size("dp") * ctx_size)
     here = (lax.axis_index("dp") * ctx_size + ctx) * size
     small = made["small"]

time: 988 us -> 981 us (level)
  waiting for transfers between devices: 239 us -> 188 us
  Pallas kernels: 545 us -> 567 us
  starting transfers between devices: 143 us -> 163 us
    ppermute x35 -> x38, waiting for transfers between devices: 167 us -> 75.8 us  [swap(): return lax.ppermute(value, axis, [(i, i ^ bit) for i in range(size)])]
    ppermute x12, waiting for transfers between devices: 72.1 us -> 112 us  [shift(): return lax.ppermute(value, 'ctx', pairs)]
    ppermute x35 -> x38, starting transfers between devices: 110 us -> 132 us  [swap(): return lax.ppermute(value, axis, [(i, i ^ bit) for i in range(size)])]
    pallas_call x44 -> x48, Pallas kernels: 545 us -> 567 us  [run(): pl.pallas_call(inner, grid_spec=pltpu.PrefetchScalarGridSpec(num_scalar_p...]
  transfers between devices with their start and end apart: 48 -> 51, of which waited for: 17 -> 17; matrix products, arithmetic and copies ran while one was open for 2% -> 1% of each run, Pallas kernels for 55% -> 58%
where the time goes in v1:
time: 981 us; the launch traced here: 969 us
  Pallas kernels  567 us (58%)
  waiting for transfers between devices  188 us (19%)
  starting transfers between devices  163 us (17%)
  local copies, waits for them, and re-layouts  22.9 us (2%)
  between operations  20.2 us (2%)
    pallas_call x48, Pallas kernels, run(): pl.pallas_call(inner, grid_spec=pltpu.PrefetchScalarGridSpec(num_scalar_p...  567 us
    ppermute x38, starting transfers between devices, swap(): return lax.ppermute(value, axis, [(i, i ^ bit) for i in range(size)])  132 us
    ppermute x12, waiting for transfers between devices, shift(): return lax.ppermute(value, 'ctx', pairs)  112 us
    ppermute x38, waiting for transfers between devices, swap(): return lax.ppermute(value, axis, [(i, i ^ bit) for i in range(size)])  75.8 us
    ppermute x12, starting transfers between devices, shift(): return lax.ppermute(value, 'ctx', pairs)  31.3 us
  transfers between devices with their start and end apart: 51, of which 17 were waited for; matrix products, arithmetic and copies ran while one was open for 1% of the time, Pallas kernels for 58%

profile of v1, /device:TPU:0, one launch (start us, length us, event | category | flops | bytes accessed | tf_op | source)
XLA Modules:
  0.0 969.0 jit_solution(13713016357365929914)
XLA Ops:
  14.9 6.6 kv_project.2
  25.7 6.6 kv_project.3
  33.5 5.5 collective-permute-done.refs_5_.refs_6_.refs_11_
  39.8 8.3 q_project.2.refs_4_.refs_3_.refs_5_
  48.2 8.5 q_project.3.refs_8_.refs_3_.refs_5_
  63.0 11.9 %collective-permute-done.2.refs_5_.refs_10_ = bf16[2,320,512]{2,1,0:T(8,128)(2,1)S(1)} collective-permute-done((bf16[2,320,512]{2,1,0:T(8,128)(2,1)S(1)}, bf16[2,320,512]{2,1,0:T(8,128)(2,1)S(1)}, u32[]{:S(2)}, u32[]{:S(2)}) %collective-permute-start.2) | collective-permute-done | bytes 655392 | tf_op jit(solution)/shard_map/ppermute | solution.py:977
  84.6 6.7 collective-permute-done.3.refs_4_.refs_9_
  91.3 6.5 collective-permute-start.4
  102.6 11.4 %attend.2 = (bf16[1280,512]{1,0:T(8,128)(2,1)}, bf16[1280,1024]{1,0:T(8,128)(2,1)}, f32[4,4,512]{2,1,0:T(4,128)}) custom-call(s32[2]{0:T(128)} %get-tuple-element.231.refs_0_, s32[2]{0:T(128)} %get-tuple-element.226.refs_1_, s32[1,512]{1,0:T(1,128)} %get-tuple-element.220.refs_2_, bf16[1280,512]{1,0:T(8,128)(2,1)} %q_project.2.refs_4_.refs_3_.refs_5_, ...), custom_call_target="tpu_custom_call" | custom-call | flops 30000001024 | bytes 1000 | tf_op jit(solution)/shard_map/attend/pallas_call | solution.py:46
  114.0 23.3 %collective-permute-start.11 = (s32[1,1]{1,0:T(1,128)}, s32[1,1]{1,0:T(1,128)}, u32[]{:S(2)}, u32[]{:S(2)}) collective-permute-start(s32[1,1]{1,0:T(1,128)} %add.83), channel_id=1, source_target_pairs={{0,2},{2,0},{4,6},{6,4},{1,3},{3,1},{5,7},{7,5},{8,10},{10,8},{12,... | collective-permute-start | bytes 20 | tf_op jit(solution)/shard_map/ppermute | solution.py:889
  139.6 11.3 %attend.3 = (bf16[1280,512]{1,0:T(8,128)(2,1)}, bf16[1280,1024]{1,0:T(8,128)(2,1)}, f32[4,4,512]{2,1,0:T(4,128)}) custom-call(s32[2]{0:T(128)} %get-tuple-element.230.refs_0_, s32[2]{0:T(128)} %get-tuple-element.227.refs_1_, s32[1,512]{1,0:T(1,128)} %get-tuple-element.221.refs_2_, ...), custom_call_target="tpu_custom_call", output_to_operand_aliasing={{1}: (8, {})} | custom-call | flops 30000001024 | bytes 1000 | tf_op jit(solution)/shard_map/attend/pallas_call | solution.py:46
  150.9 19.1 %collective-permute-start.12 = (s32[1,1]{1,0:T(1,128)}, s32[1,1]{1,0:T(1,128)}, u32[]{:S(2)}, u32[]{:S(2)}) collective-permute-start(s32[1,1]{1,0:T(1,128)} %add.84), channel_id=1, source_target_pairs={{0,4},{2,6},{4,0},{6,2},{1,5},{3,7},{5,1},{7,3},{8,12},{10,14},{12... | collective-permute-start | bytes 20 | tf_op jit(solution)/shard_map/ppermute | solution.py:889
  172.2 56.6 %forward_mlp.2 = (bf16[512,2560]{1,0:T(8,128)(2,1)}, bf16[2560,1024]{1,0:T(8,128)(2,1)}, bf16[2,512,3584]{2,1,0:T(8,128)(2,1)}, bf16[512,3584]{1,0:T(8,128)(2,1)...) custom-call(bf16[2,512,2560]{2,1,0:T(8,128)(2,1)} %refs_1_.15, f32[1,2560]{1,0:T(1,128)} %broadcast_in_dim.18.refs_1_.refs_2_, ...), custom_call_target="tpu_custom_call" | custom-call | flops 30000001024 | bytes 1000 | tf_op jit(solution)/shard_map/forward_mlp/pallas_call | solution.py:46
  231.5 57.3 %forward_mlp.3 = (bf16[512,2560]{1,0:T(8,128)(2,1)}, bf16[2560,1024]{1,0:T(8,128)(2,1)}, bf16[2,512,3584]{2,1,0:T(8,128)(2,1)}, bf16[512,3584]{1,0:T(8,128)(2,1)...) custom-call(bf16[2,512,2560]{2,1,0:T(8,128)(2,1)} %refs_1_.15, ...), custom_call_target="tpu_custom_call", output_to_operand_aliasing={{1}: (9, {}), {2}: (10, {})} | custom-call | flops 15000000512 | bytes 1000 | tf_op jit(solution)/shard_map/forward_mlp/pallas_call | solution.py:46
  290.3 8.2 output_error.2
  298.6 40.4 %backward_mlp.2 = (bf16[2,512,3584]{2,1,0:T(8,128)(2,1)}, bf16[2,512,3584]{2,1,0:T(8,128)(2,1)}, bf16[512,2560]{1,0:T(8,128)(2,1)}) custom-call(bf16[512,2560]{1,0:T(8,128)(2,1)} %get-tuple-element.139.refs_0_.refs_6_.refs_1_, bf16[3584,2560]{1,0:T(8,128)(2,1)} %refs_1_.13, bf16[512,3584]{1,0:T(8,128)(2,1)} %get-tuple-element.140.refs_2_, ...), custom_call_target="tpu_custom_call" | custom-call | flops 5000001024 | bytes 1000 | tf_op jit(solution)/shard_map/backward_mlp/pallas_call | solution.py:46
  340.5 8.3 collective-permute-done.13.refs_4_
  350.4 8.2 output_error.3
  358.6 16.7 %weight_grad.7 = (bf16[640,1536]{1,0:T(8,128)(2,1)}, bf16[320,1536]{1,0:T(8,128)(2,1)}, bf16[320,1536]{1,0:T(8,128)(2,1)}) custom-call(bf16[2560,1024]{1,0:T(8,128)(2,1)} %get-tuple-element.150.refs_0_, bf16[2,512,3584]{2,1,0:T(8,128)(2,1)} %get-tuple-element.151.refs_1_.refs_2_, bf16[2,512,3584]{2,1,0:T(8,128)(2,1)} %get-tuple-element.151.refs_1_.refs_2_, ...), custom_call_target="tpu_custom_call" | custom-call | flops 60000002048 | bytes 1000 | tf_op jit(solution)/shard_map/weight_grad/pallas_call | solution.py:46
  375.3 7.7 collective-permute-start.16
  382.9 19.9 %weight_grad.8 = (bf16[640,2048]{1,0:T(8,128)(2,1)}, bf16[320,2048]{1,0:T(8,128)(2,1)}, bf16[320,2048]{1,0:T(8,128)(2,1)}) custom-call(bf16[2560,1024]{1,0:T(8,128)(2,1)} %get-tuple-element.150.refs_0_, bf16[2,512,3584]{2,1,0:T(8,128)(2,1)} %get-tuple-element.151.refs_1_.refs_2_, bf16[2,512,3584]{2,1,0:T(8,128)(2,1)} %get-tuple-element.151.refs_1_.refs_2_, ...), custom_call_target="tpu_custom_call" | custom-call | flops 500000992 | bytes 1000 | tf_op jit(solution)/shard_map/weight_grad/pallas_call | solution.py:46
  403.1 40.4 %backward_mlp.3 = (bf16[2,512,3584]{2,1,0:T(8,128)(2,1)}, bf16[2,512,3584]{2,1,0:T(8,128)(2,1)}, bf16[512,2560]{1,0:T(8,128)(2,1)}) custom-call(bf16[512,2560]{1,0:T(8,128)(2,1)} %get-tuple-element.145.refs_3_.refs_0_.refs_1_, bf16[3584,2560]{1,0:T(8,128)(2,1)} %refs_1_.13, ...), custom_call_target="tpu_custom_call", output_to_operand_aliasing={{0}: (6, {}), {1}: (7, {})} | custom-call | flops 5000001024 | bytes 1000 | tf_op jit(solution)/shard_map/backward_mlp/pallas_call | solution.py:46
  450.2 29.9 %weight_grad.9 = (bf16[640,3584]{1,0:T(8,128)(2,1)}, bf16[320,3584]{1,0:T(8,128)(2,1)}, bf16[320,3584]{1,0:T(8,128)(2,1)}) custom-call(bf16[2560,1024]{1,0:T(8,128)(2,1)} %get-tuple-element.144.refs_0_, bf16[2,512,3584]{2,1,0:T(8,128)(2,1)} %get-tuple-element.154.refs_1_.refs_2_, bf16[2,512,3584]{2,1,0:T(8,128)(2,1)} %get-tuple-element.154.refs_1_.refs_2_, ...), custom_call_target="tpu_custom_call" | custom-call | flops 5000001024 | bytes 1000 | tf_op jit(solution)/shard_map/weight_grad/pallas_call | solution.py:46
  482.2 14.3 %middle_back.2 = (bf16[512,2560]{1,0:T(8,128)(2,1)}, bf16[2560,1024]{1,0:T(8,128)(2,1)}, f32[1,2560]{1,0:T(1,128)}, bf16[1280,512]{1,0:T(8,128)(2,1)}) custom-call(bf16[512,2560]{1,0:T(8,128)(2,1)} %get-tuple-element.133.refs_11_.refs_0_, bf16[512,2560]{1,0:T(8,128)(2,1)} %get-tuple-element.139.refs_0_.refs_6_.refs_1_, ...), custom_call_target="tpu_custom_call" | custom-call | flops 5000001024 | bytes 1000 | tf_op jit(solution)/shard_map/middle_back/pallas_call | solution.py:46
  506.4 15.7 %attend_back.2 = (bf16[1280,1024]{1,0:T(8,128)(2,1)}, bf16[2,320,512]{2,1,0:T(8,128)(2,1)}, bf16[2,320,512]{2,1,0:T(8,128)(2,1)}, bf16[2,320,512]{2,1,0:T(8,128)(2,1)}, bf16[2,320,512]{2,1,0:T(8,128)(2,1)}) custom-call(s32[2]{0:T(128)} %get-tuple-element.231.refs_0_, s32[2]{0:T(128)} %get-tuple-element.226.refs_1_, s32[1,512]{1,0:T(1,128)} %get-tuple-element.220.refs_2_, ...), custom_call_target="tpu_custom_call" | custom-call | flops 5000001024 | bytes 1000 | tf_op jit(solution)/shard_map/attend_back/pallas_call | solution.py:46
  523.4 30.0 %weight_grad.10 = (bf16[640,3584]{1,0:T(8,128)(2,1)}, bf16[320,3584]{1,0:T(8,128)(2,1)}, bf16[320,3584]{1,0:T(8,128)(2,1)}) custom-call(bf16[2560,1024]{1,0:T(8,128)(2,1)} %get-tuple-element.144.refs_0_, bf16[2,512,3584]{2,1,0:T(8,128)(2,1)} %get-tuple-element.163.refs_1_.refs_2_, bf16[2,512,3584]{2,1,0:T(8,128)(2,1)} %get-tuple-element.163.refs_1_.refs_2_, ...), custom_call_target="tpu_custom_call" | custom-call | flops 60000002048 | bytes 1000 | tf_op jit(solution)/shard_map/weight_grad/pallas_call | solution.py:46
  556.0 26.6 %collective-permute-start.32 = (bf16[160,2048]{1,0:T(8,128)(2,1)}, bf16[160,2048]{1,0:T(8,128)(2,1)}, u32[]{:S(2)}, u32[]{:S(2)}) collective-permute-start(bf16[160,2048]{1,0:T(8,128)(2,1)} %fold.8.refs_7_), channel_id=1, source_target_pairs={{0,4},{2,6},{4,0},{6,2},{1,5},{3,7},{5,1},{7,3},{8,12},{10,14},{12... | collective-permute-start | bytes 1966088 | tf_op jit(solution)/shard_map/ppermute | solution.py:889
  584.1 14.2 %middle_back.3 = (bf16[512,2560]{1,0:T(8,128)(2,1)}, bf16[2560,1024]{1,0:T(8,128)(2,1)}, f32[1,2560]{1,0:T(1,128)}, bf16[1280,512]{1,0:T(8,128)(2,1)}) custom-call(bf16[512,2560]{1,0:T(8,128)(2,1)} %get-tuple-element.134.refs_5_.refs_0_, bf16[512,2560]{1,0:T(8,128)(2,1)} %get-tuple-element.145.refs_3_.refs_0_.refs_1_, ...), custom_call_target="tpu_custom_call", output_to_operand_aliasing={{1}: (6, {})} | custom-call | flops 500000992 | bytes 1000 | tf_op jit(solution)/shard_map/middle_back/pallas_call | solution.py:46
  603.2 15.3 %collective-permute-start.25 = (bf16[320,3584]{1,0:T(8,128)(2,1)}, bf16[320,3584]{1,0:T(8,128)(2,1)}, u32[]{:S(2)}, u32[]{:S(2)}) collective-permute-start(bf16[320,3584]{1,0:T(8,128)(2,1)} %near.9.refs_14_), channel_id=1, source_target_pairs={{0,2},{2,0},{4,6},{6,4},{1,3},{3,1},{5,7},{7,5},{8,10},{10,8},{12,... | collective-permute-start | bytes 6881288 | tf_op jit(solution)/shard_map/ppermute | solution.py:889
  618.5 15.9 %attend_back.3 = (bf16[1280,1024]{1,0:T(8,128)(2,1)}, bf16[2,320,512]{2,1,0:T(8,128)(2,1)}, bf16[2,320,512]{2,1,0:T(8,128)(2,1)}, bf16[2,320,512]{2,1,0:T(8,128)(2,1)}, bf16[2,320,512]{2,1,0:T(8,128)(2,1)}) custom-call(s32[2]{0:T(128)} %get-tuple-element.230.refs_0_, s32[2]{0:T(128)} %get-tuple-element.227.refs_1_, ...), custom_call_target="tpu_custom_call", output_to_operand_aliasing={{0}: (13, {})} | custom-call | flops 99999997952 | bytes 1000 | tf_op jit(solution)/shard_map/attend_back/pallas_call | solution.py:46
  639.8 43.5 %collective-permute-done.29 = bf16[2,320,512]{2,1,0:T(8,128)(2,1)S(1)} collective-permute-done((bf16[2,320,512]{2,1,0:T(8,128)(2,1)}, bf16[2,320,512]{2,1,0:T(8,128)(2,1)S(1)}, u32[]{:S(2)}, u32[]{:S(2)}) %collective-permute-start.29) | collective-permute-done | bytes 655392 | tf_op jit(solution)/shard_map/ppermute | solution.py:977
  691.1 15.5 %weight_grad.11 = (bf16[640,1280]{1,0:T(8,128)(2,1)}, bf16[320,1280]{1,0:T(8,128)(2,1)}, bf16[320,1280]{1,0:T(8,128)(2,1)}) custom-call(bf16[2560,1024]{1,0:T(8,128)(2,1)} %get-tuple-element.180.refs_0_, bf16[1280,1024]{1,0:T(8,128)(2,1)} %get-tuple-element.159.refs_6_.refs_1_.refs_2_, bf16[1280,1024]{1,0:T(8,128)(2,1)} %get-tuple-element.159.refs_6_.refs_1_.refs_2_, ...), custom_call_target="tpu_custom_call" | custom-call | flops 5000001024 | bytes 1000 | tf_op jit(solution)/shard_map/weight_grad/pallas_call | solution.py:46
  706.6 4.8 collective-permute-done.30
  718.1 5.6 collective-permute-start.35
  723.7 11.7 %qkv_back.2 = (bf16[640,1024]{1,0:T(8,128)(2,1)}, bf16[512,2560]{1,0:T(8,128)(2,1)}) custom-call(bf16[1280,1024]{1,0:T(8,128)(2,1)} %get-tuple-element.172.refs_0_.refs_1_.refs_2_, f32[2,40,512]{2,1,0:T(8,128)} %get-tuple-element.217.refs_4_.refs_2_.refs_3_.refs_1_, f32[2,40,512]{2,1,0:T(8,128)} %get-tuple-element.216.refs_5_.refs_3_.refs_4_.refs_2_, ...), custom_call_target="tpu_custom_call" | custom-call | flops 5000001024 | bytes 1000 | tf_op jit(solution)/shard_map/qkv_back/pallas_call | solution.py:46
  739.2 19.9 %weight_grad.12 = (bf16[640,1280]{1,0:T(8,128)(2,1)}, bf16[320,1280]{1,0:T(8,128)(2,1)}, bf16[320,1280]{1,0:T(8,128)(2,1)}) custom-call(bf16[2560,1024]{1,0:T(8,128)(2,1)} %get-tuple-element.184.refs_0_, bf16[1280,1024]{1,0:T(8,128)(2,1)} %get-tuple-element.172.refs_0_.refs_1_.refs_2_, bf16[1280,1024]{1,0:T(8,128)(2,1)} %get-tuple-element.172.refs_0_.refs_1_.refs_2_, ...), custom_call_target="tpu_custom_call" | custom-call | flops 5000001024 | bytes 1000 | tf_op jit(solution)/shard_map/weight_grad/pallas_call | solution.py:46
  759.1 39.7 %collective-permute-done.31.refs_7_ = bf16[2,320,512]{2,1,0:T(8,128)(2,1)S(1)} collective-permute-done((bf16[2,320,512]{2,1,0:T(8,128)(2,1)S(1)}, bf16[2,320,512]{2,1,0:T(8,128)(2,1)S(1)}, u32[]{:S(2)}, u32[]{:S(2)}) %collective-permute-start.31) | collective-permute-done | bytes 655392 | tf_op jit(solution)/shard_map/ppermute | solution.py:977
  799.7 11.6 %qkv_back.3 = (bf16[640,1024]{1,0:T(8,128)(2,1)}, bf16[512,2560]{1,0:T(8,128)(2,1)}) custom-call(bf16[1280,1024]{1,0:T(8,128)(2,1)} %get-tuple-element.172.refs_0_.refs_1_.refs_2_, f32[2,40,512]{2,1,0:T(8,128)} %get-tuple-element.217.refs_4_.refs_2_.refs_3_.refs_1_, ...), custom_call_target="tpu_custom_call", output_to_operand_aliasing={{0}: (8, {})} | custom-call | flops 8000001024 | bytes 1000 | tf_op jit(solution)/shard_map/qkv_back/pallas_call | solution.py:46
  812.2 13.0 %weight_grad.13 = (bf16[640,640]{1,0:T(8,128)(2,1)}, bf16[320,640]{1,0:T(8,128)(2,1)}, bf16[320,640]{1,0:T(8,128)(2,1)}) custom-call(bf16[2560,1024]{1,0:T(8,128)(2,1)} %get-tuple-element.184.refs_0_, bf16[640,1024]{1,0:T(8,128)(2,1)} %get-tuple-element.192.refs_1_.refs_2_, bf16[640,1024]{1,0:T(8,128)(2,1)} %get-tuple-element.192.refs_1_.refs_2_, ...), custom_call_target="tpu_custom_call" | custom-call | flops 1000 | bytes 1000 | tf_op jit(solution)/shard_map/weight_grad/pallas_call | solution.py:46
  827.0 9.0 input_back.2
  838.6 4.5 final.9.refs_3_
  846.0 23.9 %collective-permute-done.33.refs_5_ = bf16[512,2560]{1,0:T(8,128)(2,1)S(1)} collective-permute-done((bf16[512,2560]{1,0:T(8,128)(2,1)}, bf16[512,2560]{1,0:T(8,128)(2,1)S(1)}, u32[]{:S(2)}, u32[]{:S(2)}) %collective-permute-start.33) | collective-permute-done | bytes 2621472 | tf_op jit(solution)/shard_map/ppermute | solution.py:889
  871.6 9.2 input_back.3
  894.1 5.3 collective-permute-done.41
  899.4 4.6 final.10.refs_3_
  908.5 5.3 collective-permute-done.44
  915.2 11.5 %collective-permute-done.45.refs_2_.refs_3_ = bf16[320,1280]{1,0:T(8,128)(2,1)} collective-permute-done((bf16[320,1280]{1,0:T(8,128)(2,1)}, bf16[320,1280]{1,0:T(8,128)(2,1)}, u32[]{:S(2)}, u32[]{:S(2)}) %collective-permute-start.45) | collective-permute-done | bytes 819232 | tf_op jit(solution)/shard_map/ppermute | solution.py:889
  940.1 13.3 %collective-permute-done.46.refs_4_ = bf16[160,1280]{1,0:T(8,128)(2,1)S(1)} collective-permute-done((bf16[160,1280]{1,0:T(8,128)(2,1)}, bf16[160,1280]{1,0:T(8,128)(2,1)S(1)}, u32[]{:S(2)}, u32[]{:S(2)}) %collective-permute-start.46) | collective-permute-done | bytes 409632 | tf_op jit(solution)/shard_map/ppermute | solution.py:889
  (206 shorter events, 145.4 us)
Async XLA Ops:
  7.2 163.9 %all-gather.2.cloned.1.call-start = ((), (), s32[]{:S(2)}) async-start(), calls=%async_computation | async-start | bytes 8192000 | tf_op jit(solution)/shard_map/all_gather | solution.py:967
  10.0 46.7 %collective-permute-start.8 = (bf16[320,2560]{1,0:T(8,128)(2,1)}, bf16[320,2560]{1,0:T(8,128)(2,1)S(1)}, u32[]{:S(2)}, u32[]{:S(2)}) collective-permute-start(bf16[320,2560]{1,0:T(8,128)(2,1)} %constant_dynamic-slice_fusion), channel_id=1, source_target_pairs={{0,1},{1,0},{2,3},{3,2},{4,5},{5,4},{6,7},{7,6},{8,9},{9,8},{10,11... | collective-permute-start | bytes 4915208 | tf_op jit(solution)/shard_map/ppermute | solution.py:889
  21.5 17.5 %collective-permute-start = (bf16[2,320,512]{2,1,0:T(8,128)(2,1)}, bf16[2,320,512]{2,1,0:T(8,128)(2,1)S(1)}, u32[]{:S(2)}, u32[]{:S(2)}) collective-permute-start(bf16[2,320,512]{2,1,0:T(8,128)(2,1)} %get-tuple-element.117.refs_7_.refs_12_), channel_id=1, source_target_pairs={{0,2},{2,4},{4,6},{1,3},{3,5},{5,7},{8,10},{10,12},{12,14},{9,11},... | collective-permute-start | bytes 1966088 | tf_op jit(solution)/shard_map/ppermute | solution.py:977
  25.7 6.6 collective-permute-start.1
  57.8 17.1 %collective-permute-start.2 = (bf16[2,320,512]{2,1,0:T(8,128)(2,1)S(1)}, bf16[2,320,512]{2,1,0:T(8,128)(2,1)S(1)}, u32[]{:S(2)}, u32[]{:S(2)}) collective-permute-start(bf16[2,320,512]{2,1,0:T(8,128)(2,1)S(1)} %copy-done.25), channel_id=1, source_target_pairs={{0,2},{2,4},{4,6},{1,3},{3,5},{5,7},{8,10},{10,12},{12,14},{9,11},... | collective-permute-start | bytes 1966088 | tf_op jit(solution)/shard_map/ppermute | solution.py:977
  74.9 16.3 %collective-permute-start.3 = (bf16[2,320,512]{2,1,0:T(8,128)(2,1)S(1)}, bf16[2,320,512]{2,1,0:T(8,128)(2,1)S(1)}, u32[]{:S(2)}, u32[]{:S(2)}) collective-permute-start(bf16[2,320,512]{2,1,0:T(8,128)(2,1)S(1)} %collective-permute-done.2.refs_5_.refs_10_), channel_id=1, source_target_pairs={{0,2},{2,4},{4,6},{1,3},{3,5},{5,7},{8,10},{10,12},{12,14},{9,11},... | collective-permute-start | bytes 1966088 | tf_op jit(solution)/shard_map/ppermute | solution.py:977
  91.3 47.2 %collective-permute-start.4 = (bf16[2,320,512]{2,1,0:T(8,128)(2,1)}, bf16[2,320,512]{2,1,0:T(8,128)(2,1)S(1)}, u32[]{:S(2)}, u32[]{:S(2)}) collective-permute-start(bf16[2,320,512]{2,1,0:T(8,128)(2,1)} %get-tuple-element.121.refs_7_.refs_12_), channel_id=1, source_target_pairs={{0,6},{1,7},{8,14},{9,15},{16,22},{17,23},{24,30},{25,31}} | collective-permute-start | bytes 1966088 | tf_op jit(solution)/shard_map/ppermute | solution.py:977
  97.7 40.8 %collective-permute-start.5 = (bf16[2,320,512]{2,1,0:T(8,128)(2,1)}, bf16[2,320,512]{2,1,0:T(8,128)(2,1)S(1)}, u32[]{:S(2)}, u32[]{:S(2)}) collective-permute-start(bf16[2,320,512]{2,1,0:T(8,128)(2,1)} %get-tuple-element.121.refs_7_.refs_12_), channel_id=1, source_target_pairs={{0,4},{2,6},{1,5},{3,7},{8,12},{10,14},{9,13},{11,15},{16,20},{18,... | collective-permute-start | bytes 1966088 | tf_op jit(solution)/shard_map/ppermute | solution.py:977
  99.1 39.5 %collective-permute-start.6 = (bf16[2,320,512]{2,1,0:T(8,128)(2,1)}, bf16[2,320,512]{2,1,0:T(8,128)(2,1)}, u32[]{:S(2)}, u32[]{:S(2)}) collective-permute-start(bf16[2,320,512]{2,1,0:T(8,128)(2,1)} %get-tuple-element.121.refs_7_.refs_12_), channel_id=1, source_target_pairs={{0,2},{2,4},{4,6},{1,3},{3,5},{5,7},{8,10},{10,12},{12,14},{9,11},... | collective-permute-start | bytes 1966088 | tf_op jit(solution)/shard_map/ppermute | solution.py:977
  114.0 23.8 %collective-permute-start.11 = (s32[1,1]{1,0:T(1,128)}, s32[1,1]{1,0:T(1,128)}, u32[]{:S(2)}, u32[]{:S(2)}) collective-permute-start(s32[1,1]{1,0:T(1,128)} %add.83), channel_id=1, source_target_pairs={{0,2},{2,0},{4,6},{6,4},{1,3},{3,1},{5,7},{7,5},{8,10},{10,8},{12,... | collective-permute-start | bytes 20 | tf_op jit(solution)/shard_map/ppermute | solution.py:889
  137.3 33.8 %collective-permute-start.9 = (bf16[1280,512]{1,0:T(8,128)(2,1)}, bf16[1280,512]{1,0:T(8,128)(2,1)S(1)}, u32[]{:S(2)}, u32[]{:S(2)}) collective-permute-start(bf16[1280,512]{1,0:T(8,128)(2,1)} %get-tuple-element.126.refs_5_), channel_id=1, source_target_pairs={{0,1},{1,0},{2,3},{3,2},{4,5},{5,4},{6,7},{7,6},{8,9},{9,8},{10,11... | collective-permute-start | bytes 3932168 | tf_op jit(solution)/shard_map/ppermute | solution.py:889
  150.9 19.5 %collective-permute-start.12 = (s32[1,1]{1,0:T(1,128)}, s32[1,1]{1,0:T(1,128)}, u32[]{:S(2)}, u32[]{:S(2)}) collective-permute-start(s32[1,1]{1,0:T(1,128)} %add.84), channel_id=1, source_target_pairs={{0,4},{2,6},{4,0},{6,2},{1,5},{3,7},{5,1},{7,3},{8,12},{10,14},{12... | collective-permute-start | bytes 20 | tf_op jit(solution)/shard_map/ppermute | solution.py:889
  170.0 60.5 %collective-permute-start.7 = (bf16[1280,512]{1,0:T(8,128)(2,1)}, bf16[1280,512]{1,0:T(8,128)(2,1)S(1)}, u32[]{:S(2)}, u32[]{:S(2)}) collective-permute-start(bf16[1280,512]{1,0:T(8,128)(2,1)} %get-tuple-element.124.refs_5_), channel_id=1, source_target_pairs={{0,1},{1,0},{2,3},{3,2},{4,5},{5,4},{6,7},{7,6},{8,9},{9,8},{10,11... | collective-permute-start | bytes 3932168 | tf_op jit(solution)/shard_map/ppermute | solution.py:889
  228.8 61.5 %collective-permute-start.14 = (bf16[512,2560]{1,0:T(8,128)(2,1)}, bf16[512,2560]{1,0:T(8,128)(2,1)}, u32[]{:S(2)}, u32[]{:S(2)}) collective-permute-start(bf16[512,2560]{1,0:T(8,128)(2,1)} %get-tuple-element.136.refs_3_), channel_id=1, source_target_pairs={{0,1},{1,0},{2,3},{3,2},{4,5},{5,4},{6,7},{7,6},{8,9},{9,8},{10,11... | collective-permute-start | bytes 7864328 | tf_op jit(solution)/shard_map/ppermute | solution.py:889
  288.8 60.1 %collective-permute-start.13 = (bf16[512,2560]{1,0:T(8,128)(2,1)}, bf16[512,2560]{1,0:T(8,128)(2,1)S(1)}, u32[]{:S(2)}, u32[]{:S(2)}) collective-permute-start(bf16[512,2560]{1,0:T(8,128)(2,1)} %get-tuple-element.135.refs_3_), channel_id=1, source_target_pairs={{0,1},{1,0},{2,3},{3,2},{4,5},{5,4},{6,7},{7,6},{8,9},{9,8},{10,11... | collective-permute-start | bytes 7864328 | tf_op jit(solution)/shard_map/ppermute | solution.py:889
  339.0 143.2 %collective-permute-start.15 = (bf16[512,2560]{1,0:T(8,128)(2,1)}, bf16[512,2560]{1,0:T(8,128)(2,1)}, u32[]{:S(2)}, u32[]{:S(2)}) collective-permute-start(bf16[512,2560]{1,0:T(8,128)(2,1)} %get-tuple-element.142.refs_7_.refs_4_), channel_id=1, source_target_pairs={{0,1},{1,0},{2,3},{3,2},{4,5},{5,4},{6,7},{7,6},{8,9},{9,8},{10,11... | collective-permute-start | bytes 7864328 | tf_op jit(solution)/shard_map/ppermute | solution.py:889
  375.3 70.1 %collective-permute-start.16 = (bf16[640,1536]{1,0:T(8,128)(2,1)}, bf16[640,1536]{1,0:T(8,128)(2,1)S(1)}, u32[]{:S(2)}, u32[]{:S(2)}) collective-permute-start(bf16[640,1536]{1,0:T(8,128)(2,1)} %get-tuple-element.152.refs_3_), channel_id=1, source_target_pairs={{0,16},{8,24},{16,0},{24,8},{1,17},{9,25},{17,1},{25,9},{2,18},{10... | collective-permute-start | bytes 5898248 | tf_op jit(solution)/shard_map/ppermute | solution.py:889
  402.9 93.6 %collective-permute-start.18 = (bf16[640,2048]{1,0:T(8,128)(2,1)}, bf16[640,2048]{1,0:T(8,128)(2,1)}, u32[]{:S(2)}, u32[]{:S(2)}) collective-permute-start(bf16[640,2048]{1,0:T(8,128)(2,1)} %get-tuple-element.153.refs_8_), channel_id=1, source_target_pairs={{0,16},{8,24},{16,0},{24,8},{1,17},{9,25},{17,1},{25,9},{2,18},{10... | collective-permute-start | bytes 7864328 | tf_op jit(solution)/shard_map/ppermute | solution.py:889
  443.5 139.3 %collective-permute-start.17 = (bf16[512,2560]{1,0:T(8,128)(2,1)}, bf16[512,2560]{1,0:T(8,128)(2,1)}, u32[]{:S(2)}, u32[]{:S(2)}) collective-permute-start(bf16[512,2560]{1,0:T(8,128)(2,1)} %get-tuple-element.156.refs_2_.refs_4_), channel_id=1, source_target_pairs={{0,1},{1,0},{2,3},{3,2},{4,5},{5,4},{6,7},{7,6},{8,9},{9,8},{10,11... | collective-permute-start | bytes 7864328 | tf_op jit(solution)/shard_map/ppermute | solution.py:889
  449.1 51.1 %collective-permute-start.20 = (bf16[320,1536]{1,0:T(8,128)(2,1)}, bf16[320,1536]{1,0:T(8,128)(2,1)S(1)}, u32[]{:S(2)}, u32[]{:S(2)}) collective-permute-start(bf16[320,1536]{1,0:T(8,128)(2,1)} %near.7.refs_3_), channel_id=1, source_target_pairs={{0,2},{2,0},{4,6},{6,4},{1,3},{3,1},{5,7},{7,5},{8,10},{10,8},{12,... | collective-permute-start | bytes 2949128 | tf_op jit(solution)/shard_map/ppermute | solution.py:889
  480.1 119.5 %collective-permute-start.21 = (bf16[640,3584]{1,0:T(8,128)(2,1)}, bf16[640,3584]{1,0:T(8,128)(2,1)}, u32[]{:S(2)}, u32[]{:S(2)}) collective-permute-start(bf16[640,3584]{1,0:T(8,128)(2,1)} %get-tuple-element.157.refs_6_), channel_id=1, source_target_pairs={{0,16},{8,24},{16,0},{24,8},{1,17},{9,25},{17,1},{25,9},{2,18},{10... | collective-permute-start | bytes 13762568 | tf_op jit(solution)/shard_map/ppermute | solution.py:889
  499.2 54.2 %collective-permute-start.19 = (bf16[320,2048]{1,0:T(8,128)(2,1)}, bf16[320,2048]{1,0:T(8,128)(2,1)}, u32[]{:S(2)}, u32[]{:S(2)}) collective-permute-start(bf16[320,2048]{1,0:T(8,128)(2,1)} %near.8.refs_3_), channel_id=1, source_target_pairs={{0,2},{2,0},{4,6},{6,4},{1,3},{3,1},{5,7},{7,5},{8,10},{10,8},{12,... | collective-permute-start | bytes 3932168 | tf_op jit(solution)/shard_map/ppermute | solution.py:889
  503.4 132.5 %collective-permute-start.27 = (bf16[160,1536]{1,0:T(8,128)(2,1)}, bf16[160,1536]{1,0:T(8,128)(2,1)}, u32[]{:S(2)}, u32[]{:S(2)}) collective-permute-start(bf16[160,1536]{1,0:T(8,128)(2,1)} %fold.7.refs_13_), channel_id=1, source_target_pairs={{0,4},{2,6},{4,0},{6,2},{1,5},{3,7},{5,1},{7,3},{8,12},{10,14},{12... | collective-permute-start | bytes 1474568 | tf_op jit(solution)/shard_map/ppermute | solution.py:889
  522.1 33.8 %collective-permute-start.22 = (bf16[2,320,512]{2,1,0:T(8,128)(2,1)}, bf16[2,320,512]{2,1,0:T(8,128)(2,1)S(1)}, u32[]{:S(2)}, u32[]{:S(2)}) collective-permute-start(bf16[2,320,512]{2,1,0:T(8,128)(2,1)} %get-tuple-element.166.refs_3_), channel_id=1, source_target_pairs={{2,0},{4,2},{6,4},{3,1},{5,3},{7,5},{10,8},{12,10},{14,12},{11,9},... | collective-permute-start | bytes 1966088 | tf_op jit(solution)/shard_map/ppermute | solution.py:977
  553.5 131.3 %collective-permute-start.26 = (bf16[640,3584]{1,0:T(8,128)(2,1)}, bf16[640,3584]{1,0:T(8,128)(2,1)}, u32[]{:S(2)}, u32[]{:S(2)}) collective-permute-start(bf16[640,3584]{1,0:T(8,128)(2,1)} %get-tuple-element.167.refs_3_), channel_id=1, source_target_pairs={{0,16},{8,24},{16,0},{24,8},{1,17},{9,25},{17,1},{25,9},{2,18},{10... | collective-permute-start | bytes 13762568 | tf_op jit(solution)/shard_map/ppermute | solution.py:889
  556.0 179.4 %collective-permute-start.32 = (bf16[160,2048]{1,0:T(8,128)(2,1)}, bf16[160,2048]{1,0:T(8,128)(2,1)}, u32[]{:S(2)}, u32[]{:S(2)}) collective-permute-start(bf16[160,2048]{1,0:T(8,128)(2,1)} %fold.8.refs_7_), channel_id=1, source_target_pairs={{0,4},{2,6},{4,0},{6,2},{1,5},{3,7},{5,1},{7,3},{8,12},{10,14},{12... | collective-permute-start | bytes 1966088 | tf_op jit(solution)/shard_map/ppermute | solution.py:889
  582.8 51.5 %collective-permute-start.23 = (bf16[2,320,512]{2,1,0:T(8,128)(2,1)S(1)}, bf16[2,320,512]{2,1,0:T(8,128)(2,1)S(1)}, u32[]{:S(2)}, u32[]{:S(2)}) collective-permute-start(bf16[2,320,512]{2,1,0:T(8,128)(2,1)S(1)} %add_convert_fusion.3), channel_id=1, source_target_pairs={{2,0},{4,2},{6,4},{3,1},{5,3},{7,5},{10,8},{12,10},{14,12},{11,9},... | collective-permute-start | bytes 1966088 | tf_op jit(solution)/shard_map/ppermute | solution.py:977
  603.2 110.4 %collective-permute-start.25 = (bf16[320,3584]{1,0:T(8,128)(2,1)}, bf16[320,3584]{1,0:T(8,128)(2,1)}, u32[]{:S(2)}, u32[]{:S(2)}) collective-permute-start(bf16[320,3584]{1,0:T(8,128)(2,1)} %near.9.refs_14_), channel_id=1, source_target_pairs={{0,2},{2,0},{4,6},{6,4},{1,3},{3,1},{5,7},{7,5},{8,10},{10,8},{12,... | collective-permute-start | bytes 6881288 | tf_op jit(solution)/shard_map/ppermute | solution.py:889
  634.3 49.0 %collective-permute-start.29 = (bf16[2,320,512]{2,1,0:T(8,128)(2,1)}, bf16[2,320,512]{2,1,0:T(8,128)(2,1)S(1)}, u32[]{:S(2)}, u32[]{:S(2)}) collective-permute-start(bf16[2,320,512]{2,1,0:T(8,128)(2,1)} %get-tuple-element.177.refs_5_), channel_id=1, source_target_pairs={{2,0},{4,2},{6,4},{3,1},{5,3},{7,5},{10,8},{12,10},{14,12},{11,9},... | collective-permute-start | bytes 1966088 | tf_op jit(solution)/shard_map/ppermute | solution.py:977
  635.8 82.3 %collective-permute-start.24 = (bf16[2,320,512]{2,1,0:T(8,128)(2,1)S(1)}, bf16[2,320,512]{2,1,0:T(8,128)(2,1)}, u32[]{:S(2)}, u32[]{:S(2)}) collective-permute-start(bf16[2,320,512]{2,1,0:T(8,128)(2,1)S(1)} %add_convert_fusion.2), channel_id=1, source_target_pairs={{2,0},{4,2},{6,4},{3,1},{5,3},{7,5},{10,8},{12,10},{14,12},{11,9},... | collective-permute-start | bytes 1966088 | tf_op jit(solution)/shard_map/ppermute | solution.py:977
  683.5 27.9 %collective-permute-start.30 = (bf16[2,320,512]{2,1,0:T(8,128)(2,1)S(1)}, bf16[2,320,512]{2,1,0:T(8,128)(2,1)S(1)}, u32[]{:S(2)}, u32[]{:S(2)}) collective-permute-start(bf16[2,320,512]{2,1,0:T(8,128)(2,1)S(1)} %add_convert_fusion.1), channel_id=1, source_target_pairs={{2,0},{4,2},{6,4},{3,1},{5,3},{7,5},{10,8},{12,10},{14,12},{11,9},... | collective-permute-start | bytes 1966088 | tf_op jit(solution)/shard_map/ppermute | solution.py:977
  688.4 154.7 %collective-permute-start.34 = (bf16[320,3584]{1,0:T(8,128)(2,1)}, bf16[320,3584]{1,0:T(8,128)(2,1)}, u32[]{:S(2)}, u32[]{:S(2)}) collective-permute-start(bf16[320,3584]{1,0:T(8,128)(2,1)} %near.10.refs_3_), channel_id=1, source_target_pairs={{0,2},{2,0},{4,6},{6,4},{1,3},{3,1},{5,7},{7,5},{8,10},{10,8},{12,... | collective-permute-start | bytes 6881288 | tf_op jit(solution)/shard_map/ppermute | solution.py:889
  711.4 124.6 %collective-permute-start.36 = (bf16[640,1280]{1,0:T(8,128)(2,1)}, bf16[640,1280]{1,0:T(8,128)(2,1)}, u32[]{:S(2)}, u32[]{:S(2)}) collective-permute-start(bf16[640,1280]{1,0:T(8,128)(2,1)} %get-tuple-element.182.refs_3_), channel_id=1, source_target_pairs={{0,16},{8,24},{16,0},{24,8},{1,17},{9,25},{17,1},{25,9},{2,18},{10... | collective-permute-start | bytes 4915208 | tf_op jit(solution)/shard_map/ppermute | solution.py:889
  713.6 85.2 %collective-permute-start.31 = (bf16[2,320,512]{2,1,0:T(8,128)(2,1)S(1)}, bf16[2,320,512]{2,1,0:T(8,128)(2,1)S(1)}, u32[]{:S(2)}, u32[]{:S(2)}) collective-permute-start(bf16[2,320,512]{2,1,0:T(8,128)(2,1)S(1)} %add_convert_fusion), channel_id=1, source_target_pairs={{2,0},{4,2},{6,4},{3,1},{5,3},{7,5},{10,8},{12,10},{14,12},{11,9},... | collective-permute-start | bytes 1966088 | tf_op jit(solution)/shard_map/ppermute | solution.py:977
  718.1 120.5 %collective-permute-start.35 = (bf16[160,3584]{1,0:T(8,128)(2,1)}, bf16[160,3584]{1,0:T(8,128)(2,1)}, u32[]{:S(2)}, u32[]{:S(2)}) collective-permute-start(bf16[160,3584]{1,0:T(8,128)(2,1)} %fold.9.refs_8_), channel_id=1, source_target_pairs={{0,4},{2,6},{4,0},{6,2},{1,5},{3,7},{5,1},{7,3},{8,12},{10,14},{12... | collective-permute-start | bytes 3440648 | tf_op jit(solution)/shard_map/ppermute | solution.py:889
  735.4 89.8 %collective-permute-start.28 = (bf16[512,2560]{1,0:T(8,128)(2,1)}, bf16[512,2560]{1,0:T(8,128)(2,1)}, u32[]{:S(2)}, u32[]{:S(2)}) collective-permute-start(bf16[512,2560]{1,0:T(8,128)(2,1)} %get-tuple-element.183.refs_5_.refs_4_), channel_id=1, source_target_pairs={{0,1},{1,0},{2,3},{3,2},{4,5},{5,4},{6,7},{7,6},{8,9},{9,8},{10,11... | collective-permute-start | bytes 7864328 | tf_op jit(solution)/shard_map/ppermute | solution.py:889
  811.3 58.7 %collective-permute-start.33 = (bf16[512,2560]{1,0:T(8,128)(2,1)}, bf16[512,2560]{1,0:T(8,128)(2,1)S(1)}, u32[]{:S(2)}, u32[]{:S(2)}) collective-permute-start(bf16[512,2560]{1,0:T(8,128)(2,1)} %get-tuple-element.193.refs_3_.refs_4_), channel_id=1, source_target_pairs={{0,1},{1,0},{2,3},{3,2},{4,5},{5,4},{6,7},{7,6},{8,9},{9,8},{10,11... | collective-permute-start | bytes 7864328 | tf_op jit(solution)/shard_map/ppermute | solution.py:889
  825.2 56.3 %collective-permute-start.38 = (bf16[640,640]{1,0:T(8,128)(2,1)}, bf16[640,640]{1,0:T(8,128)(2,1)}, u32[]{:S(2)}, u32[]{:S(2)}) collective-permute-start(bf16[640,640]{1,0:T(8,128)(2,1)} %get-tuple-element.194.refs_6_), channel_id=1, source_target_pairs={{0,16},{8,24},{16,0},{24,8},{1,17},{9,25},{17,1},{25,9},{2,18},{10... | collective-permute-start | bytes 2457608 | tf_op jit(solution)/shard_map/ppermute | solution.py:889
  836.0 53.8 %collective-permute-start.43 = (bf16[640,1280]{1,0:T(8,128)(2,1)}, bf16[640,1280]{1,0:T(8,128)(2,1)}, u32[]{:S(2)}, u32[]{:S(2)}) collective-permute-start(bf16[640,1280]{1,0:T(8,128)(2,1)} %get-tuple-element.191.refs_9_), channel_id=1, source_target_pairs={{0,16},{8,24},{16,0},{24,8},{1,17},{9,25},{17,1},{25,9},{2,18},{10... | collective-permute-start | bytes 4915208 | tf_op jit(solution)/shard_map/ppermute | solution.py:889
  838.6 49.1 %collective-permute-start.40 = (bf16[320,1280]{1,0:T(8,128)(2,1)}, bf16[320,1280]{1,0:T(8,128)(2,1)}, u32[]{:S(2)}, u32[]{:S(2)}) collective-permute-start(bf16[320,1280]{1,0:T(8,128)(2,1)} %near.11.refs_5_), channel_id=1, source_target_pairs={{0,2},{2,0},{4,6},{6,4},{1,3},{3,1},{5,7},{7,5},{8,10},{10,8},{12,... | collective-permute-start | bytes 2457608 | tf_op jit(solution)/shard_map/ppermute | solution.py:889
  846.0 53.4 %collective-permute-start.42 = (bf16[160,3584]{1,0:T(8,128)(2,1)}, bf16[160,3584]{1,0:T(8,128)(2,1)}, u32[]{:S(2)}, u32[]{:S(2)}) collective-permute-start(bf16[160,3584]{1,0:T(8,128)(2,1)} %fold.10.refs_7_), channel_id=1, source_target_pairs={{0,4},{2,6},{4,0},{6,2},{1,5},{3,7},{5,1},{7,3},{8,12},{10,14},{12... | collective-permute-start | bytes 3440648 | tf_op jit(solution)/shard_map/ppermute | solution.py:889
  889.8 9.5 collective-permute-start.41
  892.1 34.6 %collective-permute-start.45 = (bf16[320,1280]{1,0:T(8,128)(2,1)}, bf16[320,1280]{1,0:T(8,128)(2,1)}, u32[]{:S(2)}, u32[]{:S(2)}) collective-permute-start(bf16[320,1280]{1,0:T(8,128)(2,1)} %near.13.refs_5_), channel_id=1, source_target_pairs={{0,2},{2,0},{4,6},{6,4},{1,3},{3,1},{5,7},{7,5},{8,10},{10,8},{12,... | collective-permute-start | bytes 2457608 | tf_op jit(solution)/shard_map/ppermute | solution.py:889
  904.0 9.8 %collective-permute-start.44 = (f32[3,2560]{1,0:T(4,128)S(1)}, f32[3,2560]{1,0:T(4,128)S(1)}, u32[]{:S(2)}, u32[]{:S(2)}) collective-permute-start(f32[3,2560]{1,0:T(4,128)S(1)} %add.95), channel_id=1, source_target_pairs={{0,4},{2,6},{4,0},{6,2},{1,5},{3,7},{5,1},{7,3},{8,12},{10,14},{12... | collective-permute-start | bytes 92168 | tf_op jit(solution)/shard_map/ppermute | solution.py:889
  905.6 29.7 %collective-permute-start.47 = (bf16[320,640]{1,0:T(8,128)(2,1)S(1)}, bf16[320,640]{1,0:T(8,128)(2,1)S(1)}, u32[]{:S(2)}, u32[]{:S(2)}) collective-permute-start(bf16[320,640]{1,0:T(8,128)(2,1)S(1)} %copy-done.31), channel_id=1, source_target_pairs={{0,2},{2,0},{4,6},{6,4},{1,3},{3,1},{5,7},{7,5},{8,10},{10,8},{12,... | collective-permute-start | bytes 1228808 | tf_op jit(solution)/shard_map/ppermute | solution.py:889
  906.6 23.9 %collective-permute-start.48 = (bf16[160,1280]{1,0:T(8,128)(2,1)}, bf16[160,1280]{1,0:T(8,128)(2,1)S(1)}, u32[]{:S(2)}, u32[]{:S(2)}) collective-permute-start(bf16[160,1280]{1,0:T(8,128)(2,1)} %fold.11.refs_2_), channel_id=1, source_target_pairs={{0,4},{2,6},{4,0},{6,2},{1,5},{3,7},{5,1},{7,3},{8,12},{10,14},{12... | collective-permute-start | bytes 1228808 | tf_op jit(solution)/shard_map/ppermute | solution.py:889
  928.8 24.6 %collective-permute-start.46 = (bf16[160,1280]{1,0:T(8,128)(2,1)}, bf16[160,1280]{1,0:T(8,128)(2,1)S(1)}, u32[]{:S(2)}, u32[]{:S(2)}) collective-permute-start(bf16[160,1280]{1,0:T(8,128)(2,1)} %fold.12.refs_5_), channel_id=1, source_target_pairs={{0,4},{2,6},{4,0},{6,2},{1,5},{3,7},{5,1},{7,3},{8,12},{10,14},{12... | collective-permute-start | bytes 1228808 | tf_op jit(solution)/shard_map/ppermute | solution.py:889
  938.0 19.7 %collective-permute-start.49 = (bf16[160,640]{1,0:T(8,128)(2,1)}, bf16[160,640]{1,0:T(8,128)(2,1)S(1)}, u32[]{:S(2)}, u32[]{:S(2)}) collective-permute-start(bf16[160,640]{1,0:T(8,128)(2,1)} %fold.13.refs_5_), channel_id=1, source_target_pairs={{0,4},{2,6},{4,0},{6,2},{1,5},{3,7},{5,1},{7,3},{8,12},{10,14},{12... | collective-permute-start | bytes 614408 | tf_op jit(solution)/shard_map/ppermute | solution.py:889
  (38 other events, 348.3 us)
Sparse Core Ops, SparseCore 0:
  57.9 48.9 all-gather.1

commit v2 on v1

--- a/solution.py
+++ b/solution.py
@@ -19,9 +19,9 @@
 F32 = jnp.float32
 MIB = 1024 * 1024
 ROWS = 128
-WEIGHTS = {'at1': 30, 'ab1': 100, 'eb': 30, 'Gu': 60, 'at0': 30, 's0': 0, 'fw0': 30, 'Gb': 0.5, 'Gk': 0, 'in0': 15, 'eo': 60, 'na': 0.5, 'nk': 60, 'eq': 0, 'Ga': 60, 'nu': 15, 'fa': 0, 'h12': 0, 'fw1': 15, 'mb1': 0.5, 's1': 0, 'qb1': 8, 'h10': 60, 'c2': 1, 's3': 2, 'fg': 15}
+WEIGHTS = {'at1': 30, 'ab1': 100, 'eb': 30, 'Gu': 60, 'at0': 30, 's0': 0, 'fw0': 30, 'Gb': 0.5, 'Gk': 0, 'in0': 15, 'eo': 60, 'na': 0.5, 'nk': 60, 'nu': 15, 'fa': 0, 'h12': 0, 'fw1': 15, 'mb1': 100, 's1': 0}
 ORDER = (
-    "at0", "c2", "at1", "c3", "fw0", "fw1", "er0", "bw0", "er1", "Ga", "Gb", "bw1", "na", "Gg", "mb0", "nb", "fa", "ab0", "h00", "Gu", "fb", "h01", "mb1", "ng", "ab1", "h10", "h02", "ea", "h11", "nu", "h12", "Go", "fg", "qb0", "eb", "Gq", "qb1", "Gk", "in0", "no", "eg", "fu", "in1", "s0", "nk", "s1", "fo", "s2", "nq", "eu", "s3", "fq", "eo", "fk", "eq", "ek",
+    "at0", "c2", "qp1", "at1", "c3", "fw0", "fw1", "er0", "bw0", "er1", "Ga", "Gb", "bw1", "na", "Gg", "mb0", "nb", "fa", "ab0", "h00", "Gu", "h01", "fb", "mb1", "ng", "ab1", "h10", "h02", "ea", "h11", "nu", "h12", "Go", "fg", "qb0", "eb", "Gq", "qb1", "Gk", "in0", "no", "fu", "eg", "in1", "s0", "nk", "s1", "fo", "s2", "nq", "eu", "s3", "fq", "eo", "fk", "eq", "ek",
 )
 PRESENT = [5]
 
@@ -523,7 +523,7 @@
     num_seqs, rows, model = hidden.shape
     hidden_width = w_gate.shape[1]
     width = mixed[0].shape[0]
-    wide, narrow = divisor(hidden_width, 512), 640
+    wide, narrow = divisor(hidden_width, 512), 512
     counts = (model // narrow, rows // ROWS, hidden_width // wide, model // narrow)
     attn, norm, mid, out = (phase(sum(counts[:at]), count) for at, count in enumerate(counts))
     row_spec = pl.BlockSpec((ROWS, model), lambda i: (norm(i), 0))
@@ -1012,7 +1012,7 @@
 
     count = jnp.sum(valid_mask).reshape(1, 1)
     count = count + swap(count, "dp", 1)
-    normed, queries, kv_chunks = [], [], []
+    normed, kv_chunks = [], []
     normed_t, last = None, hidden_in
     for s in seqs:
         n_rows, normed_t, kv_own = kv_project(
@@ -1022,16 +1022,13 @@
         kv_chunks.append([kv_own])
         last = n_rows
     kv_chunks[0].append(shift(kv_chunks[0][0], 1))
-    after = [last, kv_chunks[0][-1], count]
     kv_chunks[0].append(shift(held(kv_chunks[0][-1], last), 1))
-    for s in seqs:
-        queries.append(q_project(s, normed[s], w_query, cos, sin, after))
-        last = queries[-1]
-        after = [last]
-    count = count + swap(held(count, queries[0]), "dp", 2)
+    last = q_project(0, normed[0], w_query, cos, sin, [last, kv_chunks[0][1]])
+    queries = [last]
+    count = count + swap(held(count, last), "dp", 2)
     kv_chunks[0].append(shift(held(kv_chunks[0][-1], last), 1))
     for s in seqs[1:]:
-        own = held(kv_chunks[s][0], kv_chunks[0][-1], last)
+        own = held(kv_chunks[s][0], kv_chunks[0][-1])
         for step in range(1, ctx_size):
             kv_chunks[s].append(shift(own, step))
 
@@ -1039,7 +1036,7 @@
     lse, middle, rows_a, rows_b = [], [], [], []
     losses, dys, mlp_gains, attn_gains, grad_middle = [], [], [], [], []
     heads, mlp_parts, dn2_parts, dn1_parts, pieces, came = [], [], [], [], [], [None, None]
-    w_outs = tensor_weights(w_out, queries[-1])
+    w_outs = tensor_weights(held(w_out, normed[0]), kv_chunks[0][-1])
     tokens = num_seqs * piece * ctx_size * lax.axis_size("dp")
     last_seq = num_seqs - 1
 
@@ -1061,6 +1058,10 @@
         lse.append(lse_rows)
         heads.append(tensor_copies(heads_out))
         return lse_rows
+
+    def query(s, after):
+        queries.append(q_project(s, normed[s], w_query, cos, sin, after))
+        return queries[s]
 
     def forward(s, after):
         m_rows, made["n2"], made["z"], a, b, partial = forward_mlp(
@@ -1230,6 +1231,7 @@
     for s in seqs:
         for short, one in (
             ("at", attention),
+            ("qp", query),
             ("fw", forward),
             ("er", error),
             ("bw", backward),

time: 981 us -> 966 us (0.985)
  waiting for transfers between devices: 188 us -> 177 us
    ppermute x38, starting transfers between devices: 132 us -> 121 us  [swap(): return lax.ppermute(value, axis, [(i, i ^ bit) for i in range(size)])]
    ppermute x38, waiting for transfers between devices: 75.8 us -> 65.6 us  [swap(): return lax.ppermute(value, axis, [(i, i ^ bit) for i in range(size)])]
  transfers between devices with their start and end apart: 51 -> 51, of which waited for: 17 -> 17; matrix products, arithmetic and copies ran while one was open for 1% -> 2% of each run, Pallas kernels for 58% -> 59%
where the time goes in v2:
time: 966 us; the launch traced here: 955 us
  Pallas kernels  572 us (59%)
  waiting for transfers between devices  177 us (18%)
  starting transfers between devices  154 us (16%)
  local copies, waits for them, and re-layouts  21.6 us (2%)
  between operations  20 us (2%)
  other arithmetic  9.8 us (1%)
    pallas_call x48, Pallas kernels, run(): pl.pallas_call(inner, grid_spec=pltpu.PrefetchScalarGridSpec(num_scalar_p...  572 us
    ppermute x38, starting transfers between devices, swap(): return lax.ppermute(value, axis, [(i, i ^ bit) for i in range(size)])  121 us
    ppermute x12, waiting for transfers between devices, shift(): return lax.ppermute(value, 'ctx', pairs)  111 us
    ppermute x38, waiting for transfers between devices, swap(): return lax.ppermute(value, axis, [(i, i ^ bit) for i in range(size)])  65.6 us
    ppermute x12, starting transfers between devices, shift(): return lax.ppermute(value, 'ctx', pairs)  33 us
  transfers between devices with their start and end apart: 51, of which 17 were waited for; matrix products, arithmetic and copies ran while one was open for 2% of the time, Pallas kernels for 59%

profile of v2, /device:TPU:0, one launch (start us, length us, event | category | flops | bytes accessed | tf_op | source)
XLA Modules:
  0.0 954.8 jit_solution(16335532367839980948)
XLA Ops:
  10.6 6.5 kv_project.2
  17.2 5.0 collective-permute-start
  26.4 6.5 kv_project.3
  36.4 4.4 collective-permute-start.1
  40.9 8.4 q_project.2.refs_3_.refs_8_.refs_5_
  49.2 4.7 collective-permute-done.1.refs_5_.refs_10_
  62.3 8.1 collective-permute-done.2.refs_4_.refs_9_
  78.8 6.4 collective-permute-start.3
  90.2 11.4 %attend.2 = (bf16[1280,512]{1,0:T(8,128)(2,1)}, bf16[1280,1024]{1,0:T(8,128)(2,1)}, f32[4,4,512]{2,1,0:T(4,128)}) custom-call(s32[2]{0:T(128)} %get-tuple-element.233.refs_0_, s32[2]{0:T(128)} %get-tuple-element.228.refs_1_, s32[1,512]{1,0:T(1,128)} %get-tuple-element.222.refs_2_, bf16[1280,512]{1,0:T(8,128)(2,1)} %q_project.2.refs_3_.refs_8_.refs_5_, ...), custom_call_target="tpu_custom_call" | custom-call | flops 30000001024 | bytes 1000 | tf_op jit(solution)/shard_map/attend/pallas_call | solution.py:46
  101.6 25.4 %collective-permute-start.11 = (s32[1,1]{1,0:T(1,128)}, s32[1,1]{1,0:T(1,128)}, u32[]{:S(2)}, u32[]{:S(2)}) collective-permute-start(s32[1,1]{1,0:T(1,128)} %add.83), channel_id=1, source_target_pairs={{0,2},{2,0},{4,6},{6,4},{1,3},{3,1},{5,7},{7,5},{8,10},{10,8},{12,... | collective-permute-start | bytes 20 | tf_op jit(solution)/shard_map/ppermute | solution.py:889
  128.5 8.4 q_project.3.refs_3_.refs_9_.refs_5_
  138.6 11.4 %attend.3 = (bf16[1280,512]{1,0:T(8,128)(2,1)}, bf16[1280,1024]{1,0:T(8,128)(2,1)}, f32[4,4,512]{2,1,0:T(4,128)}) custom-call(s32[2]{0:T(128)} %get-tuple-element.232.refs_0_, s32[2]{0:T(128)} %get-tuple-element.229.refs_1_, s32[1,512]{1,0:T(1,128)} %get-tuple-element.223.refs_2_, ...), custom_call_target="tpu_custom_call", output_to_operand_aliasing={{1}: (8, {})} | custom-call | flops 30000001024 | bytes 1000 | tf_op jit(solution)/shard_map/attend/pallas_call | solution.py:46
  150.0 9.7 %collective-permute-start.12 = (s32[1,1]{1,0:T(1,128)}, s32[1,1]{1,0:T(1,128)}, u32[]{:S(2)}, u32[]{:S(2)}) collective-permute-start(s32[1,1]{1,0:T(1,128)} %add.84), channel_id=1, source_target_pairs={{0,4},{2,6},{4,0},{6,2},{1,5},{3,7},{5,1},{7,3},{8,12},{10,14},{12... | collective-permute-start | bytes 20 | tf_op jit(solution)/shard_map/ppermute | solution.py:889
  162.9 54.0 %forward_mlp.2 = (bf16[512,2560]{1,0:T(8,128)(2,1)}, bf16[2560,1024]{1,0:T(8,128)(2,1)}, bf16[2,512,3584]{2,1,0:T(8,128)(2,1)}, bf16[512,3584]{1,0:T(8,128)(2,1)...) custom-call(bf16[2,512,2560]{2,1,0:T(8,128)(2,1)} %refs_1_.15, f32[1,2560]{1,0:T(1,128)} %broadcast_in_dim.18.refs_1_.refs_2_, ...), custom_call_target="tpu_custom_call" | custom-call | flops 30000001024 | bytes 1000 | tf_op jit(solution)/shard_map/forward_mlp/pallas_call | solution.py:46
  218.6 53.8 %forward_mlp.3 = (bf16[512,2560]{1,0:T(8,128)(2,1)}, bf16[2560,1024]{1,0:T(8,128)(2,1)}, bf16[2,512,3584]{2,1,0:T(8,128)(2,1)}, bf16[512,3584]{1,0:T(8,128)(2,1)...) custom-call(bf16[2,512,2560]{2,1,0:T(8,128)(2,1)} %refs_1_.15, ...), custom_call_target="tpu_custom_call", output_to_operand_aliasing={{1}: (9, {}), {2}: (10, {})} | custom-call | flops 15000000512 | bytes 1000 | tf_op jit(solution)/shard_map/forward_mlp/pallas_call | solution.py:46
  275.0 8.2 output_error.2
  283.2 40.6 %backward_mlp.2 = (bf16[2,512,3584]{2,1,0:T(8,128)(2,1)}, bf16[2,512,3584]{2,1,0:T(8,128)(2,1)}, bf16[512,2560]{1,0:T(8,128)(2,1)}) custom-call(bf16[512,2560]{1,0:T(8,128)(2,1)} %get-tuple-element.141.refs_0_.refs_6_.refs_1_, bf16[3584,2560]{1,0:T(8,128)(2,1)} %refs_1_.13, bf16[512,3584]{1,0:T(8,128)(2,1)} %get-tuple-element.142.refs_2_, ...), custom_call_target="tpu_custom_call" | custom-call | flops 5000001024 | bytes 1000 | tf_op jit(solution)/shard_map/backward_mlp/pallas_call | solution.py:46
  325.9 8.2 output_error.3
  334.1 30.8 %weight_grad.7 = (bf16[640,1536]{1,0:T(8,128)(2,1)}, bf16[320,1536]{1,0:T(8,128)(2,1)}, bf16[320,1536]{1,0:T(8,128)(2,1)}) custom-call(bf16[2560,1024]{1,0:T(8,128)(2,1)} %get-tuple-element.152.refs_0_, bf16[2,512,3584]{2,1,0:T(8,128)(2,1)} %get-tuple-element.153.refs_1_.refs_2_, bf16[2,512,3584]{2,1,0:T(8,128)(2,1)} %get-tuple-element.153.refs_1_.refs_2_, ...), custom_call_target="tpu_custom_call" | custom-call | flops 5000001024 | bytes 1000 | tf_op jit(solution)/shard_map/weight_grad/pallas_call | solution.py:46
  365.0 20.0 %weight_grad.8 = (bf16[640,2048]{1,0:T(8,128)(2,1)}, bf16[320,2048]{1,0:T(8,128)(2,1)}, bf16[320,2048]{1,0:T(8,128)(2,1)}) custom-call(bf16[2560,1024]{1,0:T(8,128)(2,1)} %get-tuple-element.152.refs_0_, bf16[2,512,3584]{2,1,0:T(8,128)(2,1)} %get-tuple-element.153.refs_1_.refs_2_, bf16[2,512,3584]{2,1,0:T(8,128)(2,1)} %get-tuple-element.153.refs_1_.refs_2_, ...), custom_call_target="tpu_custom_call" | custom-call | flops 500000992 | bytes 1000 | tf_op jit(solution)/shard_map/weight_grad/pallas_call | solution.py:46
  387.1 40.7 %backward_mlp.3 = (bf16[2,512,3584]{2,1,0:T(8,128)(2,1)}, bf16[2,512,3584]{2,1,0:T(8,128)(2,1)}, bf16[512,2560]{1,0:T(8,128)(2,1)}) custom-call(bf16[512,2560]{1,0:T(8,128)(2,1)} %get-tuple-element.147.refs_3_.refs_0_.refs_1_, bf16[3584,2560]{1,0:T(8,128)(2,1)} %refs_1_.13, ...), custom_call_target="tpu_custom_call", output_to_operand_aliasing={{0}: (6, {}), {1}: (7, {})} | custom-call | flops 5000001024 | bytes 1000 | tf_op jit(solution)/shard_map/backward_mlp/pallas_call | solution.py:46
  434.4 6.6 collective-permute-start.20
  441.1 29.9 %weight_grad.9 = (bf16[640,3584]{1,0:T(8,128)(2,1)}, bf16[320,3584]{1,0:T(8,128)(2,1)}, bf16[320,3584]{1,0:T(8,128)(2,1)}) custom-call(bf16[2560,1024]{1,0:T(8,128)(2,1)} %get-tuple-element.146.refs_0_, bf16[2,512,3584]{2,1,0:T(8,128)(2,1)} %get-tuple-element.156.refs_1_.refs_2_, bf16[2,512,3584]{2,1,0:T(8,128)(2,1)} %get-tuple-element.156.refs_1_.refs_2_, ...), custom_call_target="tpu_custom_call" | custom-call | flops 5000001024 | bytes 1000 | tf_op jit(solution)/shard_map/weight_grad/pallas_call | solution.py:46
  471.1 13.9 %middle_back.2 = (bf16[512,2560]{1,0:T(8,128)(2,1)}, bf16[2560,1024]{1,0:T(8,128)(2,1)}, f32[1,2560]{1,0:T(1,128)}, bf16[1280,512]{1,0:T(8,128)(2,1)}) custom-call(bf16[512,2560]{1,0:T(8,128)(2,1)} %get-tuple-element.135.refs_11_.refs_0_, bf16[512,2560]{1,0:T(8,128)(2,1)} %get-tuple-element.141.refs_0_.refs_6_.refs_1_, ...), custom_call_target="tpu_custom_call" | custom-call | flops 5000001024 | bytes 1000 | tf_op jit(solution)/shard_map/middle_back/pallas_call | solution.py:46
  492.8 16.1 %attend_back.2 = (bf16[1280,1024]{1,0:T(8,128)(2,1)}, bf16[2,320,512]{2,1,0:T(8,128)(2,1)}, bf16[2,320,512]{2,1,0:T(8,128)(2,1)}, bf16[2,320,512]{2,1,0:T(8,128)(2,1)}, bf16[2,320,512]{2,1,0:T(8,128)(2,1)}) custom-call(s32[2]{0:T(128)} %get-tuple-element.233.refs_0_, s32[2]{0:T(128)} %get-tuple-element.228.refs_1_, s32[1,512]{1,0:T(1,128)} %get-tuple-element.222.refs_2_, ...), custom_call_target="tpu_custom_call" | custom-call | flops 5000001024 | bytes 1000 | tf_op jit(solution)/shard_map/attend_back/pallas_call | solution.py:46
  510.2 30.0 %weight_grad.10 = (bf16[640,3584]{1,0:T(8,128)(2,1)}, bf16[320,3584]{1,0:T(8,128)(2,1)}, bf16[320,3584]{1,0:T(8,128)(2,1)}) custom-call(bf16[2560,1024]{1,0:T(8,128)(2,1)} %get-tuple-element.146.refs_0_, bf16[2,512,3584]{2,1,0:T(8,128)(2,1)} %get-tuple-element.165.refs_1_.refs_2_, bf16[2,512,3584]{2,1,0:T(8,128)(2,1)} %get-tuple-element.165.refs_1_.refs_2_, ...), custom_call_target="tpu_custom_call" | custom-call | flops 60000002048 | bytes 1000 | tf_op jit(solution)/shard_map/weight_grad/pallas_call | solution.py:46
  550.3 25.5 %collective-permute-start.32 = (bf16[160,2048]{1,0:T(8,128)(2,1)}, bf16[160,2048]{1,0:T(8,128)(2,1)}, u32[]{:S(2)}, u32[]{:S(2)}) collective-permute-start(bf16[160,2048]{1,0:T(8,128)(2,1)} %fold.8.refs_7_), channel_id=1, source_target_pairs={{0,4},{2,6},{4,0},{6,2},{1,5},{3,7},{5,1},{7,3},{8,12},{10,14},{12... | collective-permute-start | bytes 1966088 | tf_op jit(solution)/shard_map/ppermute | solution.py:889
  575.8 13.9 %middle_back.3 = (bf16[512,2560]{1,0:T(8,128)(2,1)}, bf16[2560,1024]{1,0:T(8,128)(2,1)}, f32[1,2560]{1,0:T(1,128)}, bf16[1280,512]{1,0:T(8,128)(2,1)}) custom-call(bf16[512,2560]{1,0:T(8,128)(2,1)} %get-tuple-element.136.refs_5_.refs_0_, bf16[512,2560]{1,0:T(8,128)(2,1)} %get-tuple-element.147.refs_3_.refs_0_.refs_1_, ...), custom_call_target="tpu_custom_call", output_to_operand_aliasing={{1}: (6, {})} | custom-call | flops 99999997952 | bytes 1000 | tf_op jit(solution)/shard_map/middle_back/pallas_call | solution.py:46
  594.6 15.5 %collective-permute-start.25 = (bf16[320,3584]{1,0:T(8,128)(2,1)}, bf16[320,3584]{1,0:T(8,128)(2,1)}, u32[]{:S(2)}, u32[]{:S(2)}) collective-permute-start(bf16[320,3584]{1,0:T(8,128)(2,1)} %near.9.refs_14_), channel_id=1, source_target_pairs={{0,2},{2,0},{4,6},{6,4},{1,3},{3,1},{5,7},{7,5},{8,10},{10,8},{12,... | collective-permute-start | bytes 6881288 | tf_op jit(solution)/shard_map/ppermute | solution.py:889
  610.1 15.8 %attend_back.3 = (bf16[1280,1024]{1,0:T(8,128)(2,1)}, bf16[2,320,512]{2,1,0:T(8,128)(2,1)}, bf16[2,320,512]{2,1,0:T(8,128)(2,1)}, bf16[2,320,512]{2,1,0:T(8,128)(2,1)}, bf16[2,320,512]{2,1,0:T(8,128)(2,1)}) custom-call(s32[2]{0:T(128)} %get-tuple-element.232.refs_0_, s32[2]{0:T(128)} %get-tuple-element.229.refs_1_, ...), custom_call_target="tpu_custom_call", output_to_operand_aliasing={{0}: (13, {})} | custom-call | flops 99999997952 | bytes 1000 | tf_op jit(solution)/shard_map/attend_back/pallas_call | solution.py:46
  632.6 42.5 %collective-permute-done.29 = bf16[2,320,512]{2,1,0:T(8,128)(2,1)S(1)} collective-permute-done((bf16[2,320,512]{2,1,0:T(8,128)(2,1)}, bf16[2,320,512]{2,1,0:T(8,128)(2,1)S(1)}, u32[]{:S(2)}, u32[]{:S(2)}) %collective-permute-start.29) | collective-permute-done | bytes 655392 | tf_op jit(solution)/shard_map/ppermute | solution.py:977
  682.7 15.5 %weight_grad.11 = (bf16[640,1280]{1,0:T(8,128)(2,1)}, bf16[320,1280]{1,0:T(8,128)(2,1)}, bf16[320,1280]{1,0:T(8,128)(2,1)}) custom-call(bf16[2560,1024]{1,0:T(8,128)(2,1)} %get-tuple-element.182.refs_0_, bf16[1280,1024]{1,0:T(8,128)(2,1)} %get-tuple-element.161.refs_6_.refs_1_.refs_2_, bf16[1280,1024]{1,0:T(8,128)(2,1)} %get-tuple-element.161.refs_6_.refs_1_.refs_2_, ...), custom_call_target="tpu_custom_call" | custom-call | flops 5000001024 | bytes 1000 | tf_op jit(solution)/shard_map/weight_grad/pallas_call | solution.py:46
  698.3 4.9 collective-permute-done.30
  707.9 6.6 collective-permute-start.34
  714.5 11.7 %qkv_back.2 = (bf16[640,1024]{1,0:T(8,128)(2,1)}, bf16[512,2560]{1,0:T(8,128)(2,1)}) custom-call(bf16[1280,1024]{1,0:T(8,128)(2,1)} %get-tuple-element.174.refs_0_.refs_1_.refs_2_, f32[2,40,512]{2,1,0:T(8,128)} %get-tuple-element.219.refs_4_.refs_2_.refs_3_.refs_1_, f32[2,40,512]{2,1,0:T(8,128)} %get-tuple-element.218.refs_5_.refs_3_.refs_4_.refs_2_, ...), custom_call_target="tpu_custom_call" | custom-call | flops 5000001024 | bytes 1000 | tf_op jit(solution)/shard_map/qkv_back/pallas_call | solution.py:46
  729.5 16.5 %weight_grad.12 = (bf16[640,1280]{1,0:T(8,128)(2,1)}, bf16[320,1280]{1,0:T(8,128)(2,1)}, bf16[320,1280]{1,0:T(8,128)(2,1)}) custom-call(bf16[2560,1024]{1,0:T(8,128)(2,1)} %get-tuple-element.186.refs_0_, bf16[1280,1024]{1,0:T(8,128)(2,1)} %get-tuple-element.174.refs_0_.refs_1_.refs_2_, bf16[1280,1024]{1,0:T(8,128)(2,1)} %get-tuple-element.174.refs_0_.refs_1_.refs_2_, ...), custom_call_target="tpu_custom_call" | custom-call | flops 5000001024 | bytes 1000 | tf_op jit(solution)/shard_map/weight_grad/pallas_call | solution.py:46
  746.1 44.1 %collective-permute-done.31.refs_7_ = bf16[2,320,512]{2,1,0:T(8,128)(2,1)S(1)} collective-permute-done((bf16[2,320,512]{2,1,0:T(8,128)(2,1)S(1)}, bf16[2,320,512]{2,1,0:T(8,128)(2,1)S(1)}, u32[]{:S(2)}, u32[]{:S(2)}) %collective-permute-start.31) | collective-permute-done | bytes 655392 | tf_op jit(solution)/shard_map/ppermute | solution.py:977
  791.0 11.6 %qkv_back.3 = (bf16[640,1024]{1,0:T(8,128)(2,1)}, bf16[512,2560]{1,0:T(8,128)(2,1)}) custom-call(bf16[1280,1024]{1,0:T(8,128)(2,1)} %get-tuple-element.174.refs_0_.refs_1_.refs_2_, f32[2,40,512]{2,1,0:T(8,128)} %get-tuple-element.219.refs_4_.refs_2_.refs_3_.refs_1_, ...), custom_call_target="tpu_custom_call", output_to_operand_aliasing={{0}: (8, {})} | custom-call | flops 5000001024 | bytes 1000 | tf_op jit(solution)/shard_map/qkv_back/pallas_call | solution.py:46
  803.2 13.1 %weight_grad.13 = (bf16[640,640]{1,0:T(8,128)(2,1)}, bf16[320,640]{1,0:T(8,128)(2,1)}, bf16[320,640]{1,0:T(8,128)(2,1)}) custom-call(bf16[2560,1024]{1,0:T(8,128)(2,1)} %get-tuple-element.186.refs_0_, bf16[640,1024]{1,0:T(8,128)(2,1)} %get-tuple-element.194.refs_1_.refs_2_, bf16[640,1024]{1,0:T(8,128)(2,1)} %get-tuple-element.194.refs_1_.refs_2_, ...), custom_call_target="tpu_custom_call" | custom-call | flops 1000 | bytes 1000 | tf_op jit(solution)/shard_map/weight_grad/pallas_call | solution.py:46
  816.6 9.0 input_back.2
  832.7 4.5 final.9.refs_7_
  837.1 23.9 %collective-permute-done.33.refs_5_ = bf16[512,2560]{1,0:T(8,128)(2,1)S(1)} collective-permute-done((bf16[512,2560]{1,0:T(8,128)(2,1)}, bf16[512,2560]{1,0:T(8,128)(2,1)S(1)}, u32[]{:S(2)}, u32[]{:S(2)}) %collective-permute-start.33) | collective-permute-done | bytes 2621472 | tf_op jit(solution)/shard_map/ppermute | solution.py:889
  862.6 9.0 input_back.3
  886.0 4.6 final.10.refs_3_
  895.1 9.6 %collective-permute-done.44 = f32[3,2560]{1,0:T(4,128)S(1)} collective-permute-done((f32[3,2560]{1,0:T(4,128)S(1)}, f32[3,2560]{1,0:T(4,128)S(1)}, u32[]{:S(2)}, u32[]{:S(2)}) %collective-permute-start.44) | collective-permute-done | bytes 30752 | tf_op jit(solution)/shard_map/ppermute | solution.py:889
  906.6 7.5 collective-permute-done.45.refs_2_.refs_3_
  916.2 6.2 collective-permute-done.48.refs_4_
  931.5 7.7 collective-permute-done.46.refs_4_
  (202 shorter events, 145.9 us)
Async XLA Ops:
  7.2 154.6 %all-gather.2.cloned.1.call-start = ((), (), s32[]{:S(2)}) async-start(), calls=%async_computation | async-start | bytes 8192000 | tf_op jit(solution)/shard_map/all_gather | solution.py:967
  17.2 19.2 %collective-permute-start = (bf16[2,320,512]{2,1,0:T(8,128)(2,1)}, bf16[2,320,512]{2,1,0:T(8,128)(2,1)S(1)}, u32[]{:S(2)}, u32[]{:S(2)}) collective-permute-start(bf16[2,320,512]{2,1,0:T(8,128)(2,1)} %get-tuple-element.118.refs_7_.refs_12_), channel_id=1, source_target_pairs={{0,2},{2,4},{4,6},{1,3},{3,5},{5,7},{8,10},{10,12},{12,14},{9,11},... | collective-permute-start | bytes 1966088 | tf_op jit(solution)/shard_map/ppermute | solution.py:977
  24.9 37.5 %collective-permute-start.7 = (bf16[320,2560]{1,0:T(8,128)(2,1)}, bf16[320,2560]{1,0:T(8,128)(2,1)S(1)}, u32[]{:S(2)}, u32[]{:S(2)}) collective-permute-start(bf16[320,2560]{1,0:T(8,128)(2,1)} %constant_dynamic-slice_fusion), channel_id=1, source_target_pairs={{0,1},{1,0},{2,3},{3,2},{4,5},{5,4},{6,7},{7,6},{8,9},{9,8},{10,11... | collective-permute-start | bytes 4915208 | tf_op jit(solution)/shard_map/ppermute | solution.py:889
  36.4 17.5 %collective-permute-start.1 = (bf16[2,320,512]{2,1,0:T(8,128)(2,1)S(1)}, bf16[2,320,512]{2,1,0:T(8,128)(2,1)S(1)}, u32[]{:S(2)}, u32[]{:S(2)}) collective-permute-start(bf16[2,320,512]{2,1,0:T(8,128)(2,1)S(1)} %collective-permute-done.refs_5_.refs_6_.refs_11_), channel_id=1, source_target_pairs={{0,2},{2,4},{4,6},{1,3},{3,5},{5,7},{8,10},{10,12},{12,14},{9,11},... | collective-permute-start | bytes 1966088 | tf_op jit(solution)/shard_map/ppermute | solution.py:977
  53.9 16.6 %collective-permute-start.2 = (bf16[2,320,512]{2,1,0:T(8,128)(2,1)S(1)}, bf16[2,320,512]{2,1,0:T(8,128)(2,1)S(1)}, u32[]{:S(2)}, u32[]{:S(2)}) collective-permute-start(bf16[2,320,512]{2,1,0:T(8,128)(2,1)S(1)} %collective-permute-done.1.refs_5_.refs_10_), channel_id=1, source_target_pairs={{0,2},{2,4},{4,6},{1,3},{3,5},{5,7},{8,10},{10,12},{12,14},{9,11},... | collective-permute-start | bytes 1966088 | tf_op jit(solution)/shard_map/ppermute | solution.py:977
  78.8 58.8 %collective-permute-start.3 = (bf16[2,320,512]{2,1,0:T(8,128)(2,1)}, bf16[2,320,512]{2,1,0:T(8,128)(2,1)S(1)}, u32[]{:S(2)}, u32[]{:S(2)}) collective-permute-start(bf16[2,320,512]{2,1,0:T(8,128)(2,1)} %get-tuple-element.123.refs_7_.refs_12_), channel_id=1, source_target_pairs={{0,6},{1,7},{8,14},{9,15},{16,22},{17,23},{24,30},{25,31}} | collective-permute-start | bytes 1966088 | tf_op jit(solution)/shard_map/ppermute | solution.py:977
  85.2 52.3 %collective-permute-start.4 = (bf16[2,320,512]{2,1,0:T(8,128)(2,1)}, bf16[2,320,512]{2,1,0:T(8,128)(2,1)S(1)}, u32[]{:S(2)}, u32[]{:S(2)}) collective-permute-start(bf16[2,320,512]{2,1,0:T(8,128)(2,1)} %get-tuple-element.123.refs_7_.refs_12_), channel_id=1, source_target_pairs={{0,4},{2,6},{1,5},{3,7},{8,12},{10,14},{9,13},{11,15},{16,20},{18,... | collective-permute-start | bytes 1966088 | tf_op jit(solution)/shard_map/ppermute | solution.py:977
  86.6 51.0 %collective-permute-start.5 = (bf16[2,320,512]{2,1,0:T(8,128)(2,1)}, bf16[2,320,512]{2,1,0:T(8,128)(2,1)}, u32[]{:S(2)}, u32[]{:S(2)}) collective-permute-start(bf16[2,320,512]{2,1,0:T(8,128)(2,1)} %get-tuple-element.123.refs_7_.refs_12_), channel_id=1, source_target_pairs={{0,2},{2,4},{4,6},{1,3},{3,5},{5,7},{8,10},{10,12},{12,14},{9,11},... | collective-permute-start | bytes 1966088 | tf_op jit(solution)/shard_map/ppermute | solution.py:977
  101.6 35.3 %collective-permute-start.11 = (s32[1,1]{1,0:T(1,128)}, s32[1,1]{1,0:T(1,128)}, u32[]{:S(2)}, u32[]{:S(2)}) collective-permute-start(s32[1,1]{1,0:T(1,128)} %add.83), channel_id=1, source_target_pairs={{0,2},{2,0},{4,6},{6,4},{1,3},{3,1},{5,7},{7,5},{8,10},{10,8},{12,... | collective-permute-start | bytes 20 | tf_op jit(solution)/shard_map/ppermute | solution.py:889
  127.1 34.7 %collective-permute-start.8 = (bf16[1280,512]{1,0:T(8,128)(2,1)}, bf16[1280,512]{1,0:T(8,128)(2,1)S(1)}, u32[]{:S(2)}, u32[]{:S(2)}) collective-permute-start(bf16[1280,512]{1,0:T(8,128)(2,1)} %get-tuple-element.128.refs_5_), channel_id=1, source_target_pairs={{0,1},{1,0},{2,3},{3,2},{4,5},{5,4},{6,7},{7,6},{8,9},{9,8},{10,11... | collective-permute-start | bytes 3932168 | tf_op jit(solution)/shard_map/ppermute | solution.py:889
  150.0 11.2 %collective-permute-start.12 = (s32[1,1]{1,0:T(1,128)}, s32[1,1]{1,0:T(1,128)}, u32[]{:S(2)}, u32[]{:S(2)}) collective-permute-start(s32[1,1]{1,0:T(1,128)} %add.84), channel_id=1, source_target_pairs={{0,4},{2,6},{4,0},{6,2},{1,5},{3,7},{5,1},{7,3},{8,12},{10,14},{12... | collective-permute-start | bytes 20 | tf_op jit(solution)/shard_map/ppermute | solution.py:889
  159.7 57.8 %collective-permute-start.6 = (bf16[1280,512]{1,0:T(8,128)(2,1)}, bf16[1280,512]{1,0:T(8,128)(2,1)S(1)}, u32[]{:S(2)}, u32[]{:S(2)}) collective-permute-start(bf16[1280,512]{1,0:T(8,128)(2,1)} %get-tuple-element.125.refs_5_), channel_id=1, source_target_pairs={{0,1},{1,0},{2,3},{3,2},{4,5},{5,4},{6,7},{7,6},{8,9},{9,8},{10,11... | collective-permute-start | bytes 3932168 | tf_op jit(solution)/shard_map/ppermute | solution.py:889
  216.9 58.1 %collective-permute-start.14 = (bf16[512,2560]{1,0:T(8,128)(2,1)}, bf16[512,2560]{1,0:T(8,128)(2,1)}, u32[]{:S(2)}, u32[]{:S(2)}) collective-permute-start(bf16[512,2560]{1,0:T(8,128)(2,1)} %get-tuple-element.138.refs_3_), channel_id=1, source_target_pairs={{0,1},{1,0},{2,3},{3,2},{4,5},{5,4},{6,7},{7,6},{8,9},{9,8},{10,11... | collective-permute-start | bytes 7864328 | tf_op jit(solution)/shard_map/ppermute | solution.py:889
  272.4 52.0 %collective-permute-start.13 = (bf16[512,2560]{1,0:T(8,128)(2,1)}, bf16[512,2560]{1,0:T(8,128)(2,1)S(1)}, u32[]{:S(2)}, u32[]{:S(2)}) collective-permute-start(bf16[512,2560]{1,0:T(8,128)(2,1)} %get-tuple-element.137.refs_3_), channel_id=1, source_target_pairs={{0,1},{1,0},{2,3},{3,2},{4,5},{5,4},{6,7},{7,6},{8,9},{9,8},{10,11... | collective-permute-start | bytes 7864328 | tf_op jit(solution)/shard_map/ppermute | solution.py:889
  323.8 147.3 %collective-permute-start.15 = (bf16[512,2560]{1,0:T(8,128)(2,1)}, bf16[512,2560]{1,0:T(8,128)(2,1)}, u32[]{:S(2)}, u32[]{:S(2)}) collective-permute-start(bf16[512,2560]{1,0:T(8,128)(2,1)} %get-tuple-element.144.refs_7_.refs_4_), channel_id=1, source_target_pairs={{0,1},{1,0},{2,3},{3,2},{4,5},{5,4},{6,7},{7,6},{8,9},{9,8},{10,11... | collective-permute-start | bytes 7864328 | tf_op jit(solution)/shard_map/ppermute | solution.py:889
  365.0 65.8 %collective-permute-start.16 = (bf16[640,1536]{1,0:T(8,128)(2,1)}, bf16[640,1536]{1,0:T(8,128)(2,1)S(1)}, u32[]{:S(2)}, u32[]{:S(2)}) collective-permute-start(bf16[640,1536]{1,0:T(8,128)(2,1)} %get-tuple-element.154.refs_3_), channel_id=1, source_target_pairs={{0,16},{8,24},{16,0},{24,8},{1,17},{9,25},{17,1},{25,9},{2,18},{10... | collective-permute-start | bytes 5898248 | tf_op jit(solution)/shard_map/ppermute | solution.py:889
  385.0 100.0 %collective-permute-start.18 = (bf16[640,2048]{1,0:T(8,128)(2,1)}, bf16[640,2048]{1,0:T(8,128)(2,1)}, u32[]{:S(2)}, u32[]{:S(2)}) collective-permute-start(bf16[640,2048]{1,0:T(8,128)(2,1)} %get-tuple-element.155.refs_8_), channel_id=1, source_target_pairs={{0,16},{8,24},{16,0},{24,8},{1,17},{9,25},{17,1},{25,9},{2,18},{10... | collective-permute-start | bytes 7864328 | tf_op jit(solution)/shard_map/ppermute | solution.py:889
  427.8 122.5 %collective-permute-start.17 = (bf16[512,2560]{1,0:T(8,128)(2,1)}, bf16[512,2560]{1,0:T(8,128)(2,1)}, u32[]{:S(2)}, u32[]{:S(2)}) collective-permute-start(bf16[512,2560]{1,0:T(8,128)(2,1)} %get-tuple-element.158.refs_2_.refs_4_), channel_id=1, source_target_pairs={{0,1},{1,0},{2,3},{3,2},{4,5},{5,4},{6,7},{7,6},{8,9},{9,8},{10,11... | collective-permute-start | bytes 7864328 | tf_op jit(solution)/shard_map/ppermute | solution.py:889
  434.4 53.6 %collective-permute-start.20 = (bf16[320,1536]{1,0:T(8,128)(2,1)}, bf16[320,1536]{1,0:T(8,128)(2,1)S(1)}, u32[]{:S(2)}, u32[]{:S(2)}) collective-permute-start(bf16[320,1536]{1,0:T(8,128)(2,1)} %near.7.refs_3_), channel_id=1, source_target_pairs={{0,2},{2,0},{4,6},{6,4},{1,3},{3,1},{5,7},{7,5},{8,10},{10,8},{12,... | collective-permute-start | bytes 2949128 | tf_op jit(solution)/shard_map/ppermute | solution.py:889
  471.0 120.1 %collective-permute-start.21 = (bf16[640,3584]{1,0:T(8,128)(2,1)}, bf16[640,3584]{1,0:T(8,128)(2,1)}, u32[]{:S(2)}, u32[]{:S(2)}) collective-permute-start(bf16[640,3584]{1,0:T(8,128)(2,1)} %get-tuple-element.159.refs_6_), channel_id=1, source_target_pairs={{0,16},{8,24},{16,0},{24,8},{1,17},{9,25},{17,1},{25,9},{2,18},{10... | collective-permute-start | bytes 13762568 | tf_op jit(solution)/shard_map/ppermute | solution.py:889
  487.8 58.7 %collective-permute-start.19 = (bf16[320,2048]{1,0:T(8,128)(2,1)}, bf16[320,2048]{1,0:T(8,128)(2,1)S(1)}, u32[]{:S(2)}, u32[]{:S(2)}) collective-permute-start(bf16[320,2048]{1,0:T(8,128)(2,1)} %near.8.refs_3_), channel_id=1, source_target_pairs={{0,2},{2,0},{4,6},{6,4},{1,3},{3,1},{5,7},{7,5},{8,10},{10,8},{12,... | collective-permute-start | bytes 3932168 | tf_op jit(solution)/shard_map/ppermute | solution.py:889
  491.2 137.4 %collective-permute-start.27 = (bf16[160,1536]{1,0:T(8,128)(2,1)}, bf16[160,1536]{1,0:T(8,128)(2,1)}, u32[]{:S(2)}, u32[]{:S(2)}) collective-permute-start(bf16[160,1536]{1,0:T(8,128)(2,1)} %fold.7.refs_13_), channel_id=1, source_target_pairs={{0,4},{2,6},{4,0},{6,2},{1,5},{3,7},{5,1},{7,3},{8,12},{10,14},{12... | collective-permute-start | bytes 1474568 | tf_op jit(solution)/shard_map/ppermute | solution.py:889
  508.8 34.9 %collective-permute-start.22 = (bf16[2,320,512]{2,1,0:T(8,128)(2,1)}, bf16[2,320,512]{2,1,0:T(8,128)(2,1)S(1)}, u32[]{:S(2)}, u32[]{:S(2)}) collective-permute-start(bf16[2,320,512]{2,1,0:T(8,128)(2,1)} %get-tuple-element.168.refs_3_), channel_id=1, source_target_pairs={{2,0},{4,2},{6,4},{3,1},{5,3},{7,5},{10,8},{12,10},{14,12},{11,9},... | collective-permute-start | bytes 1966088 | tf_op jit(solution)/shard_map/ppermute | solution.py:977
  543.7 132.8 %collective-permute-start.26 = (bf16[640,3584]{1,0:T(8,128)(2,1)}, bf16[640,3584]{1,0:T(8,128)(2,1)}, u32[]{:S(2)}, u32[]{:S(2)}) collective-permute-start(bf16[640,3584]{1,0:T(8,128)(2,1)} %get-tuple-element.169.refs_3_), channel_id=1, source_target_pairs={{0,16},{8,24},{16,0},{24,8},{1,17},{9,25},{17,1},{25,9},{2,18},{10... | collective-permute-start | bytes 13762568 | tf_op jit(solution)/shard_map/ppermute | solution.py:889
  546.5 79.5 %collective-permute-start.23 = (bf16[2,320,512]{2,1,0:T(8,128)(2,1)}, bf16[2,320,512]{2,1,0:T(8,128)(2,1)}, u32[]{:S(2)}, u32[]{:S(2)}) collective-permute-start(bf16[2,320,512]{2,1,0:T(8,128)(2,1)} %add_convert_fusion.3), channel_id=1, source_target_pairs={{2,0},{4,2},{6,4},{3,1},{5,3},{7,5},{10,8},{12,10},{14,12},{11,9},... | collective-permute-start | bytes 1966088 | tf_op jit(solution)/shard_map/ppermute | solution.py:977
  550.3 175.9 %collective-permute-start.32 = (bf16[160,2048]{1,0:T(8,128)(2,1)}, bf16[160,2048]{1,0:T(8,128)(2,1)}, u32[]{:S(2)}, u32[]{:S(2)}) collective-permute-start(bf16[160,2048]{1,0:T(8,128)(2,1)} %fold.8.refs_7_), channel_id=1, source_target_pairs={{0,4},{2,6},{4,0},{6,2},{1,5},{3,7},{5,1},{7,3},{8,12},{10,14},{12... | collective-permute-start | bytes 1966088 | tf_op jit(solution)/shard_map/ppermute | solution.py:889
  594.6 108.8 %collective-permute-start.25 = (bf16[320,3584]{1,0:T(8,128)(2,1)}, bf16[320,3584]{1,0:T(8,128)(2,1)}, u32[]{:S(2)}, u32[]{:S(2)}) collective-permute-start(bf16[320,3584]{1,0:T(8,128)(2,1)} %near.9.refs_14_), channel_id=1, source_target_pairs={{0,2},{2,0},{4,6},{6,4},{1,3},{3,1},{5,7},{7,5},{8,10},{10,8},{12,... | collective-permute-start | bytes 6881288 | tf_op jit(solution)/shard_map/ppermute | solution.py:889
  626.0 49.0 %collective-permute-start.29 = (bf16[2,320,512]{2,1,0:T(8,128)(2,1)}, bf16[2,320,512]{2,1,0:T(8,128)(2,1)S(1)}, u32[]{:S(2)}, u32[]{:S(2)}) collective-permute-start(bf16[2,320,512]{2,1,0:T(8,128)(2,1)} %get-tuple-element.179.refs_5_), channel_id=1, source_target_pairs={{2,0},{4,2},{6,4},{3,1},{5,3},{7,5},{10,8},{12,10},{14,12},{11,9},... | collective-permute-start | bytes 1966088 | tf_op jit(solution)/shard_map/ppermute | solution.py:977
  628.6 79.3 %collective-permute-start.24 = (bf16[2,320,512]{2,1,0:T(8,128)(2,1)S(1)}, bf16[2,320,512]{2,1,0:T(8,128)(2,1)}, u32[]{:S(2)}, u32[]{:S(2)}) collective-permute-start(bf16[2,320,512]{2,1,0:T(8,128)(2,1)S(1)} %add_convert_fusion.2), channel_id=1, source_target_pairs={{2,0},{4,2},{6,4},{3,1},{5,3},{7,5},{10,8},{12,10},{14,12},{11,9},... | collective-permute-start | bytes 1966088 | tf_op jit(solution)/shard_map/ppermute | solution.py:977
  675.2 27.9 %collective-permute-start.30 = (bf16[2,320,512]{2,1,0:T(8,128)(2,1)S(1)}, bf16[2,320,512]{2,1,0:T(8,128)(2,1)S(1)}, u32[]{:S(2)}, u32[]{:S(2)}) collective-permute-start(bf16[2,320,512]{2,1,0:T(8,128)(2,1)S(1)} %add_convert_fusion.1), channel_id=1, source_target_pairs={{2,0},{4,2},{6,4},{3,1},{5,3},{7,5},{10,8},{12,10},{14,12},{11,9},... | collective-permute-start | bytes 1966088 | tf_op jit(solution)/shard_map/ppermute | solution.py:977
  680.1 149.6 %collective-permute-start.35 = (bf16[320,3584]{1,0:T(8,128)(2,1)}, bf16[320,3584]{1,0:T(8,128)(2,1)}, u32[]{:S(2)}, u32[]{:S(2)}) collective-permute-start(bf16[320,3584]{1,0:T(8,128)(2,1)} %near.10.refs_3_), channel_id=1, source_target_pairs={{0,2},{2,0},{4,6},{6,4},{1,3},{3,1},{5,7},{7,5},{8,10},{10,8},{12,... | collective-permute-start | bytes 6881288 | tf_op jit(solution)/shard_map/ppermute | solution.py:889
  703.1 122.5 %collective-permute-start.36 = (bf16[640,1280]{1,0:T(8,128)(2,1)}, bf16[640,1280]{1,0:T(8,128)(2,1)}, u32[]{:S(2)}, u32[]{:S(2)}) collective-permute-start(bf16[640,1280]{1,0:T(8,128)(2,1)} %get-tuple-element.184.refs_3_), channel_id=1, source_target_pairs={{0,16},{8,24},{16,0},{24,8},{1,17},{9,25},{17,1},{25,9},{2,18},{10... | collective-permute-start | bytes 4915208 | tf_op jit(solution)/shard_map/ppermute | solution.py:889
  703.4 86.8 %collective-permute-start.31 = (bf16[2,320,512]{2,1,0:T(8,128)(2,1)S(1)}, bf16[2,320,512]{2,1,0:T(8,128)(2,1)S(1)}, u32[]{:S(2)}, u32[]{:S(2)}) collective-permute-start(bf16[2,320,512]{2,1,0:T(8,128)(2,1)S(1)} %add_convert_fusion), channel_id=1, source_target_pairs={{2,0},{4,2},{6,4},{3,1},{5,3},{7,5},{10,8},{12,10},{14,12},{11,9},... | collective-permute-start | bytes 1966088 | tf_op jit(solution)/shard_map/ppermute | solution.py:977
  707.9 124.8 %collective-permute-start.34 = (bf16[160,3584]{1,0:T(8,128)(2,1)}, bf16[160,3584]{1,0:T(8,128)(2,1)}, u32[]{:S(2)}, u32[]{:S(2)}) collective-permute-start(bf16[160,3584]{1,0:T(8,128)(2,1)} %fold.9.refs_8_), channel_id=1, source_target_pairs={{0,4},{2,6},{4,0},{6,2},{1,5},{3,7},{5,1},{7,3},{8,12},{10,14},{12... | collective-permute-start | bytes 3440648 | tf_op jit(solution)/shard_map/ppermute | solution.py:889
  726.2 90.1 %collective-permute-start.28 = (bf16[512,2560]{1,0:T(8,128)(2,1)}, bf16[512,2560]{1,0:T(8,128)(2,1)}, u32[]{:S(2)}, u32[]{:S(2)}) collective-permute-start(bf16[512,2560]{1,0:T(8,128)(2,1)} %get-tuple-element.185.refs_5_.refs_4_), channel_id=1, source_target_pairs={{0,1},{1,0},{2,3},{3,2},{4,5},{5,4},{6,7},{7,6},{8,9},{9,8},{10,11... | collective-permute-start | bytes 7864328 | tf_op jit(solution)/shard_map/ppermute | solution.py:889
  802.6 58.4 %collective-permute-start.33 = (bf16[512,2560]{1,0:T(8,128)(2,1)}, bf16[512,2560]{1,0:T(8,128)(2,1)S(1)}, u32[]{:S(2)}, u32[]{:S(2)}) collective-permute-start(bf16[512,2560]{1,0:T(8,128)(2,1)} %get-tuple-element.195.refs_3_.refs_4_), channel_id=1, source_target_pairs={{0,1},{1,0},{2,3},{3,2},{4,5},{5,4},{6,7},{7,6},{8,9},{9,8},{10,11... | collective-permute-start | bytes 7864328 | tf_op jit(solution)/shard_map/ppermute | solution.py:889
  816.3 56.2 %collective-permute-start.38 = (bf16[640,640]{1,0:T(8,128)(2,1)}, bf16[640,640]{1,0:T(8,128)(2,1)}, u32[]{:S(2)}, u32[]{:S(2)}) collective-permute-start(bf16[640,640]{1,0:T(8,128)(2,1)} %get-tuple-element.196.refs_6_), channel_id=1, source_target_pairs={{0,16},{8,24},{16,0},{24,8},{1,17},{9,25},{17,1},{25,9},{2,18},{10... | collective-permute-start | bytes 2457608 | tf_op jit(solution)/shard_map/ppermute | solution.py:889
  825.7 55.0 %collective-permute-start.43 = (bf16[640,1280]{1,0:T(8,128)(2,1)}, bf16[640,1280]{1,0:T(8,128)(2,1)}, u32[]{:S(2)}, u32[]{:S(2)}) collective-permute-start(bf16[640,1280]{1,0:T(8,128)(2,1)} %get-tuple-element.193.refs_9_), channel_id=1, source_target_pairs={{0,16},{8,24},{16,0},{24,8},{1,17},{9,25},{17,1},{25,9},{2,18},{10... | collective-permute-start | bytes 4915208 | tf_op jit(solution)/shard_map/ppermute | solution.py:889
  829.7 48.9 %collective-permute-start.40 = (bf16[320,1280]{1,0:T(8,128)(2,1)}, bf16[320,1280]{1,0:T(8,128)(2,1)}, u32[]{:S(2)}, u32[]{:S(2)}) collective-permute-start(bf16[320,1280]{1,0:T(8,128)(2,1)} %near.11.refs_3_), channel_id=1, source_target_pairs={{0,2},{2,0},{4,6},{6,4},{1,3},{3,1},{5,7},{7,5},{8,10},{10,8},{12,... | collective-permute-start | bytes 2457608 | tf_op jit(solution)/shard_map/ppermute | solution.py:889
  832.6 53.4 %collective-permute-start.42 = (bf16[160,3584]{1,0:T(8,128)(2,1)}, bf16[160,3584]{1,0:T(8,128)(2,1)}, u32[]{:S(2)}, u32[]{:S(2)}) collective-permute-start(bf16[160,3584]{1,0:T(8,128)(2,1)} %fold.10.refs_5_), channel_id=1, source_target_pairs={{0,4},{2,6},{4,0},{6,2},{1,5},{3,7},{5,1},{7,3},{8,12},{10,14},{12... | collective-permute-start | bytes 3440648 | tf_op jit(solution)/shard_map/ppermute | solution.py:889
  874.4 4.1 collective-permute-start.39
  880.7 5.3 collective-permute-start.41
  882.9 31.2 %collective-permute-start.45 = (bf16[320,1280]{1,0:T(8,128)(2,1)}, bf16[320,1280]{1,0:T(8,128)(2,1)}, u32[]{:S(2)}, u32[]{:S(2)}) collective-permute-start(bf16[320,1280]{1,0:T(8,128)(2,1)} %near.13.refs_5_), channel_id=1, source_target_pairs={{0,2},{2,0},{4,6},{6,4},{1,3},{3,1},{5,7},{7,5},{8,10},{10,8},{12,... | collective-permute-start | bytes 2457608 | tf_op jit(solution)/shard_map/ppermute | solution.py:889
  890.6 14.1 %collective-permute-start.44 = (f32[3,2560]{1,0:T(4,128)S(1)}, f32[3,2560]{1,0:T(4,128)S(1)}, u32[]{:S(2)}, u32[]{:S(2)}) collective-permute-start(f32[3,2560]{1,0:T(4,128)S(1)} %add.95), channel_id=1, source_target_pairs={{0,4},{2,6},{4,0},{6,2},{1,5},{3,7},{5,1},{7,3},{8,12},{10,14},{12... | collective-permute-start | bytes 92168 | tf_op jit(solution)/shard_map/ppermute | solution.py:889
  892.2 33.3 %collective-permute-start.47 = (bf16[320,640]{1,0:T(8,128)(2,1)S(1)}, bf16[320,640]{1,0:T(8,128)(2,1)S(1)}, u32[]{:S(2)}, u32[]{:S(2)}) collective-permute-start(bf16[320,640]{1,0:T(8,128)(2,1)S(1)} %copy-done.28), channel_id=1, source_target_pairs={{0,2},{2,0},{4,6},{6,4},{1,3},{3,1},{5,7},{7,5},{8,10},{10,8},{12,... | collective-permute-start | bytes 1228808 | tf_op jit(solution)/shard_map/ppermute | solution.py:889
  893.2 29.3 %collective-permute-start.48 = (bf16[160,1280]{1,0:T(8,128)(2,1)}, bf16[160,1280]{1,0:T(8,128)(2,1)S(1)}, u32[]{:S(2)}, u32[]{:S(2)}) collective-permute-start(bf16[160,1280]{1,0:T(8,128)(2,1)} %fold.11.refs_2_), channel_id=1, source_target_pairs={{0,4},{2,6},{4,0},{6,2},{1,5},{3,7},{5,1},{7,3},{8,12},{10,14},{12... | collective-permute-start | bytes 1228808 | tf_op jit(solution)/shard_map/ppermute | solution.py:889
  916.2 23.0 %collective-permute-start.46 = (bf16[160,1280]{1,0:T(8,128)(2,1)}, bf16[160,1280]{1,0:T(8,128)(2,1)S(1)}, u32[]{:S(2)}, u32[]{:S(2)}) collective-permute-start(bf16[160,1280]{1,0:T(8,128)(2,1)} %fold.12.refs_5_), channel_id=1, source_target_pairs={{0,4},{2,6},{4,0},{6,2},{1,5},{3,7},{5,1},{7,3},{8,12},{10,14},{12... | collective-permute-start | bytes 1228808 | tf_op jit(solution)/shard_map/ppermute | solution.py:889
  928.2 15.3 %collective-permute-start.49 = (bf16[160,640]{1,0:T(8,128)(2,1)}, bf16[160,640]{1,0:T(8,128)(2,1)S(1)}, u32[]{:S(2)}, u32[]{:S(2)}) collective-permute-start(bf16[160,640]{1,0:T(8,128)(2,1)} %fold.13.refs_5_), channel_id=1, source_target_pairs={{0,4},{2,6},{4,0},{6,2},{1,5},{3,7},{5,1},{7,3},{8,12},{10,14},{12... | collective-permute-start | bytes 614408 | tf_op jit(solution)/shard_map/ppermute | solution.py:889
  (36 other events, 395.0 us)
Sparse Core Ops, SparseCore 0:
  70.6 50.0 all-gather.1
